TPU v7x, 128 devices: a whole 4x4x4 slice. The times are simulated.
128 devices in a mesh: pool: 16 (over x_lo, z, core), head: 8 (over y, x_hi).
Axes of the slice: x: 4 (x_hi: 2, x_lo: 2; x = x_hi * 2 + x_lo), y: 4, z: 4, core: 2. Of those that a mesh axis runs over, the one named last changes fastest.
Arguments:
- hidden: bfloat16 [8192, 4096], P('pool')
- w_query: bfloat16 [4096, 4096], P(None, 'head'), may hold values from -0.09375 to 0.09375
- w_key: bfloat16 [4096, 4096], P(None, 'head'), may hold values from -0.09375 to 0.09375
- w_value: bfloat16 [4096, 4096], P(None, 'head'), may hold values from -0.09375 to 0.09375
- w_output: bfloat16 [4096, 4096], P('head'), may hold values from -6 to 6
- prefix_keys: bfloat16 [512, 16, 4096], P(('pool', 'head')), may hold values from -6 to 6
- prefix_values: bfloat16 [512, 16, 4096], P(('pool', 'head')), may hold values from -6 to 6
- block_slot: int32 [512], replicated, may hold values from 0 to 511, each once
- suffix_len: int32 [16], P('pool'), may hold values from 128 to 512, as said below
Outputs:
- mixed: bfloat16 [8192, 4096], P(('pool', 'head'))
Inputs may be any that keep to these rules, and one draw needn't show every extreme that they name: `suffix_len`: one request has all 512 suffix tokens live.
All inputs are finite; a program needn't handle non-finite values.
Results may differ from a plain program's by a relative error of at most 0.04.
Values may be sent and summed in bfloat16 or wider, within the bound.
No kernel may reach another device: no remote copies, remote signals or barrier semaphores. Data moves between devices by JAX's collectives and lax.ppermute only.
A program may use at most 256 MiB of HBM per device.

v0:
```python
import math

import jax
import jax.numpy as jnp
from jax import lax
from jax.sharding import PartitionSpec as P

HD = 128


def rope(values, positions):
    half = values.shape[-1] // 2
    freq = jnp.exp(
        -math.log(10000.0) * jnp.arange(half).astype(jnp.float32) * 2.0 / values.shape[-1]
    )
    angle = positions.astype(jnp.float32)[:, None] * freq[None, :]
    cosine = jnp.cos(angle)[:, None, :]
    sine = jnp.sin(angle)[:, None, :]
    first = values[..., :half]
    second = values[..., half:]
    return jnp.concatenate(
        [first * cosine - second * sine, first * sine + second * cosine], axis=-1
    )


def token_positions(slot_ids, block_slot, block):
    blocks = jnp.arange(block_slot.shape[0])
    owner = jnp.sum(jnp.where(block_slot[None, :] == slot_ids[:, None], blocks[None, :], 0), axis=1)
    return (owner[:, None] * block + jnp.arange(block)[None, :]).reshape(-1)


def rotate_keys(keys, slot_ids, block_slot):
    count, block, feats = keys.shape
    positions = token_positions(slot_ids, block_slot, block)
    turned = rope(keys.astype(jnp.float32).reshape(count * block, feats // HD, HD), positions)
    return turned.astype(jnp.bfloat16).reshape(count, block, feats)


def absorb(carry, query, keys, values, scale):
    top, total, acc = carry
    scores = jnp.einsum("qhd,khd->hqk", query, keys, preferred_element_type=jnp.float32) * scale
    new_top = jnp.maximum(top, jnp.max(scores, axis=2))
    shrink = jnp.exp(top - new_top)
    weights = jnp.exp(scores - new_top[:, :, None]).astype(jnp.bfloat16)
    total = total * shrink + jnp.sum(weights.astype(jnp.float32), axis=2)
    acc = acc * shrink.T[:, :, None] + jnp.einsum(
        "hqk,khd->qhd", weights, values, preferred_element_type=jnp.float32
    )
    return (new_top, total, acc)


def body(
    hidden, w_query, w_key, w_value, w_output, prefix_keys, prefix_values, block_slot, suffix_len
):
    suf = hidden.shape[0]
    heads_dev = w_query.shape[1] // HD
    blk_dev, block, feats = prefix_keys.shape
    nblk = block_slot.shape[0]
    scale = 1.0 / math.sqrt(HD)
    length = suffix_len[0]
    spos = nblk * block + jnp.arange(suf)
    query = rope(
        jnp.dot(hidden, w_query, preferred_element_type=jnp.float32).reshape(suf, heads_dev, HD),
        spos,
    ).astype(jnp.bfloat16)
    key_suffix = rope(
        jnp.dot(hidden, w_key, preferred_element_type=jnp.float32).reshape(suf, heads_dev, HD), spos
    ).astype(jnp.bfloat16)
    value_suffix = (
        jnp.dot(hidden, w_value, preferred_element_type=jnp.float32)
        .astype(jnp.bfloat16)
        .reshape(suf, heads_dev, HD)
    )
    scores = (
        jnp.einsum("qhd,khd->hqk", query, key_suffix, preferred_element_type=jnp.float32) * scale
    )
    row_ids = jnp.arange(suf)[:, None]
    col_ids = jnp.arange(suf)[None, :]
    allowed = (col_ids <= row_ids) & (col_ids < length)
    scores = jnp.where(allowed[None, :, :], scores, -jnp.inf)
    top = jnp.max(scores, axis=2)
    weights = jnp.exp(scores - top[:, :, None]).astype(jnp.bfloat16)
    total = jnp.sum(weights.astype(jnp.float32), axis=2)
    acc = jnp.einsum("hqk,khd->qhd", weights, value_suffix, preferred_element_type=jnp.float32)
    carry = (top, total, acc)
    head_keys, head_values = (
        lax.all_to_all(prefix_keys, "head", split_axis=2, concat_axis=0, tiled=True),
        lax.all_to_all(prefix_values, "head", split_axis=2, concat_axis=0, tiled=True),
    )
    keys = lax.all_gather(head_keys, "pool", axis=0, tiled=True)
    values = lax.all_gather(head_values, "pool", axis=0, tiled=True)
    slot_ids = jnp.arange(keys.shape[0])
    consume_keys = keys
    consume_keys = rotate_keys(consume_keys, slot_ids, block_slot)
    count = consume_keys.shape[0] * block
    carry = absorb(
        carry,
        query,
        consume_keys.reshape(count, heads_dev, HD),
        values.reshape(count, heads_dev, HD),
        scale,
    )
    top, total, acc = carry
    attended = acc / total.T[:, :, None]
    attended = jnp.where(jnp.arange(suf)[:, None, None] < length, attended, 0.0)
    attended = attended.astype(jnp.bfloat16).reshape(suf, heads_dev * HD)
    return lax.psum_scatter(
        jnp.dot(attended, w_output, preferred_element_type=jnp.float32).astype(jnp.bfloat16),
        "head",
        scatter_dimension=0,
        tiled=True,
    )


def solution(mesh):
    placed = (
        P("pool", None),
        P(None, "head"),
        P(None, "head"),
        P(None, "head"),
        P("head", None),
        P(("pool", "head"), None, None),
        P(("pool", "head"), None, None),
        P(),
        P("pool"),
    )
    return jax.shard_map(
        body, mesh=mesh, in_specs=placed, out_specs=P(("pool", "head"), None), check_vma=False
    )
```

profile of v0, /device:TPU:0, one launch (start us, length us, event | category | flops | bytes accessed | tf_op | source)
XLA Modules:
  0.0 367.3 jit_solution(16348548940373985816)
XLA Ops:
  6.5 5.9 %copy.53 = bf16[4,16,4096]{1,0,2:T(4,128)(2,1)} copy(bf16[4,16,4096]{2,1,0:T(8,128)(2,1)} %param.14) | data formatting | bytes 1048576 | tf_op args[5]
  12.4 5.7 %reshape.202 = bf16[8,2,16384]{2,1,0:T(2,128)(2,1)S(1)} reshape(bf16[4096,4,16]{2,1,0:T(4,128)(2,1)} %bitcast.56) | data formatting | bytes 1048576
  18.2 18.4 %all_to_all.36 = bf16[8,2,16384]{2,1,0:T(2,128)(2,1)S(1)} all-to-all(bf16[8,2,16384]{2,1,0:T(2,128)(2,1)S(1)} %reshape.202), channel_id=1, replica_groups=mesh['pool'=16,'head'=8] {'head'}, dimensions={0} | all-to-all | bytes 1048576 | tf_op jit(solution)/shard_map/all_to_all | solution.py:87
  36.6 4.1 %reshape.203 = bf16[4096,4,16]{2,1,0:T(4,128)(2,1)} reshape(bf16[8,2,16384]{2,1,0:T(2,128)(2,1)S(1)} %all_to_all.36) | data formatting | bytes 1048576
  40.7 6.5 %copy.63 = bf16[4,16,8,512]{3,1,0,2:T(8,128)(2,1)} copy(bf16[4,16,8,512]{1,0,3,2:T(4,128)(2,1)} %bitcast.54) | data formatting | bytes 1048576 | tf_op jit(solution)/shard_map/all_to_all | solution.py:87
  47.2 0.0 all-gather.3.cloned.1.call-update
  47.2 4.7 %copy.58 = bf16[4,16,4096]{1,0,2:T(4,128)(2,1)} copy(bf16[4,16,4096]{2,1,0:T(8,128)(2,1)S(1)} %copy-done.9) | data formatting | bytes 1048576 | tf_op args[6]
  51.9 6.6 %reshape.200 = bf16[8,2,16384]{2,1,0:T(2,128)(2,1)} reshape(bf16[4096,4,16]{2,1,0:T(4,128)(2,1)} %bitcast.57) | data formatting | bytes 1048576
  58.5 4.1 %all-to-all-start.1 = ((bf16[8,2,16384]{2,1,0:T(2,128)(2,1)}), bf16[8,2,16384]{2,1,0:T(2,128)(2,1)}, u32[]{:S(2)}, u32[]{:S(2)}) async-start(bf16[8,2,16384]{2,1,0:T(2,128)(2,1)} %reshape.200), calls=%async_computation.1 | async-start | bytes 1048576 | tf_op jit(solution)/shard_map/all_to_all | solution.py:88
  62.7 0.2 all-gather.5.cloned.1.call-start
  62.9 6.0 %fusion.28 = f32[512,512]{0,1:T(8,128)S(1)} fusion(bf16[512,4096]{1,0:T(8,128)(2,1)} %param.9, bf16[4096,512]{1,0:T(8,128)(2,1)} %param.10), kind=kOutput, calls=%fused_computation.56 | convolution fusion | flops 2147483648 | bytes 9437184 | tf_op jit(solution)/shard_map/dot_general | solution.py:63
  68.9 0.1 fusion.27
  69.0 0.3 copy.64
  69.4 0.3 copy.65
  69.7 5.9 %fusion.29 = f32[512,512]{0,1:T(8,128)S(1)} fusion(bf16[512,4096]{1,0:T(8,128)(2,1)} %param.9, bf16[4096,512]{1,0:T(8,128)(2,1)} %param.11), kind=kOutput, calls=%fused_computation.57 | convolution fusion | flops 2147483648 | bytes 9437184 | tf_op jit(solution)/shard_map/dot_general | solution.py:67
  75.6 0.0 copy-start.10
  75.7 0.1 fusion.26
  75.8 1.3 copy.66
  77.1 1.4 copy.67
  79.2 0.2 select_reduce_fusion
  79.4 0.1 add_convert_fusion.3
  79.5 1.0 multiply_cosine_fusion.1
  80.5 3.1 subtract_convert_fusion.1
  83.7 5.6 %reshape.201 = bf16[4096,4,16]{2,1,0:T(4,128)(2,1)} reshape(bf16[8,2,16384]{2,1,0:T(2,128)(2,1)} %all-to-all-done.1) | data formatting | bytes 1048576
  89.3 6.7 %copy.59 = bf16[8,4,16,512]{3,2,1,0:T(8,128)(2,1)} copy(bf16[8,4,16,512]{2,1,3,0:T(4,128)(2,1)} %bitcast.55) | data formatting | bytes 1048576 | tf_op jit(solution)/shard_map/all_to_all | solution.py:88
  95.9 0.0 all-gather.5.cloned.1.call-update
  96.0 0.3 reduce-scatter.2.cloned.1.call-start
  96.2 0.1 fusion.15
  96.4 0.1 convert_element_type.87
  96.5 0.0 copy-start.11
  96.6 1.3 fusion.6
  97.9 2.1 copy-done.1
  100.1 0.9 convert_reduce_fusion.1
  101.0 0.6 copy-done.12
  101.6 3.2 convolution_convert_fusion.1
  104.8 17.9 %multiply_cosine_fusion = (f32[8192,64]{1,0:T(8,128)}, f32[8192,64]{1,0:T(8,128)}) fusion(f32[64]{0:T(128)S(1)} %multiply_exponential_fusion, f32[8192]{0:T(1024)S(1)} %convert_element_type.87), kind=kLoop, calls=%fused_computation.12 | loop fusion | flops 524288 | bytes 4227328 | tf_op jit(solution)/shard_map/cos | solution.py:17
  122.7 15.6 %reshape.199 = f32[8192,4,128]{2,1,0:T(4,128)} reshape(bf16[512,16,512]{2,1,0:T(8,128)(2,1)} %all-gather.3.cloned.1.call-done) | data formatting | bytes 25165824 | tf_op jit(solution)/shard_map/reshape | solution.py:35
  138.3 22.3 %fusion.25 = (f32[8192,4,64]{2,1,0:T(4,128)S(1)}, f32[8192,4,64]{2,1,0:T(4,128)}) fusion(f32[8192,4,128]{2,1,0:T(4,128)} %reshape.199), kind=kLoop, calls=%fused_computation.53 | loop fusion | bytes 33554432 | tf_op jit(solution)/shard_map/slice | solution.py:19
  160.6 15.0 %subtract_convert_fusion = (bf16[8192,4,64]{2,0,1:T(8,128)(2,1)}, bf16[8192,4,64]{2,0,1:T(8,128)(2,1)}) fusion(f32[8192,4,64]{2,1,0:T(4,128)} %get-tuple-element.10, f32[8192,4,64]{2,1,0:T(4,128)S(1)} %get-tuple-element.9, f32[8192,64]{1,0:T(8,128)} %get-tuple-element.22, f32[8192,64]{1,0:T(8,128)S(1)} %copy-done), kind=kLoop, calls=%fused_computation.4 | loop fusion | flops 16777216 | bytes 29360128 | tf_op jit(solution)/shard_map/convert.1
  175.6 30.0 %multiply_reduce_fusion = (f32[4,512]{1,0:T(4,128)S(1)}, f32[4,512,8192]{2,1,0:T(8,128)}) fusion(bf16[8192,4,64]{2,0,1:T(8,128)(2,1)} %get-tuple-element.8, bf16[8192,4,64]{2,0,1:T(8,128)(2,1)} %get-tuple-element.7, bf16[512,4,64]{2,0,1:T(8,128)(2,1)} %copy-done.2, bf16[512,4,64]{2,0,1:T(8,128)(2,1)} %copy-done.3), kind=kOutput, calls=%fused_computation.2 | convolution fusion | flops 4346345472 | bytes 76029952 | tf_op jit(solution)/shard_map/qhd,khd->hqk/dot_general | solution.py:41
  205.6 21.2 %convert_reduce_fusion = f32[4,512]{1,0:T(4,128)S(1)} fusion(f32[4,512]{1,0:T(4,128)S(1)} %max.12, f32[4,512,8192]{2,1,0:T(8,128)} %get-tuple-element.28), kind=kLoop, calls=%fused_computation | loop fusion | flops 83884032 | bytes 67125248 | tf_op jit(solution)/shard_map/reduce_sum | solution.py:45
  226.8 0.0 all-gather.5.cloned.1.call-done
  226.8 12.6 %reshape.196 = bf16[8192,4,128]{2,1,0:T(4,128)(2,1)} reshape(bf16[512,16,512]{2,1,0:T(8,128)(2,1)} %all-gather.5.cloned.1.call-done) | data formatting | bytes 16777216 | tf_op jit(solution)/shard_map/reshape | solution.py:100
  239.4 26.7 %fusion.10 = f32[512,4,128]{0,2,1:T(8,128)S(1)} fusion(bf16[8192,4,128]{2,1,0:T(4,128)(2,1)} %reshape.196, f32[4,512,8192]{2,1,0:T(8,128)} %get-tuple-element.28, f32[4,512]{1,0:T(4,128)S(1)} %max.12), kind=kOutput, calls=%fused_computation.22 | convolution fusion | flops 4345298944 | bytes 76554240 | tf_op jit(solution)/shard_map/hqk,khd->qhd/dot_general | solution.py:46
  266.1 3.7 %fusion.14 = bf16[512,4,128]{0,2,1:T(8,128)(2,1)S(1)} fusion(f32[512,4,128]{0,2,1:T(8,128)S(1)} %fusion.10, bf16[512,4,128]{0,2,1:T(8,128)(2,1)S(1)} %bitcast.63, f32[512,4]{0,1:T(4,128)S(1)} %get-tuple-element.5, f32[512,4]{0,1:T(4,128)S(1)} %get-tuple-element.6, pred[512]{0:T(512)(128)(4,1)S(1)} %iota_compare_fusion.2, f32[4,512,512]{1,2,0:T(8,128)} %copy-done.1, ...), kind=kOutput, calls=%fused_computation.25 | convolution fusion | flops 273940480 | bytes 6578688 | tf_op jit(solution)/shard_map/hqk,khd->qhd/dot_general | solution.py:84
  269.9 4.3 %convolution_convert_fusion = bf16[512,4096]{1,0:T(8,128)(2,1)} fusion(bf16[512,512]{0,1:T(8,128)(2,1)S(1)} %bitcast.62, bf16[512,4096]{1,0:T(8,128)(2,1)S(1)} %copy-done.4), kind=kOutput, calls=%fused_computation.13 | convolution fusion | flops 2149580800 | bytes 8912896 | tf_op jit(solution)/shard_map/dot_general | solution.py:108
  274.2 0.0 reduce-scatter.2.cloned.1.call-update
  274.2 86.6 %reduce-scatter.2.cloned.1.call-done = bf16[64,4096]{1,0:T(8,128)(2,1)} async-done(((bf16[512,4096]{1,0:T(8,128)(2,1)}), bf16[64,4096]{1,0:T(8,128)(2,1)}) %reduce-scatter.2.cloned.1.call-update) | async-done | bytes 524304 | tf_op jit(solution)/shard_map/reduce_scatter | solution.py:107
  (33 shorter events, 0.1 us)
Async XLA Ops:
  6.5 116.2 %all-gather.3.cloned.1.call-start = ((), (), s32[]{:S(2)}) async-start(), calls=%async_computation.3 | async-start | bytes 8912896 | tf_op jit(solution)/shard_map/all_gather | solution.py:90
  36.5 10.7 %copy-start.9 = (bf16[4,16,4096]{2,1,0:T(8,128)(2,1)S(1)}, bf16[4,16,4096]{2,1,0:T(8,128)(2,1)}, u32[]{:S(2)}) copy-start(bf16[4,16,4096]{2,1,0:T(8,128)(2,1)} %param.15) | copy-start | bytes 1572868
  58.5 25.1 %all-to-all-start.1 = ((bf16[8,2,16384]{2,1,0:T(2,128)(2,1)}), bf16[8,2,16384]{2,1,0:T(2,128)(2,1)}, u32[]{:S(2)}, u32[]{:S(2)}) async-start(bf16[8,2,16384]{2,1,0:T(2,128)(2,1)} %reshape.200), calls=%async_computation.1 | async-start | bytes 1048576 | tf_op jit(solution)/shard_map/all_to_all | solution.py:88
  62.7 164.1 %all-gather.5.cloned.1.call-start = ((), (), s32[]{:S(2)}) async-start(), calls=%async_computation.4 | async-start | bytes 8912896 | tf_op jit(solution)/shard_map/all_gather | solution.py:91
  75.6 3.5 copy-start.10
  83.6 12.9 %copy-start.2 = (bf16[512,4,64]{2,0,1:T(8,128)(2,1)}, bf16[512,4,64]{2,0,1:T(8,128)(2,1)S(1)}, u32[]{:S(2)}) copy-start(bf16[512,4,64]{2,0,1:T(8,128)(2,1)S(1)} %get-tuple-element.19) | copy-start | bytes 786436
  83.6 12.9 %copy-start.3 = (bf16[512,4,64]{2,0,1:T(8,128)(2,1)}, bf16[512,4,64]{2,0,1:T(8,128)(2,1)S(1)}, u32[]{:S(2)}) copy-start(bf16[512,4,64]{2,0,1:T(8,128)(2,1)S(1)} %get-tuple-element.20) | copy-start | bytes 786436
  83.6 12.9 %copy-start.7 = (bf16[512,4,64]{2,0,1:T(8,128)(2,1)S(1)}, bf16[512,4,64]{2,0,1:T(8,128)(2,1)}, u32[]{:S(2)}) copy-start(bf16[512,4,64]{2,0,1:T(8,128)(2,1)} %get-tuple-element.11) | copy-start | bytes 786436
  83.6 12.9 %copy-start.8 = (bf16[512,4,64]{2,0,1:T(8,128)(2,1)S(1)}, bf16[512,4,64]{2,0,1:T(8,128)(2,1)}, u32[]{:S(2)}) copy-start(bf16[512,4,64]{2,0,1:T(8,128)(2,1)} %get-tuple-element.12) | copy-start | bytes 786436
  96.0 264.8 %reduce-scatter.2.cloned.1.call-start = ((), (), s32[]{:S(2)}) async-start(), calls=%async_computation.5 | async-start | bytes 4718592 | tf_op jit(solution)/shard_map/reduce_scatter | solution.py:107
  96.4 4.6 %copy-start.5 = (pred[512,512]{0,1:T(8,128)(4,1)}, pred[512,512]{0,1:T(8,128)(4,1)S(1)}, u32[]{:S(2)}) copy-start(pred[512,512]{0,1:T(8,128)(4,1)S(1)} %fusion.15) | copy-start | bytes 786436
  96.5 4.5 %copy-start.11 = (bf16[512,4096]{1,0:T(8,128)(2,1)S(1)}, bf16[512,4096]{1,0:T(8,128)(2,1)}, u32[]{:S(2)}) copy-start(bf16[512,4096]{1,0:T(8,128)(2,1)} %param.9) | copy-start | bytes 12582916
  96.6 5.0 %copy-start.12 = (bf16[4096,512]{1,0:T(8,128)(2,1)S(1)}, bf16[4096,512]{1,0:T(8,128)(2,1)}, u32[]{:S(2)}) copy-start(bf16[4096,512]{1,0:T(8,128)(2,1)} %param.12) | copy-start | bytes 12582916
  97.9 2.1 copy-start.1
  138.3 22.3 %copy-start = (f32[8192,64]{1,0:T(8,128)S(1)}, f32[8192,64]{1,0:T(8,128)}, u32[]{:S(2)}) copy-start(f32[8192,64]{1,0:T(8,128)} %get-tuple-element.21) | copy-start | bytes 6291460
  239.4 26.7 %copy-start.6 = (pred[512,512]{0,1:T(8,128)(4,1)S(1)}, pred[512,512]{0,1:T(8,128)(4,1)}, u32[]{:S(2)}) copy-start(pred[512,512]{0,1:T(8,128)(4,1)} %copy-done.5) | copy-start | bytes 786436
  239.4 26.7 %copy-start.13 = (bf16[512,512]{0,1:T(8,128)(2,1)S(1)}, bf16[512,512]{0,1:T(8,128)(2,1)}, u32[]{:S(2)}) copy-start(bf16[512,512]{0,1:T(8,128)(2,1)} %convolution_convert_fusion.1) | copy-start | bytes 1572868
  266.1 3.7 %copy-start.4 = (bf16[512,4096]{1,0:T(8,128)(2,1)S(1)}, bf16[512,4096]{1,0:T(8,128)(2,1)}, u32[]{:S(2)}) copy-start(bf16[512,4096]{1,0:T(8,128)(2,1)} %param.13) | copy-start | bytes 12582916
Sparse Core Ops, SparseCore 0:
  47.4 55.8 all-gather.2
  105.0 53.0 all-gather.4
  274.3 86.3 reduce-scatter.1
where the time goes:
time: 369 us; the launch traced here: 367 us
  local copies, waits for them, and re-layouts  103 us (28%)
  waiting for transfers between devices  86.6 us (23%)
  matrix products  81.1 us (22%)
  other arithmetic  59.7 us (16%)
  blocking collectives  18.4 us (5%)
  between operations  14.1 us (4%)
  starting transfers between devices  4.63 us (1%)
    reduce_scatter x1, waiting for transfers between devices, body(): lax.psum_scatter(jnp.dot(attended, w_output, preferred_element_type=jnp.f...  86.6 us
    unnamed x38, local copies, waits for them, and re-layouts  38.8 us
    dot_general x1, matrix products, absorb(): jnp.einsum('qhd,khd->hqk', query, keys, preferred_element_type=jnp.float32)  30 us
    dot_general x1, matrix products, absorb(): jnp.einsum('hqk,khd->qhd', weights, values, preferred_element_type=jnp.fl...  26.7 us
    slice x3, local copies, waits for them, and re-layouts, rope(): first = values[..., :half]  22.5 us
    reduce_sum x1, other arithmetic, absorb(): total = total * shrink + jnp.sum(weights.astype(jnp.float32), axis=2)  21.2 us
    cos x2, other arithmetic, rope(): cosine = jnp.cos(angle)[:, None, :]  18.9 us
    all_to_all x1, blocking collectives, body(): lax.all_to_all(prefix_keys, 'head', split_axis=2, concat_axis=0, tiled=True)  18.4 us
  transfers between devices with their start and end apart: 4, of which 1 were waited for; matrix products, arithmetic and copies ran while one was open for 47% of the time, Pallas kernels for 0%

commit v1 on v0

v1 whole, which is shorter than its diff:
```python
import functools
import math

import jax
import jax.numpy as jnp
import numpy as np
from jax import lax
from jax.experimental import pallas as pl
from jax.experimental.pallas import tpu as pltpu
from jax.sharding import Mesh, PartitionSpec as P

HD = 128
HQL = 4
BLOCK = 16
SUF = 512
PREFIX = 8192
WIDTH = HQL * HD
LOG2E = 1.4426950408889634
VMEM_LIMIT = 48 * 2**20
BF = jnp.bfloat16
F32 = jnp.float32


def frequencies():
    return np.exp(-math.log(10000.0) * np.arange(HD // 2) * 2.0 / HD)


def suffix_tables():
    angle = (PREFIX + np.arange(SUF))[:, None] * frequencies()[None, :]
    cosine, sine = np.cos(angle), np.sin(angle)
    return (
        np.concatenate([cosine, cosine], axis=1).astype(np.float32),
        np.concatenate([-sine, sine], axis=1).astype(np.float32),
    )


def call(kernel, name, flops, nbytes, **kwargs):
    return pl.pallas_call(
        kernel,
        name=name,
        cost_estimate=pl.CostEstimate(
            flops=int(flops), bytes_accessed=int(nbytes), transcendentals=0
        ),
        compiler_params=pltpu.CompilerParams(vmem_limit_bytes=VMEM_LIMIT),
        **kwargs,
    )


def turn(values, cosine, sine):
    return values * cosine + pltpu.roll(values, HD // 2, 1) * sine


def prep_kernel(place, slots, freq, keys, values, *outs):
    y, xhi, slot0 = place[0], place[1], place[2]
    shape = (slots.shape[0], slots.shape[1])
    block = (
        lax.broadcasted_iota(jnp.int32, shape, 0) * shape[1]
        + lax.broadcasted_iota(jnp.int32, shape, 1)
    ).astype(F32)
    rows = keys.shape[0]
    token = lax.broadcasted_iota(jnp.int32, (rows, HD), 0)
    position = jnp.zeros((rows, HD), F32)
    for i in range(rows // BLOCK):
        owner = jnp.sum(jnp.where(slots[...] == slot0 + i, block, 0.0))
        position = jnp.where(token // BLOCK == i, owner * BLOCK, position)
    position = position + (token % BLOCK).astype(F32)
    angle = position * freq[...]
    cosine = jnp.cos(angle)
    lane = lax.broadcasted_iota(jnp.int32, (rows, HD), 1)
    sine = jnp.sin(angle)
    sine = jnp.where(lane < HD // 2, -sine, sine)
    for d, out in enumerate(outs):
        target = lax.rem(y + d, 4)
        for part in range(2):
            group = 2 * target + (xhi if part == 0 else 1 - xhi)
            for h in range(HQL):
                at = pl.ds(pl.multiple_of(group * WIDTH + h * HD, HD), HD)
                to = pl.ds(h * HD, HD)
                turned = turn(keys[:, at].astype(F32), cosine, sine)
                out[pl.ds(part * 2 * rows, rows), to] = turned.astype(BF)
                out[pl.ds((part * 2 + 1) * rows, rows), to] = values[:, at]


def prepare(place, block_slot, keys, values):
    rows = keys.shape[0]
    freq = np.tile(frequencies(), 2)[None, :].astype(np.float32)
    vmem = pl.BlockSpec(memory_space=pltpu.VMEM)
    return call(
        prep_kernel,
        "prepare",
        1e7,
        3 * 2**20,
        in_specs=[pl.BlockSpec(memory_space=pltpu.SMEM)] + [vmem] * 4,
        out_specs=[vmem] * 4,
        out_shape=[jax.ShapeDtypeStruct((4 * rows, WIDTH), BF)] * 4,
    )(place, block_slot.reshape(4, -1), jnp.asarray(freq), keys, values)


def project_kernel(kinds, scale, hidden, *refs):
    n = len(kinds)
    weights, (cosine, sine) = refs[:n], refs[n : n + 2]
    outs, sums = refs[n + 2 : 2 * n + 2], refs[2 * n + 2 :]
    step = pl.program_id(0)
    for weight, total in zip(weights, sums):
        part = jnp.dot(hidden[...], weight[...], preferred_element_type=F32)

        @pl.when(step == 0)
        def _():
            total[...] = part

        @pl.when(step > 0)
        def _():
            total[...] += part

    @pl.when(step == pl.num_programs(0) - 1)
    def _():
        for kind, out, total in zip(kinds, outs, sums):
            for h in range(HQL):
                at = pl.ds(h * HD, HD)
                value = total[:, at]
                if kind != "v":
                    value = turn(value, cosine[...], sine[...])
                if kind == "q":
                    value = value * scale
                out[:, at] = value.astype(BF)


def project(kinds, hidden, weights, tables):
    rows, width = hidden.shape
    deep = 512
    n = len(kinds)
    whole = pl.BlockSpec((rows, HD), lambda i: (0, 0))
    return call(
        functools.partial(project_kernel, kinds, LOG2E / math.sqrt(HD)),
        "project_" + kinds,
        2 * n * rows * width * WIDTH,
        2 * (1 + n) * rows * width,
        grid=(width // deep,),
        in_specs=[pl.BlockSpec((rows, deep), lambda i: (0, i))]
        + [pl.BlockSpec((deep, WIDTH), lambda i: (i, 0))] * n
        + [whole] * 2,
        out_specs=[pl.BlockSpec((rows, WIDTH), lambda i: (0, 0))] * n,
        out_shape=[jax.ShapeDtypeStruct((rows, WIDTH), BF)] * n,
        scratch_shapes=[pltpu.VMEM((rows, WIDTH), F32)] * n,
    )(hidden, *weights, *tables)


def attend_tile(q, k, v_one, mask=None):
    s = lax.dot_general(q, k, (((1,), (1,)), ((), ())), preferred_element_type=F32)
    if mask is not None:
        s = jnp.where(mask, s, -1e30)
    top = jnp.max(s, axis=1, keepdims=True)
    p = jnp.exp2(s - top).astype(BF)
    both = jnp.dot(p, v_one, preferred_element_type=F32)
    return top, both[:, :HD], both[:, HD:]


def widen(v):
    return jnp.concatenate([v, jnp.ones_like(v)], axis=1)


def suffix_kernel(length, q_ref, k_ref, v_ref, o_ref, l_ref):
    h = pl.program_id(0)
    tile = 128
    for t in range(SUF // tile):
        rows, keys = pl.ds(t * tile, tile), (t + 1) * tile
        row = t * tile + lax.broadcasted_iota(jnp.int32, (tile, keys), 0)
        column = lax.broadcasted_iota(jnp.int32, (tile, keys), 1)
        mask = (column <= row) & (column < length[0])
        top, acc, total = attend_tile(
            q_ref[rows, :], k_ref[:keys, :], widen(v_ref[:keys, :]), mask
        )
        o_ref[rows, :] = acc / total
        lane = lax.broadcasted_iota(jnp.int32, (tile, HD), 1)
        l_ref[rows, :] = jnp.where(lane == h, top + jnp.log2(total), l_ref[rows, :])


def suffix_attention(length, q, k, v):
    head = pl.BlockSpec((SUF, HD), lambda h: (0, h))
    return call(
        suffix_kernel,
        "suffix_attention",
        4 * HQL * SUF * SUF * HD,
        4 * 2**20,
        grid=(HQL,),
        in_specs=[pl.BlockSpec(memory_space=pltpu.SMEM)] + [head] * 3,
        out_specs=[head, pl.BlockSpec((SUF, HD), lambda h: (0, 0))],
        out_shape=[
            jax.ShapeDtypeStruct((SUF, WIDTH), F32),
            jax.ShapeDtypeStruct((SUF, HD), F32),
        ],
    )(length, q, k, v)


def prefix_kernel(nq, nkv, held, last, *refs):
    qs, kvs = refs[:nq], refs[nq : nq + nkv]
    old, at = [], nq + nkv
    for has in held:
        old.append(refs[at : at + 2] if has else None)
        at += 2 * has
    outs, stats = refs[at : at + nq], refs[at + nq : at + 2 * nq]
    h = pl.program_id(0)
    half = kvs[0].shape[0] // 2
    k = jnp.concatenate([r[:half, :] for r in kvs], axis=0)
    v_one = widen(jnp.concatenate([r[half:, :] for r in kvs], axis=0))
    tile = 128
    lane = lax.broadcasted_iota(jnp.int32, (tile, HD), 1)
    for r in range(nq):
        for t in range(SUF // tile):
            rows = pl.ds(t * tile, tile)
            top, acc, total = attend_tile(qs[r][rows, :], k, v_one)
            if old[r] is not None:
                before = jnp.max(
                    jnp.where(lane == h, old[r][1][rows, :], -jnp.inf),
                    axis=1,
                    keepdims=True,
                )
                both = jnp.maximum(top, before)
                shrink, grow = jnp.exp2(before - both), jnp.exp2(top - both)
                total = shrink + grow * total
                acc = shrink * old[r][0][rows, :] + grow * acc
                top = both
            outs[r][rows, :] = (acc / total).astype(outs[r].dtype)
            keep = refs[-1].at[r] if last else stats[r]
            keep[rows, :] = jnp.where(lane == h, top + jnp.log2(total), keep[rows, :])
    if last:

        @pl.when(h == HQL - 1)
        def _():
            for r in range(nq):
                stats[r][...] = refs[-1][r].T[: stats[r].shape[0], :]


def prefix_attention(name, qs, kvs, states, last):
    nq, nkv = len(qs), len(kvs)
    held = [state is not None for state in states]
    head = pl.BlockSpec((SUF, HD), lambda h: (0, h))
    piece = pl.BlockSpec((kvs[0].shape[0], HD), lambda h: (0, h))
    stat = pl.BlockSpec((SUF, HD), lambda h: (0, 0))
    flat = pl.BlockSpec((8, SUF), lambda h: (0, 0))
    extra = [x for state in states if state is not None for x in state]
    tokens = nkv * kvs[0].shape[0] // 2
    out = call(
        functools.partial(prefix_kernel, nq, nkv, held, last),
        name,
        2 * 4 * nq * HQL * SUF * tokens * HD,
        nq * 4 * 2**20,
        grid=(HQL,),
        in_specs=[head] * nq + [piece] * nkv + [head, stat] * sum(held),
        out_specs=[head] * nq + [flat if last else stat] * nq,
        out_shape=[jax.ShapeDtypeStruct((SUF, WIDTH), BF if last else F32)] * nq
        + [jax.ShapeDtypeStruct((8, SUF) if last else (SUF, HD), F32)] * nq,
        scratch_shapes=[pltpu.VMEM((nq, SUF, HD), F32)] if last else [],
    )(*qs, *kvs, *extra)
    return list(zip(out[:nq], out[nq:]))


def output_kernel(n, length, *refs):
    parts, stats, weight, out, attended = refs[:n], refs[n : 2 * n], *refs[2 * n :]

    @pl.when(pl.program_id(0) == 0)
    def _():
        columns = []
        for stat in stats:
            tall = jnp.concatenate(
                [stat[...], jnp.zeros((HD - stat.shape[0], SUF), F32)], axis=0
            )
            columns.append(tall.T)
        top = functools.reduce(jnp.maximum, columns)
        shares = [jnp.exp2(c - top) for c in columns]
        total = functools.reduce(lambda a, b: a + b, shares)
        row = lax.broadcasted_iota(jnp.int32, (SUF, HD), 0)
        live = row < length[0]
        for h in range(HQL):
            at = pl.ds(h * HD, HD)
            acc = jnp.zeros((SUF, HD), F32)
            for share, part in zip(shares, parts):
                acc += (share / total)[:, h : h + 1] * part[:, at].astype(F32)
            attended[:, at] = jnp.where(live, acc, 0.0).astype(BF)

    out[...] = jnp.dot(
        attended[...], weight[...], preferred_element_type=F32
    ).astype(BF)


def output_projection(length, pieces, weight):
    n = len(pieces)
    width = weight.shape[1]
    wide = 1024
    whole = pl.BlockSpec((SUF, WIDTH), lambda i: (0, 0))
    flat = pl.BlockSpec((8, SUF), lambda i: (0, 0))
    return call(
        functools.partial(output_kernel, n),
        "output_projection",
        2 * SUF * WIDTH * width,
        12 * 2**20,
        grid=(width // wide,),
        in_specs=[pl.BlockSpec(memory_space=pltpu.SMEM)]
        + [whole] * n
        + [flat] * n
        + [pl.BlockSpec((WIDTH, wide), lambda i: (0, i))],
        out_specs=pl.BlockSpec((SUF, wide), lambda i: (0, i)),
        out_shape=jax.ShapeDtypeStruct((SUF, width), BF),
        scratch_shapes=[pltpu.VMEM((SUF, WIDTH), BF)],
    )(length, *[p[0] for p in pieces], *[p[1] for p in pieces], weight)


def shift(n, by):
    return [(i, (i + by) % n) for i in range(n)]


def body(
    hidden, w_query, w_key, w_value, w_output, prefix_keys, prefix_values, block_slot, suffix_len
):
    slots, block, feats = prefix_keys.shape
    device = lax.axis_index(("xlo", "z", "core", "y", "xhi"))
    y, xhi = lax.axis_index("y"), lax.axis_index("xhi")
    place = jnp.stack([y, xhi, device * slots]).astype(jnp.int32)
    tables = [jnp.asarray(t) for t in suffix_tables()]

    sent = prepare(
        place,
        block_slot,
        prefix_keys.reshape(slots * block, feats),
        prefix_values.reshape(slots * block, feats),
    )
    (q,) = project("q", hidden, [w_query], tables)
    got = [sent[0]] + [lax.ppermute(sent[d], "y", shift(4, d)) for d in (1, 2, 3)]
    qs = [q] + [lax.ppermute(q, "z", shift(4, d)) for d in (1, 2, 3)]
    k_suffix, v_suffix = project("kv", hidden, [w_key, w_value], tables)

    rows = slots * block

    def pack(first):
        return jnp.concatenate(
            [g[first : first + rows] for g in got]
            + [g[first + rows : first + 2 * rows] for g in got],
            axis=0,
        )

    near, far = pack(0), pack(2 * rows)
    cross = [(0, 3), (3, 0), (1, 2), (2, 1)]

    def core(x):
        return lax.ppermute(x, "core", shift(2, 1))

    near_x = lax.ppermute(near, "xlo", shift(2, 1))
    far_x = lax.ppermute(far, ("xlo", "xhi"), cross)
    far_xx = lax.ppermute(far_x, "xlo", shift(2, 1))

    own = suffix_attention(suffix_len, q, k_suffix, v_suffix)
    states = [own, None, None, None]
    states = prefix_attention("attend_near", qs, [near, core(near)], states, False)
    states = prefix_attention(
        "attend_middle", qs, [near_x, far_x, core(near_x), core(far_x)], states, False
    )
    final = [far_xx, core(far_xx)]
    pieces = []
    for d in (2, 1, 3, 0):
        part, stat = prefix_attention("attend_last", [qs[d]], final, [states[d]], True)[0]
        if d:
            part = lax.ppermute(part, "z", shift(4, -d))
            stat = lax.ppermute(stat, "z", shift(4, -d))
        pieces.append((part, stat))
    partial = output_projection(suffix_len, pieces, w_output)
    shares = lax.all_to_all(
        partial.reshape(8, SUF // 8, feats), ("y", "xhi"), split_axis=0, concat_axis=0
    )
    return jnp.sum(shares.astype(F32), axis=0).astype(BF)


def solution(mesh):
    fine = Mesh(
        mesh.devices.reshape(2, 4, 2, 4, 2), ("xlo", "z", "core", "y", "xhi")
    )
    pool, head = ("xlo", "z", "core"), ("y", "xhi")
    placed = (
        P(pool, None),
        P(None, head),
        P(None, head),
        P(None, head),
        P(head, None),
        P(pool + head, None, None),
        P(pool + head, None, None),
        P(),
        P(pool),
    )
    return jax.shard_map(
        body, mesh=fine, in_specs=placed, out_specs=P(pool + head, None), check_vma=False
    )
```

time: 369 us -> 197 us (0.53)
  local copies, waits for them, and re-layouts: 103 us -> 12.9 us
  matrix products: 81.1 us -> 0 us
  Pallas kernels: 0 us -> 69.7 us
  waiting for transfers between devices: 86.6 us -> 26.2 us
  other arithmetic: 59.7 us -> 3.92 us
  blocking collectives: 18.4 us -> 54 us
  starting transfers between devices: 4.63 us -> 28.7 us
  between operations: 14.1 us -> 0.86 us
    reduce_scatter x1 -> x0, waiting for transfers between devices: 86.6 us -> none  [body(): lax.psum_scatter(jnp.dot(attended, w_output, preferred_element_type=jnp.f...]
    dot_general x8 -> x0, matrix products: 81.1 us -> none  [the longest x1 30 us: absorb(): jnp.einsum('qhd,khd->hqk', query, keys, preferred_element_type=jnp.float32)]
    pallas_call x0 -> x11, Pallas kernels: none -> 69.7 us  [the longest x6 37.3 us: prefix_attention(): call(functools.partial(prefix_kernel, nq, nkv, held, last), name, 2 * 4 *...]
    all_to_all x1, blocking collectives: 18.4 us -> 54 us  [body(): lax.all_to_all(partial.reshape(8, SUF // 8, feats), ('y', 'xhi'), split_a...]
    ppermute x0 -> x19, starting transfers between devices: none -> 28.7 us  [the longest x3 7.19 us: body(): qs = [q] + [lax.ppermute(q, 'z', shift(4, d)) for d in (1, 2, 3)]]
    reshape x2 -> x0, local copies, waits for them, and re-layouts: 28.1 us -> none  [the longest x1 15.6 us: rotate_keys(): keys.astype(jnp.float32).reshape(count * block, feats // HD, HD)]
    ppermute x0 -> x19, waiting for transfers between devices: none -> 26.2 us  [the longest x3 14.7 us: body(): qs = [q] + [lax.ppermute(q, 'z', shift(4, d)) for d in (1, 2, 3)]]
    unnamed x38 -> x35, local copies, waits for them, and re-layouts: 38.8 us -> 12.9 us
  transfers between devices with their start and end apart: 4 -> 19, of which waited for: 1 -> 5; matrix products, arithmetic and copies ran while one was open for 47% -> 0% of each run, Pallas kernels for 0% -> 29%
where the time goes in v1:
time: 197 us; the launch traced here: 196 us
  Pallas kernels  69.7 us (35%)
  blocking collectives  54 us (27%)
  starting transfers between devices  28.7 us (15%)
  waiting for transfers between devices  26.2 us (13%)
  local copies, waits for them, and re-layouts  12.9 us (7%)
  other arithmetic  3.92 us (2%)
    all_to_all x1, blocking collectives, body(): lax.all_to_all(partial.reshape(8, SUF // 8, feats), ('y', 'xhi'), split_a...  54 us
    pallas_call x6, Pallas kernels, prefix_attention(): call(functools.partial(prefix_kernel, nq, nkv, held, last), name, 2 * 4 *...  37.3 us
    pallas_call x2, Pallas kernels, project(): call(functools.partial(project_kernel, kinds, LOG2E / math.sqrt(HD)), 'pr...  18.3 us
    ppermute x3, waiting for transfers between devices, body(): qs = [q] + [lax.ppermute(q, 'z', shift(4, d)) for d in (1, 2, 3)]  14.7 us
    unnamed x35, local copies, waits for them, and re-layouts  12.9 us
    ppermute x3, waiting for transfers between devices, body(): stat = lax.ppermute(stat, 'z', shift(4, -d))  10.3 us
    pallas_call x1, Pallas kernels, output_projection(): call(functools.partial(output_kernel, n), 'output_projection', 2 * SUF *...  7.84 us
    ppermute x3, starting transfers between devices, body(): qs = [q] + [lax.ppermute(q, 'z', shift(4, d)) for d in (1, 2, 3)]  7.19 us
  transfers between devices with their start and end apart: 19, of which 5 were waited for; matrix products, arithmetic and copies ran while one was open for 0% of the time, Pallas kernels for 29%

profile of v1, /device:TPU:0, one launch (start us, length us, event | category | flops | bytes accessed | tf_op | source)
XLA Modules:
  0.0 196.2 jit_solution(15626874586087264868)
XLA Ops:
  0.0 0.1 pad_add_fusion.place
  0.1 1.0 copy-done.1
  1.1 1.0 copy-done.2
  2.2 0.7 copy-done.5
  2.8 0.7 copy-done.6
  3.5 1.1 prepare.1
  4.6 1.7 collective-permute-start.1
  6.3 2.9 %collective-permute-start.2 = (bf16[256,512]{1,0:T(8,128)(2,1)S(1)}, bf16[256,512]{1,0:T(8,128)(2,1)S(1)}, u32[]{:S(2)}, u32[]{:S(2)}) collective-permute-start(bf16[256,512]{1,0:T(8,128)(2,1)S(1)} %get-tuple-element.39), channel_id=1, source_target_pairs={{0,4},{2,6},{4,0},{6,2},{1,5},{3,7},{5,1},{7,3},{8,12},{10,14},{12... | collective-permute-start | bytes 786440 | tf_op jit(solution)/shard_map/ppermute | solution.py:328
  9.2 1.3 collective-permute-start.3
  10.6 2.2 %copy-done = bf16[512,4096]{1,0:T(8,128)(2,1)S(1)} copy-done((bf16[512,4096]{1,0:T(8,128)(2,1)S(1)}, bf16[512,4096]{1,0:T(8,128)(2,1)}, u32[]{:S(2)}) %copy-start) | copy-done | bytes 4194328
  12.8 0.9 copy-done.3
  13.7 0.9 copy-done.4
  14.7 7.5 %project_q.1.q_ref.refs_0_ = bf16[512,512]{1,0:T(8,128)(2,1)S(1)} custom-call(bf16[512,4096]{1,0:T(8,128)(2,1)S(1)} %copy-done, bf16[4096,512]{1,0:T(8,128)(2,1)} %refs_0_.2, f32[512,128]{1,0:T(8,128)S(1)} %copy-done.3, f32[512,128]{1,0:T(8,128)S(1)} %copy-done.4), custom_call_target="tpu_custom_call" | custom-call | flops 2147483648 | bytes 8388608 | tf_op jit(solution)/shard_map/project_q/pallas_call | solution.py:133
  22.2 4.0 %collective-permute-start = (bf16[512,512]{1,0:T(8,128)(2,1)S(1)}, bf16[512,512]{1,0:T(8,128)(2,1)S(1)}, u32[]{:S(2)}, u32[]{:S(2)}) collective-permute-start(bf16[512,512]{1,0:T(8,128)(2,1)S(1)} %project_q.1.q_ref.refs_0_), channel_id=1, source_target_pairs={{0,32},{16,48},{32,0},{48,16},{1,33},{17,49},{33,1},{49,17},{2,34}... | collective-permute-start | bytes 1572872 | tf_op jit(solution)/shard_map/ppermute | solution.py:329
  26.3 2.8 %collective-permute-start.4 = (bf16[512,512]{1,0:T(8,128)(2,1)S(1)}, bf16[512,512]{1,0:T(8,128)(2,1)S(1)}, u32[]{:S(2)}, u32[]{:S(2)}) collective-permute-start(bf16[512,512]{1,0:T(8,128)(2,1)S(1)} %get-tuple-element.70), channel_id=1, source_target_pairs={{0,65},{65,0},{1,64},{64,1},{2,67},{67,2},{3,66},{66,3},{4,69},{69... | collective-permute-start | bytes 1572872 | tf_op jit(solution)/shard_map/ppermute | solution.py:348
  29.2 1.0 collective-permute-start.7
  30.2 0.2 collective-permute-start.9
  30.4 2.2 %collective-permute-start.8 = (bf16[512,512]{1,0:T(8,128)(2,1)S(1)}, bf16[512,512]{1,0:T(8,128)(2,1)S(1)}, u32[]{:S(2)}, u32[]{:S(2)}) collective-permute-start(bf16[512,512]{1,0:T(8,128)(2,1)S(1)} %project_q.1.q_ref.refs_0_), channel_id=1, source_target_pairs={{0,48},{16,0},{32,16},{48,32},{1,49},{17,1},{33,17},{49,33},{2,50}... | collective-permute-start | bytes 1572872 | tf_op jit(solution)/shard_map/ppermute | solution.py:329
  32.6 6.4 %collective-permute-done.refs_2_.refs_0_ = bf16[512,512]{1,0:T(8,128)(2,1)S(1)} collective-permute-done((bf16[512,512]{1,0:T(8,128)(2,1)S(1)}, bf16[512,512]{1,0:T(8,128)(2,1)S(1)}, u32[]{:S(2)}, u32[]{:S(2)}) %collective-permute-start) | collective-permute-done | bytes 524320 | tf_op jit(solution)/shard_map/ppermute | solution.py:329
  39.0 0.0 collective-permute-start.12
  39.0 1.1 collective-permute-done.4.refs_5_
  40.2 8.3 %collective-permute-done.7.refs_1_.refs_0_ = bf16[512,512]{1,0:T(8,128)(2,1)S(1)} collective-permute-done((bf16[512,512]{1,0:T(8,128)(2,1)S(1)}, bf16[512,512]{1,0:T(8,128)(2,1)S(1)}, u32[]{:S(2)}, u32[]{:S(2)}) %collective-permute-start.7) | collective-permute-done | bytes 524320 | tf_op jit(solution)/shard_map/ppermute | solution.py:329
  48.5 1.5 collective-permute-start.5
  50.0 0.0 collective-permute-start.10
  50.0 10.8 %project_kv.1 = (bf16[512,512]{1,0:T(8,128)(2,1)S(1)}, bf16[512,512]{1,0:T(8,128)(2,1)S(1)}) custom-call(bf16[512,4096]{1,0:T(8,128)(2,1)S(1)} %copy-done, bf16[4096,512]{1,0:T(8,128)(2,1)} %refs_0_.3, bf16[4096,512]{1,0:T(8,128)(2,1)} %refs_1_.2, f32[512,128]{1,0:T(8,128)S(1)} %copy-done.3, f32[512,128]{1,0:T(8,128)S(1)} %copy-done.4), custom_call_target="tpu_custom_call" | custom-call | flops 4294967296 | bytes 12582912 | tf_op jit(solution)/shard_map/project_kv/pallas_call | solution.py:133
  61.4 5.2 %suffix_attention.1 = (f32[512,512]{1,0:T(8,128)S(1)}, f32[512,128]{1,0:T(8,128)S(1)}) custom-call(s32[1]{0:T(128)S(6)} %copy.27.length, bf16[512,512]{1,0:T(8,128)(2,1)S(1)} %project_q.1.q_ref.refs_0_, bf16[512,512]{1,0:T(8,128)(2,1)S(1)} %get-tuple-element.41.k_ref, bf16[512,512]{1,0:T(8,128)(2,1)S(1)} %get-tuple-element.42.v_ref), custom_call_target="tpu_custom_call" | custom-call | flops 536870912 | bytes 4194304 | tf_op jit(solution)/shard_map/suffix_attention/pallas_call | solution.py:180
  66.6 1.0 copy-done.7
  67.5 8.7 %attend_near.1 = (f32[512,512]{1,0:T(8,128)S(1)}, f32[512,512]{1,0:T(8,128)}, f32[512,512]{1,0:T(8,128)}, f32[512,512]{1,0:T(8,128)}, f32[512,128]{1,0:T(8,128)S...) custom-call(bf16[512,512]{1,0:T(8,128)(2,1)S(1)} %project_q.1.q_ref.refs_0_, ...), custom_call_target="tpu_custom_call" | custom-call | flops 4294967296 | bytes 16777216 | tf_op jit(solution)/shard_map/attend_near/pallas_call | solution.py:243
  76.3 1.0 copy-done.12
  77.3 0.5 collective-permute-start.6
  77.8 0.8 copy-done.13
  78.6 15.0 %attend_middle.1 = (f32[512,512]{1,0:T(8,128)}, f32[512,512]{1,0:T(8,128)}, f32[512,512]{1,0:T(8,128)}, f32[512,512]{1,0:T(8,128)}, f32[512,128]{1,0:T(8,128)S(1...) custom-call(bf16[512,512]{1,0:T(8,128)(2,1)S(1)} %project_q.1.q_ref.refs_0_, ...), custom_call_target="tpu_custom_call" | custom-call | flops 8589934592 | bytes 16777216 | tf_op jit(solution)/shard_map/attend_middle/pallas_call | solution.py:243
  93.6 1.3 copy-done.11
  94.9 3.4 %attend_last.6 = (bf16[512,512]{1,0:T(8,128)(2,1)S(1)}, f32[8,512]{1,0:T(8,128)S(1)}) custom-call(bf16[512,512]{1,0:T(8,128)(2,1)S(1)} %collective-permute-done.8.refs_3_.refs_0_, bf16[512,512]{1,0:T(8,128)(2,1)S(1)} %collective-permute-done.5.refs_1_, bf16[512,512]{1,0:T(8,128)(2,1)S(1)} %collective-permute-done.6.refs_2_, f32[512,512]{1,0:T(8,128)S(1)} %copy-done.11, ...), custom_call_target="tpu_custom_call" | custom-call | flops 1073741824 | bytes 4194304 | tf_op jit(solution)/shard_map/attend_last/pallas_call | solution.py:243
  98.3 1.8 collective-permute-start.15
  100.1 1.2 copy-done.10
  101.4 3.4 %attend_last.5 = (bf16[512,512]{1,0:T(8,128)(2,1)S(1)}, f32[8,512]{1,0:T(8,128)S(1)}) custom-call(bf16[512,512]{1,0:T(8,128)(2,1)S(1)} %collective-permute-done.7.refs_1_.refs_0_, bf16[512,512]{1,0:T(8,128)(2,1)S(1)} %collective-permute-done.5.refs_1_, bf16[512,512]{1,0:T(8,128)(2,1)S(1)} %collective-permute-done.6.refs_2_, f32[512,512]{1,0:T(8,128)S(1)} %copy-done.10, ...), custom_call_target="tpu_custom_call" | custom-call | flops 1073741824 | bytes 4194304 | tf_op jit(solution)/shard_map/attend_last/pallas_call | solution.py:243
  104.8 1.5 collective-permute-start.14
  106.3 3.4 %attend_last.4 = (bf16[512,512]{1,0:T(8,128)(2,1)S(1)}, f32[8,512]{1,0:T(8,128)S(1)}) custom-call(bf16[512,512]{1,0:T(8,128)(2,1)S(1)} %collective-permute-done.refs_2_.refs_0_, bf16[512,512]{1,0:T(8,128)(2,1)S(1)} %collective-permute-done.5.refs_1_, bf16[512,512]{1,0:T(8,128)(2,1)S(1)} %collective-permute-done.6.refs_2_, f32[512,512]{1,0:T(8,128)S(1)} %copy-done.9, ...), custom_call_target="tpu_custom_call" | custom-call | flops 1073741824 | bytes 4194304 | tf_op jit(solution)/shard_map/attend_last/pallas_call | solution.py:243
  109.7 2.1 %collective-permute-start.13 = (bf16[512,512]{1,0:T(8,128)(2,1)S(1)}, bf16[512,512]{1,0:T(8,128)(2,1)S(1)}, u32[]{:S(2)}, u32[]{:S(2)}) collective-permute-start(bf16[512,512]{1,0:T(8,128)(2,1)S(1)} %get-tuple-element.55), channel_id=1, source_target_pairs={{0,32},{16,48},{32,0},{48,16},{1,33},{17,49},{33,1},{49,17},{2,34}... | collective-permute-start | bytes 1572872 | tf_op jit(solution)/shard_map/ppermute | solution.py:362
  111.8 3.2 %collective-permute-start.17 = (f32[8,512]{1,0:T(8,128)S(1)}, f32[8,512]{1,0:T(8,128)S(1)}, u32[]{:S(2)}, u32[]{:S(2)}) collective-permute-start(f32[8,512]{1,0:T(8,128)S(1)} %get-tuple-element.66), channel_id=1, source_target_pairs={{0,48},{16,0},{32,16},{48,32},{1,49},{17,1},{33,17},{49,33},{2,50}... | collective-permute-start | bytes 49160 | tf_op jit(solution)/shard_map/ppermute | solution.py:363
  115.0 10.2 %collective-permute-done.18.refs_6_ = f32[8,512]{1,0:T(8,128)S(1)} collective-permute-done((f32[8,512]{1,0:T(8,128)S(1)}, f32[8,512]{1,0:T(8,128)S(1)}, u32[]{:S(2)}, u32[]{:S(2)}) %collective-permute-start.18) | collective-permute-done | bytes 16416 | tf_op jit(solution)/shard_map/ppermute | solution.py:363
  125.3 1.7 collective-permute-start.16
  127.0 3.4 %attend_last.7 = (bf16[512,512]{1,0:T(8,128)(2,1)S(1)}, f32[8,512]{1,0:T(8,128)S(1)}) custom-call(bf16[512,512]{1,0:T(8,128)(2,1)S(1)} %project_q.1.q_ref.refs_0_, bf16[512,512]{1,0:T(8,128)(2,1)S(1)} %collective-permute-done.5.refs_1_, bf16[512,512]{1,0:T(8,128)(2,1)S(1)} %collective-permute-done.6.refs_2_, f32[512,512]{1,0:T(8,128)S(1)} %copy-done.8, ...), custom_call_target="tpu_custom_call" | custom-call | flops 1073741824 | bytes 4194304 | tf_op jit(solution)/shard_map/attend_last/pallas_call | solution.py:243
  130.5 0.1 collective-permute-done.16.refs_4_
  130.6 7.8 %output_projection.1 = bf16[512,4096]{1,0:T(8,128)(2,1)} custom-call(s32[1]{0:T(128)S(6)} %copy.27.length, bf16[512,512]{1,0:T(8,128)(2,1)S(1)} %collective-permute-done.13.refs_0_, bf16[512,512]{1,0:T(8,128)(2,1)S(1)} %collective-permute-done.14.refs_1_, bf16[512,512]{1,0:T(8,128)(2,1)S(1)} %collective-permute-done.15.refs_2_, ...), custom_call_target="tpu_custom_call" | custom-call | flops 2147483648 | bytes 12582912 | tf_op jit(solution)/shard_map/output_projection/pallas_call | solution.py:292
  138.4 54.0 %all_to_all.5 = bf16[8,64,4096]{2,1,0:T(8,128)(2,1)} all-to-all(bf16[8,64,4096]{2,1,0:T(8,128)(2,1)} %bitcast.10), channel_id=1, replica_groups=mesh['xlo'=2,'z'=4,'core'=2,'y'=4,'xhi'=2] {'y','xhi'}, dimensions={0} | all-to-all | bytes 8388608 | tf_op jit(solution)/shard_map/all_to_all | solution.py:366
  192.4 3.8 %reduce_sum.12 = bf16[64,4096]{1,0:T(8,128)(2,1)} reduce(bf16[8,64,4096]{2,1,0:T(8,128)(2,1)} %all_to_all.5, bf16[]{:T(256)} %constant.37.clone.1), dimensions={0}, to_apply=%region_0.0 | reduce | flops 1835008 | bytes 4718594 | tf_op jit(solution)/shard_map/reduce_sum | solution.py:369
  (40 shorter events, 0.2 us)
Async XLA Ops:
  0.1 1.0 copy-start.1
  1.1 1.0 copy-start.2
  2.2 0.7 copy-start.5
  2.8 0.7 copy-start.6
  4.6 21.6 %collective-permute-start.1 = (bf16[256,512]{1,0:T(8,128)(2,1)S(1)}, bf16[256,512]{1,0:T(8,128)(2,1)S(1)}, u32[]{:S(2)}, u32[]{:S(2)}) collective-permute-start(bf16[256,512]{1,0:T(8,128)(2,1)S(1)} %get-tuple-element.38), channel_id=1, source_target_pairs={{0,2},{2,4},{4,6},{6,0},{1,3},{3,5},{5,7},{7,1},{8,10},{10,12},{12... | collective-permute-start | bytes 786440 | tf_op jit(solution)/shard_map/ppermute | solution.py:328
  6.3 19.9 %collective-permute-start.2 = (bf16[256,512]{1,0:T(8,128)(2,1)S(1)}, bf16[256,512]{1,0:T(8,128)(2,1)S(1)}, u32[]{:S(2)}, u32[]{:S(2)}) collective-permute-start(bf16[256,512]{1,0:T(8,128)(2,1)S(1)} %get-tuple-element.39), channel_id=1, source_target_pairs={{0,4},{2,6},{4,0},{6,2},{1,5},{3,7},{5,1},{7,3},{8,12},{10,14},{12... | collective-permute-start | bytes 786440 | tf_op jit(solution)/shard_map/ppermute | solution.py:328
  9.2 17.0 %collective-permute-start.3 = (bf16[256,512]{1,0:T(8,128)(2,1)S(1)}, bf16[256,512]{1,0:T(8,128)(2,1)S(1)}, u32[]{:S(2)}, u32[]{:S(2)}) collective-permute-start(bf16[256,512]{1,0:T(8,128)(2,1)S(1)} %get-tuple-element.40), channel_id=1, source_target_pairs={{0,6},{2,0},{4,2},{6,4},{1,7},{3,1},{5,3},{7,5},{8,14},{10,8},{12,... | collective-permute-start | bytes 786440 | tf_op jit(solution)/shard_map/ppermute | solution.py:328
  10.6 2.2 %copy-start = (bf16[512,4096]{1,0:T(8,128)(2,1)S(1)}, bf16[512,4096]{1,0:T(8,128)(2,1)}, u32[]{:S(2)}) copy-start(bf16[512,4096]{1,0:T(8,128)(2,1)} %hidden.3) | copy-start | bytes 12582916
  12.8 0.9 copy-start.3
  13.7 0.9 copy-start.4
  22.2 16.8 %collective-permute-start = (bf16[512,512]{1,0:T(8,128)(2,1)S(1)}, bf16[512,512]{1,0:T(8,128)(2,1)S(1)}, u32[]{:S(2)}, u32[]{:S(2)}) collective-permute-start(bf16[512,512]{1,0:T(8,128)(2,1)S(1)} %project_q.1.q_ref.refs_0_), channel_id=1, source_target_pairs={{0,32},{16,48},{32,0},{48,16},{1,33},{17,49},{33,1},{49,17},{2,34}... | collective-permute-start | bytes 1572872 | tf_op jit(solution)/shard_map/ppermute | solution.py:329
  26.3 13.8 %collective-permute-start.4 = (bf16[512,512]{1,0:T(8,128)(2,1)S(1)}, bf16[512,512]{1,0:T(8,128)(2,1)S(1)}, u32[]{:S(2)}, u32[]{:S(2)}) collective-permute-start(bf16[512,512]{1,0:T(8,128)(2,1)S(1)} %get-tuple-element.70), channel_id=1, source_target_pairs={{0,65},{65,0},{1,64},{64,1},{2,67},{67,2},{3,66},{66,3},{4,69},{69... | collective-permute-start | bytes 1572872 | tf_op jit(solution)/shard_map/ppermute | solution.py:348
  29.2 19.3 %collective-permute-start.7 = (bf16[512,512]{1,0:T(8,128)(2,1)S(1)}, bf16[512,512]{1,0:T(8,128)(2,1)S(1)}, u32[]{:S(2)}, u32[]{:S(2)}) collective-permute-start(bf16[512,512]{1,0:T(8,128)(2,1)S(1)} %project_q.1.q_ref.refs_0_), channel_id=1, source_target_pairs={{0,16},{16,32},{32,48},{48,0},{1,17},{17,33},{33,49},{49,1},{2,18}... | collective-permute-start | bytes 1572872 | tf_op jit(solution)/shard_map/ppermute | solution.py:329
  30.2 19.8 %collective-permute-start.9 = (bf16[512,512]{1,0:T(8,128)(2,1)S(1)}, bf16[512,512]{1,0:T(8,128)(2,1)S(1)}, u32[]{:S(2)}, u32[]{:S(2)}) collective-permute-start(bf16[512,512]{1,0:T(8,128)(2,1)S(1)} %get-tuple-element.69.refs_4_), channel_id=1, source_target_pairs={{0,64},{64,0},{1,65},{65,1},{2,66},{66,2},{3,67},{67,3},{4,68},{68... | collective-permute-start | bytes 1572872 | tf_op jit(solution)/shard_map/ppermute | solution.py:347
  30.4 37.1 %collective-permute-start.8 = (bf16[512,512]{1,0:T(8,128)(2,1)S(1)}, bf16[512,512]{1,0:T(8,128)(2,1)S(1)}, u32[]{:S(2)}, u32[]{:S(2)}) collective-permute-start(bf16[512,512]{1,0:T(8,128)(2,1)S(1)} %project_q.1.q_ref.refs_0_), channel_id=1, source_target_pairs={{0,48},{16,0},{32,16},{48,32},{1,49},{17,1},{33,17},{49,33},{2,50}... | collective-permute-start | bytes 1572872 | tf_op jit(solution)/shard_map/ppermute | solution.py:329
  39.0 28.5 %collective-permute-start.12 = (bf16[512,512]{1,0:T(8,128)(2,1)S(1)}, bf16[512,512]{1,0:T(8,128)(2,1)S(1)}, u32[]{:S(2)}, u32[]{:S(2)}) collective-permute-start(bf16[512,512]{1,0:T(8,128)(2,1)S(1)} %get-tuple-element.69.refs_4_), channel_id=1, source_target_pairs={{0,8},{8,0},{1,9},{9,1},{2,10},{10,2},{3,11},{11,3},{4,12},{12,4},... | collective-permute-start | bytes 1572872 | tf_op jit(solution)/shard_map/ppermute | solution.py:345
  40.2 37.6 %collective-permute-start.11 = (bf16[512,512]{1,0:T(8,128)(2,1)S(1)}, bf16[512,512]{1,0:T(8,128)(2,1)S(1)}, u32[]{:S(2)}, u32[]{:S(2)}) collective-permute-start(bf16[512,512]{1,0:T(8,128)(2,1)S(1)} %collective-permute-done.4.refs_5_), channel_id=1, source_target_pairs={{0,8},{8,0},{1,9},{9,1},{2,10},{10,2},{3,11},{11,3},{4,12},{12,4},... | collective-permute-start | bytes 1572872 | tf_op jit(solution)/shard_map/ppermute | solution.py:345
  48.5 28.8 %collective-permute-start.5 = (bf16[512,512]{1,0:T(8,128)(2,1)S(1)}, bf16[512,512]{1,0:T(8,128)(2,1)S(1)}, u32[]{:S(2)}, u32[]{:S(2)}) collective-permute-start(bf16[512,512]{1,0:T(8,128)(2,1)S(1)} %collective-permute-done.4.refs_5_), channel_id=1, source_target_pairs={{0,64},{64,0},{1,65},{65,1},{2,66},{66,2},{3,67},{67,3},{4,68},{68... | collective-permute-start | bytes 1572872 | tf_op jit(solution)/shard_map/ppermute | solution.py:349
  50.0 27.8 %collective-permute-start.10 = (bf16[512,512]{1,0:T(8,128)(2,1)S(1)}, bf16[512,512]{1,0:T(8,128)(2,1)S(1)}, u32[]{:S(2)}, u32[]{:S(2)}) collective-permute-start(bf16[512,512]{1,0:T(8,128)(2,1)S(1)} %collective-permute-done.9.refs_4_), channel_id=1, source_target_pairs={{0,8},{8,0},{1,9},{9,1},{2,10},{10,2},{3,11},{11,3},{4,12},{12,4},... | collective-permute-start | bytes 1572872 | tf_op jit(solution)/shard_map/ppermute | solution.py:345
  66.6 1.0 copy-start.7
  76.3 1.0 copy-start.12
  77.3 16.3 %collective-permute-start.6 = (bf16[512,512]{1,0:T(8,128)(2,1)S(1)}, bf16[512,512]{1,0:T(8,128)(2,1)S(1)}, u32[]{:S(2)}, u32[]{:S(2)}) collective-permute-start(bf16[512,512]{1,0:T(8,128)(2,1)S(1)} %collective-permute-done.5.refs_1_), channel_id=1, source_target_pairs={{0,8},{8,0},{1,9},{9,1},{2,10},{10,2},{3,11},{11,3},{4,12},{12,4},... | collective-permute-start | bytes 1572872 | tf_op jit(solution)/shard_map/ppermute | solution.py:345
  77.8 0.8 copy-start.13
  93.6 12.7 %copy-start.9 = (f32[512,512]{1,0:T(8,128)S(1)}, f32[512,512]{1,0:T(8,128)}, u32[]{:S(2)}) copy-start(f32[512,512]{1,0:T(8,128)} %get-tuple-element.53.refs_3_) | copy-start | bytes 3145732
  93.6 1.3 copy-start.11
  98.3 28.8 %copy-start.8 = (f32[512,512]{1,0:T(8,128)S(1)}, f32[512,512]{1,0:T(8,128)}, u32[]{:S(2)}) copy-start(f32[512,512]{1,0:T(8,128)} %get-tuple-element.62.refs_3_) | copy-start | bytes 3145732
  98.3 32.2 %collective-permute-start.15 = (bf16[512,512]{1,0:T(8,128)(2,1)S(1)}, bf16[512,512]{1,0:T(8,128)(2,1)S(1)}, u32[]{:S(2)}, u32[]{:S(2)}) collective-permute-start(bf16[512,512]{1,0:T(8,128)(2,1)S(1)} %get-tuple-element.61), channel_id=1, source_target_pairs={{0,16},{16,32},{32,48},{48,0},{1,17},{17,33},{33,49},{49,1},{2,18}... | collective-permute-start | bytes 1572872 | tf_op jit(solution)/shard_map/ppermute | solution.py:362
  100.1 1.2 copy-start.10
  104.8 25.8 %collective-permute-start.14 = (bf16[512,512]{1,0:T(8,128)(2,1)S(1)}, bf16[512,512]{1,0:T(8,128)(2,1)S(1)}, u32[]{:S(2)}, u32[]{:S(2)}) collective-permute-start(bf16[512,512]{1,0:T(8,128)(2,1)S(1)} %get-tuple-element.58), channel_id=1, source_target_pairs={{0,48},{16,0},{32,16},{48,32},{1,49},{17,1},{33,17},{49,33},{2,50}... | collective-permute-start | bytes 1572872 | tf_op jit(solution)/shard_map/ppermute | solution.py:362
  109.7 20.9 %collective-permute-start.13 = (bf16[512,512]{1,0:T(8,128)(2,1)S(1)}, bf16[512,512]{1,0:T(8,128)(2,1)S(1)}, u32[]{:S(2)}, u32[]{:S(2)}) collective-permute-start(bf16[512,512]{1,0:T(8,128)(2,1)S(1)} %get-tuple-element.55), channel_id=1, source_target_pairs={{0,32},{16,48},{32,0},{48,16},{1,33},{17,49},{33,1},{49,17},{2,34}... | collective-permute-start | bytes 1572872 | tf_op jit(solution)/shard_map/ppermute | solution.py:362
  111.8 13.5 %collective-permute-start.18 = (f32[8,512]{1,0:T(8,128)S(1)}, f32[8,512]{1,0:T(8,128)S(1)}, u32[]{:S(2)}, u32[]{:S(2)}) collective-permute-start(f32[8,512]{1,0:T(8,128)S(1)} %get-tuple-element.67), channel_id=1, source_target_pairs={{0,16},{16,32},{32,48},{48,0},{1,17},{17,33},{33,49},{49,1},{2,18}... | collective-permute-start | bytes 49160 | tf_op jit(solution)/shard_map/ppermute | solution.py:363
  111.8 18.6 %collective-permute-start.17 = (f32[8,512]{1,0:T(8,128)S(1)}, f32[8,512]{1,0:T(8,128)S(1)}, u32[]{:S(2)}, u32[]{:S(2)}) collective-permute-start(f32[8,512]{1,0:T(8,128)S(1)} %get-tuple-element.66), channel_id=1, source_target_pairs={{0,48},{16,0},{32,16},{48,32},{1,49},{17,1},{33,17},{49,33},{2,50}... | collective-permute-start | bytes 49160 | tf_op jit(solution)/shard_map/ppermute | solution.py:363
  125.3 5.2 %collective-permute-start.16 = (f32[8,512]{1,0:T(8,128)S(1)}, f32[8,512]{1,0:T(8,128)S(1)}, u32[]{:S(2)}, u32[]{:S(2)}) collective-permute-start(f32[8,512]{1,0:T(8,128)S(1)} %get-tuple-element.65), channel_id=1, source_target_pairs={{0,32},{16,48},{32,0},{48,16},{1,33},{17,49},{33,1},{49,17},{2,34}... | collective-permute-start | bytes 49160 | tf_op jit(solution)/shard_map/ppermute | solution.py:363

commit v2 on v1

v2 whole, which is shorter than its diff:
```python
import functools
import math

import jax
import jax.numpy as jnp
import numpy as np
from jax import lax
from jax.experimental import pallas as pl
from jax.experimental.pallas import tpu as pltpu
from jax.sharding import Mesh, PartitionSpec as P

HD = 128
HQL = 4
BLOCK = 16
SUF = 512
PREFIX = 8192
WIDTH = HQL * HD
LOG2E = 1.4426950408889634
EXTRA = 16
SLABS = 8
BF = jnp.bfloat16
F32 = jnp.float32


def frequencies():
    return np.exp(-math.log(10000.0) * np.arange(HD // 2) * 2.0 / HD)


def suffix_tables():
    angle = (PREFIX + np.arange(SUF))[:, None] * frequencies()[None, :]
    cosine, sine = np.cos(angle), np.sin(angle)
    return (
        np.concatenate([cosine, cosine], axis=1).astype(np.float32),
        np.concatenate([-sine, sine], axis=1).astype(np.float32),
    )


def call(kernel, name, vmem=24, flops=1, **kwargs):
    return pl.pallas_call(
        kernel,
        name=name,
        cost_estimate=pl.CostEstimate(flops=flops, bytes_accessed=1, transcendentals=0),
        compiler_params=pltpu.CompilerParams(vmem_limit_bytes=vmem * 2**20),
        **kwargs,
    )


def turn(values, cosine, sine):
    return values * cosine + pltpu.roll(values, HD // 2, 1) * sine


def prep_kernel(slots, freq, keys_hbm, values_hbm, *refs):
    outs, (keys, values, sems) = refs[:-3], refs[-3:]
    copies = [
        pltpu.make_async_copy(keys_hbm, keys, sems.at[0]),
        pltpu.make_async_copy(values_hbm, values, sems.at[1]),
    ]
    for copy in copies:
        copy.start()
    y, xhi = lax.axis_index("y"), lax.axis_index("xhi")
    chip = lax.axis_index("xlo") * 4 + lax.axis_index("z")
    device = (chip * 2 + lax.axis_index("core")) * 8 + y * 2 + xhi
    slot0 = device * (keys.shape[0] // BLOCK)
    shape = (slots.shape[0], slots.shape[1])
    block = (
        lax.broadcasted_iota(jnp.int32, shape, 0) * shape[1]
        + lax.broadcasted_iota(jnp.int32, shape, 1)
    ).astype(F32)
    rows = keys.shape[0]
    token = lax.broadcasted_iota(jnp.int32, (rows, HD), 0)
    position = jnp.zeros((rows, HD), F32)
    for i in range(rows // BLOCK):
        owner = jnp.sum(jnp.where(slots[...] == slot0 + i, block, 0.0))
        position = jnp.where(token // BLOCK == i, owner * BLOCK, position)
    position = position + (token % BLOCK).astype(F32)
    angle = position * freq[...]
    cosine = jnp.cos(angle)
    lane = lax.broadcasted_iota(jnp.int32, (rows, HD), 1)
    sine = jnp.sin(angle)
    sine = jnp.where(lane < HD // 2, -sine, sine)
    for kind, copy in enumerate(copies):
        copy.wait()
        for d, out in enumerate(outs):
            target = lax.rem(y + d, 4)
            for part in range(2):
                group = 2 * target + (xhi if part == 0 else 1 - xhi)
                to = pl.ds((part * 2 + kind) * rows, rows)
                for h in range(HQL):
                    at = pl.ds(pl.multiple_of(group * WIDTH + h * HD, HD), HD)
                    if kind == 0:
                        value = turn(keys[:, at].astype(F32), cosine, sine).astype(BF)
                    else:
                        value = values[:, at]
                    out[to, pl.ds(h * HD, HD)] = value


def prepare(block_slot, keys, values):
    rows = keys.shape[0]
    freq = np.tile(frequencies(), 2)[None, :].astype(np.float32)
    vmem = pl.BlockSpec(memory_space=pltpu.VMEM)
    return call(
        prep_kernel,
        "prepare",
        60,
        in_specs=[vmem] * 2
        + [pl.BlockSpec(memory_space=pltpu.HBM)] * 2,
        out_specs=[vmem] * 4,
        out_shape=[jax.ShapeDtypeStruct((4 * rows, WIDTH), BF)] * 4,
        scratch_shapes=[
            pltpu.VMEM(keys.shape, BF),
            pltpu.VMEM(values.shape, BF),
            pltpu.SemaphoreType.DMA((2,)),
        ],
    )(block_slot.reshape(4, -1), jnp.asarray(freq), keys, values)


def project_kernel(kinds, scale, fetched, hidden, cosine, sine, *refs):
    n = len(kinds)
    weights, outs, refs = refs[:n], refs[n : 2 * n], refs[2 * n :]
    rows = hidden
    if not fetched:
        rows, refs = refs[0], refs[1:]
    slabs, sems = refs[:n], refs[n]
    depth = hidden.shape[1]
    deep = depth // SLABS
    copies = []
    for i in range(SLABS):
        at = pl.ds(i * deep, deep)
        slab = [(w.at[at, :], v.at[at, :]) for w, v in zip(weights, slabs)]
        if not fetched:
            slab.append((hidden.at[:, at], rows.at[:, at]))
        copies.append(
            [
                pltpu.make_async_copy(src, dst, sems.at[i, j])
                for j, (src, dst) in enumerate(slab)
            ]
        )
        for copy in copies[-1]:
            copy.start()
    totals = [0.0] * n
    for i in range(SLABS):
        for copy in copies[i]:
            copy.wait()
        at = slice(i * deep, (i + 1) * deep)
        for j, slab in enumerate(slabs):
            totals[j] += jnp.dot(rows[:, at], slab[at, :], preferred_element_type=F32)
    for kind, out, total in zip(kinds, outs, totals):
        for h in range(HQL):
            at = slice(h * HD, (h + 1) * HD)
            value = total[:, at]
            if kind != "v":
                value = turn(value, cosine[...], sine[...])
            if kind == "q":
                value = value * scale
            out[:, at] = value.astype(BF)


def project(kinds, hidden, weights, tables, fetched):
    rows, depth = hidden.shape
    n = len(kinds)
    vmem = pl.BlockSpec(memory_space=pltpu.VMEM)
    hbm = pl.BlockSpec(memory_space=pltpu.HBM)
    more = not fetched
    return call(
        functools.partial(project_kernel, kinds, LOG2E / math.sqrt(HD), fetched),
        "project_" + kinds,
        40 if fetched else 50,
        in_specs=[vmem if fetched else hbm] + [vmem] * 2 + [hbm] * n,
        out_specs=[vmem] * (n + more),
        out_shape=[jax.ShapeDtypeStruct((rows, WIDTH), BF)] * n
        + [jax.ShapeDtypeStruct((rows, depth), BF)] * more,
        scratch_shapes=[pltpu.VMEM((depth, WIDTH), BF)] * n
        + [pltpu.SemaphoreType.DMA((SLABS, n + more))],
    )(hidden, *tables, *weights)


def pack_kernel(n, *refs):
    got, outs = refs[:n], refs[n:]
    rows = got[0].shape[0] // 4
    for part, out in enumerate(outs):
        for kind in range(2):
            for i, piece in enumerate(got):
                at = pl.ds((kind * n + i) * rows, rows)
                out[at, :] = piece[pl.ds((2 * part + kind) * rows, rows), :]


def pack(got):
    rows, width = got[0].shape
    vmem = pl.BlockSpec(memory_space=pltpu.VMEM)
    return call(
        functools.partial(pack_kernel, len(got)),
        "pack",
        in_specs=[vmem] * len(got),
        out_specs=[vmem] * 2,
        out_shape=[jax.ShapeDtypeStruct((len(got) * rows // 2, width), BF)] * 2,
    )(*got)


def widen(v):
    return jnp.concatenate([v, jnp.ones_like(v)], axis=1)


def suffix_kernel(length, q_ref, k_ref, v_ref, sum_ref, top_ref):
    tile = 128
    for t in range(SUF // tile):
        rows, keys = pl.ds(t * tile, tile), (t + 1) * tile
        row = t * tile + lax.broadcasted_iota(jnp.int32, (tile, keys), 0)
        column = lax.broadcasted_iota(jnp.int32, (tile, keys), 1)
        mask = (column <= row) & (column < length[0])
        for h in range(HQL):
            head = slice(h * HD, (h + 1) * HD)
            s = lax.dot_general(
                q_ref[rows, head],
                k_ref[:keys, head],
                (((1,), (1,)), ((), ())),
                preferred_element_type=F32,
            )
            s = jnp.where(mask, s, -1e30)
            top = jnp.max(s, axis=1, keepdims=True)
            p = jnp.exp2(s - top).astype(BF)
            sum_ref[rows, 2 * h * HD : 2 * (h + 1) * HD] = jnp.dot(
                p, widen(v_ref[:keys, head]), preferred_element_type=F32
            )
            top_ref[rows, head] = jnp.broadcast_to(top, (tile, HD))


def suffix_attention(length, q, k, v):
    vmem = pl.BlockSpec(memory_space=pltpu.VMEM)
    return call(
        suffix_kernel,
        "suffix_attention",
        flops=2 * 10**10,
        in_specs=[pl.BlockSpec(memory_space=pltpu.SMEM)] + [vmem] * 3,
        out_specs=[vmem] * 2,
        out_shape=STATE,
    )(length, q, k, v)


def split_log(log):
    high = log.astype(BF)
    rest = log - high.astype(F32)
    middle = rest.astype(BF)
    return high, middle, (rest - middle.astype(F32)).astype(BF)


def prefix_kernel(nq, nkv, used, held, last, *refs):
    qs, kvs = refs[:nq], refs[nq : nq + nkv]
    old, at = [], nq + nkv
    for has in held:
        old.append(refs[at : at + 2] if has else None)
        at += 2 * has
    outs = refs[at:]
    half = kvs[0].shape[0] // 2
    tile = 256

    def one_tile(h, r, rows):
        head = slice(h * HD, (h + 1) * HD)
        wide = slice(2 * h * HD, 2 * (h + 1) * HD)
        n = used[r]
        k = jnp.concatenate([kv[:half, head] for kv in kvs[:n]], axis=0)
        v = jnp.concatenate([kv[half:, head] for kv in kvs[:n]], axis=0)
        s = lax.dot_general(
            qs[r][rows, head],
            k,
            (((1,), (1,)), ((), ())),
            preferred_element_type=F32,
        )
        top = jnp.broadcast_to(jnp.max(s, axis=1, keepdims=True), (tile, HD))
        if old[r] is not None:
            before = old[r][1][rows, head]
            top = jnp.maximum(before, top)
        p = jnp.exp2(s - jnp.concatenate([top] * (n * half // HD), axis=1)).astype(BF)
        both = jnp.dot(p, widen(v), preferred_element_type=F32)
        if old[r] is not None:
            shrink = jnp.exp2(before - top)
            both += jnp.concatenate([shrink] * 2, axis=1) * old[r][0][rows, wide]
        if not last:
            outs[2 * r][rows, wide] = both
            outs[2 * r + 1][rows, head] = top
            return []
        acc, total = both[:, :HD], both[:, HD:]
        outs[r][rows, head] = (acc / total).astype(BF)
        log = top + jnp.log2(total)
        return [log[i : i + HD].T[:1] for i in range(0, tile, HD)]

    if not last:

        @pl.loop(0, SUF // tile)
        def _(t):
            rows = pl.ds(pl.multiple_of(t * tile, tile), tile)
            for h in range(HQL):
                for r in range(nq):
                    one_tile(h, r, rows)

        return
    for h in range(HQL):
        for r in range(nq):
            logs = []
            for t in range(SUF // tile):
                logs += one_tile(h, r, pl.ds(t * tile, tile))
            rest = jnp.zeros((EXTRA - 3 * len(logs), HD), BF)
            parts = split_log(jnp.concatenate(logs, axis=0))
            tail = jnp.concatenate([*parts, rest], axis=0)
            outs[r][SUF:, h * HD : (h + 1) * HD] = tail


STATE = [
    jax.ShapeDtypeStruct((SUF, 2 * WIDTH), F32),
    jax.ShapeDtypeStruct((SUF, WIDTH), F32),
]


def prefix_attention(name, qs, kvs, used, states, last):
    nq, nkv = len(qs), len(kvs)
    held = [state is not None for state in states]
    extra = [x for state in states if state is not None for x in state]
    vmem = pl.BlockSpec(memory_space=pltpu.VMEM)
    message = [jax.ShapeDtypeStruct((SUF + EXTRA, WIDTH), BF)]
    out = call(
        functools.partial(prefix_kernel, nq, nkv, used, held, last),
        name,
        in_specs=[vmem] * (nq + nkv + len(extra)),
        out_specs=[vmem] * (nq if last else 2 * nq),
        out_shape=(message if last else STATE) * nq,
    )(*qs, *kvs, *extra)
    return list(out) if last else [out[i : i + 2] for i in range(0, 2 * nq, 2)]


def combine(parts, length, attended):
    tile = HD
    count = SUF // tile
    row = lax.broadcasted_iota(jnp.int32, (tile, HD), 0)
    for h in range(HQL):
        at = pl.ds(h * HD, HD)
        logs = []
        for part in parts:
            tail = part[SUF:, at].astype(F32)
            logs.append(
                tail[:count] + tail[count : 2 * count] + tail[2 * count : 3 * count]
            )
        top = functools.reduce(jnp.maximum, logs)
        shares = [jnp.exp2(log - top) for log in logs]
        total = functools.reduce(lambda a, b: a + b, shares)
        shares = [share / total for share in shares]
        for t in range(count):
            rows = pl.ds(t * tile, tile)
            acc = jnp.zeros((tile, HD), F32)
            for share, part in zip(shares, parts):
                wide = jnp.broadcast_to(share[t : t + 1, :], (tile, HD)).T
                acc += wide * part[rows, at].astype(F32)
            live = t * tile + row < length[0]
            attended[rows, at] = jnp.where(live, acc, 0.0).astype(BF)


def product(rows, weight, out):
    out[...] = jnp.dot(rows[...], weight[...], preferred_element_type=F32).astype(BF)


def first_half_kernel(n, length, *refs):
    parts, (weight, theirs, ours, by_y, attended, by_x) = refs[:n], refs[n:]
    y, xhi = lax.axis_index("y"), lax.axis_index("xhi")
    few = SUF // 8

    @pl.when(pl.program_id(0) == 0)
    def _():
        combine(parts, length, attended)
        for d in range(4):
            target = lax.rem(y + d, 4)
            at = pl.ds(pl.multiple_of(target * 2 * few, 2 * few), 2 * few)
            by_y[pl.ds(d * 2 * few, 2 * few), :] = attended[at, :]
            for part in range(2):
                group = 2 * d + (1 - xhi if part == 0 else xhi)
                at = pl.ds(pl.multiple_of(group * few, few), few)
                by_x[pl.ds((part * 4 + d) * few, few), :] = attended[at, :]

    half = SUF // 2
    product(by_x.at[pl.ds(0, half)], weight, theirs)
    product(by_x.at[pl.ds(half, half)], weight, ours)


def first_half(length, parts, weight):
    n = len(parts)
    width = weight.shape[1] // 2
    wide = 1024
    half = SUF // 2
    whole = pl.BlockSpec((SUF + EXTRA, WIDTH), lambda i: (0, 0))
    return call(
        functools.partial(first_half_kernel, n),
        "first_half",
        grid=(width // wide,),
        in_specs=[pl.BlockSpec(memory_space=pltpu.SMEM)]
        + [whole] * n
        + [pl.BlockSpec((WIDTH, wide), lambda i: (0, i))],
        out_specs=[pl.BlockSpec((half, wide), lambda i: (0, i))] * 2
        + [pl.BlockSpec((SUF, WIDTH), lambda i: (0, 0))],
        out_shape=[jax.ShapeDtypeStruct((half, width), BF)] * 2
        + [jax.ShapeDtypeStruct((SUF, WIDTH), BF)],
        scratch_shapes=[pltpu.VMEM((SUF, WIDTH), BF)] * 2,
    )(length, *parts, weight)


def second_half_kernel(by_y, weight, *outs):
    rows = outs[0].shape[0]
    for d, out in enumerate(outs):
        product(by_y.at[pl.ds(d * rows, rows)], weight, out)


def second_half(by_y, weight):
    width = weight.shape[1] // 2
    wide = 1024
    skip = width // wide
    return call(
        second_half_kernel,
        "second_half",
        grid=(width // wide,),
        in_specs=[
            pl.BlockSpec((SUF, WIDTH), lambda i: (0, 0)),
            pl.BlockSpec((WIDTH, wide), lambda i: (0, i + skip)),
        ],
        out_specs=[pl.BlockSpec((SUF // 4, wide), lambda i: (0, i))] * 4,
        out_shape=[jax.ShapeDtypeStruct((SUF // 4, width), BF)] * 4,
    )(by_y, weight)


def sum_x_kernel(ours, theirs, *outs):
    y = lax.axis_index("y")
    rows = outs[0].shape[0]
    for d, out in enumerate(outs):
        at = pl.ds(pl.multiple_of(lax.rem(y + d, 4) * rows, rows), rows)
        out[...] = (ours[at, :].astype(F32) + theirs[at, :].astype(F32)).astype(BF)


def sum_x(ours, theirs):
    rows, width = ours.shape
    wide = 512
    return call(
        sum_x_kernel,
        "sum_x",
        grid=(width // wide,),
        in_specs=[pl.BlockSpec((rows, wide), lambda i: (0, i))] * 2,
        out_specs=[pl.BlockSpec((rows // 4, wide), lambda i: (0, i))] * 4,
        out_shape=[jax.ShapeDtypeStruct((rows // 4, width), BF)] * 4,
    )(ours, theirs)


def add_up(refs, at=slice(None)):
    return functools.reduce(lambda a, b: a + b, [r[at, :].astype(F32) for r in refs])


def sum_y_kernel(n, *refs):
    parts, (theirs, ours) = refs[:n], refs[n:]
    xhi = lax.axis_index("xhi")
    rows = ours.shape[0]
    for part, out in ((1 - xhi, theirs), (xhi, ours)):
        at = pl.ds(pl.multiple_of(part * rows, rows), rows)
        out[...] = add_up(parts, at).astype(BF)


def sum_y(parts):
    rows, width = parts[0].shape
    wide = 512
    return call(
        functools.partial(sum_y_kernel, len(parts)),
        "sum_y",
        grid=(width // wide,),
        in_specs=[pl.BlockSpec((rows, wide), lambda i: (0, i))] * len(parts),
        out_specs=[pl.BlockSpec((rows // 2, wide), lambda i: (0, i))] * 2,
        out_shape=[jax.ShapeDtypeStruct((rows // 2, width), BF)] * 2,
    )(*parts)


def finish_kernel(n, *refs):
    left, right, out = refs[:n], refs[n:-1], refs[-1]
    width = left[0].shape[1]
    out[:, :width] = add_up(left).astype(BF)
    out[:, width:] = add_up(right).astype(BF)


def finish(left, right):
    rows, width = left[0].shape
    vmem = pl.BlockSpec(memory_space=pltpu.VMEM)
    return call(
        functools.partial(finish_kernel, len(left)),
        "finish",
        in_specs=[vmem] * (len(left) + len(right)),
        out_specs=vmem,
        out_shape=jax.ShapeDtypeStruct((rows, 2 * width), BF),
    )(*left, *right)


def shift(n, by):
    return [(i, (i + by) % n) for i in range(n)]


def in_order(values, *others):
    return lax.optimization_barrier((*values, *others))[: len(values)]


def body(
    hidden, w_query, w_key, w_value, w_output, prefix_keys, prefix_values, block_slot, suffix_len
):
    slots, block, feats = prefix_keys.shape
    rows = slots * block
    tables = [jnp.asarray(t) for t in suffix_tables()]

    def core(x):
        return lax.ppermute(x, "core", shift(2, 1))

    def along_z(x, by):
        return lax.ppermute(x, "z", shift(4, by))

    sent = prepare(
        block_slot, prefix_keys.reshape(rows, feats), prefix_values.reshape(rows, feats)
    )
    got = [sent[0]] + [lax.ppermute(sent[d], "y", shift(4, d)) for d in (1, 2, 3)]

    (hidden,) = in_order([hidden], sent[0])
    q, hidden = project("q", hidden, [w_query], tables, False)
    q1, q3 = along_z(q, 1), along_z(q, -1)
    k_suffix, v_suffix = project("kv", hidden, [w_key, w_value], tables, True)

    got = in_order(got, k_suffix)
    near, far = pack(got)
    near_x = lax.ppermute(near, "xlo", shift(2, 1))
    far_x = lax.ppermute(far, ("xlo", "xhi"), [(0, 3), (3, 0), (1, 2), (2, 1)])
    q2 = along_z(in_order([q], near)[0], 2)
    (k_suffix,) = in_order([k_suffix], near)
    own = suffix_attention(suffix_len, q, k_suffix, v_suffix)

    q1, q3 = in_order([q1, q3], own[0])
    near_c = core(in_order([near], q1, q3)[0])
    state0, state1, state3 = prefix_attention(
        "attend_near", [q, q1, q3], [near, near_c], [2, 2, 2], [own, None, None], False
    )
    near_x, far_x = in_order([near_x, far_x], state0[0])
    far_xx = lax.ppermute(far_x, "xlo", shift(2, 1))
    states = prefix_attention(
        "attend_middle",
        [q, q1, q3, q2],
        [near_x, far_x, core(near_x), core(far_x), near, near_c],
        [4, 4, 4, 6],
        [state0, state1, state3, None],
        False,
    )
    (far_xx,) = in_order([far_xx], states[0][0])
    final = [far_xx, core(far_xx)]
    parts = []
    for state, query, back in zip(
        [states[3], states[1], states[2], states[0]], [q2, q1, q3, q], [2, -1, 1, 0]
    ):
        (part,) = prefix_attention("attend_last", [query], final, [2], [state], True)
        parts.append(along_z(part, back) if back else part)
    parts[:3] = in_order(parts[:3], parts[3])
    theirs, ours, by_y = first_half(suffix_len, parts, w_output)
    theirs = lax.ppermute(theirs, "xhi", shift(2, 1))
    cut = second_half(by_y, w_output)
    cut = [cut[0]] + [lax.ppermute(cut[d], "y", shift(4, d)) for d in (1, 2, 3)]
    left = sum_x(ours, theirs)
    left = [left[0]] + [lax.ppermute(left[d], "y", shift(4, d)) for d in (1, 2, 3)]
    theirs, ours = sum_y(cut)
    return finish(left, [ours, lax.ppermute(theirs, "xhi", shift(2, 1))])


def solution(mesh):
    fine = Mesh(
        mesh.devices.reshape(2, 4, 2, 4, 2), ("xlo", "z", "core", "y", "xhi")
    )
    pool, head = ("xlo", "z", "core"), ("y", "xhi")
    placed = (
        P(pool, None),
        P(None, head),
        P(None, head),
        P(None, head),
        P(head, None),
        P(pool + head, None, None),
        P(pool + head, None, None),
        P(),
        P(pool),
    )
    return jax.shard_map(
        body, mesh=fine, in_specs=placed, out_specs=P(pool + head, None), check_vma=False
    )
```

time: 197 us -> 153 us (0.78)
  blocking collectives: 54 us -> 0 us
  waiting for transfers between devices: 26.2 us -> 70.9 us
  Pallas kernels: 69.7 us -> 49.2 us
  local copies, waits for them, and re-layouts: 12.9 us -> 4.1 us
  other arithmetic: 3.92 us -> 0 us
    all_to_all x1 -> x0, blocking collectives: 54 us -> none  [body(): lax.all_to_all(partial.reshape(8, SUF // 8, feats), ('y', 'xhi'), split_a...]
    ppermute x10 -> x15, waiting for transfers between devices: 26.2 us -> 66.7 us  [the longest x6 23.7 us: along_z(): return lax.ppermute(x, 'z', shift(4, by))]
    pallas_call x11 -> x16, Pallas kernels: 69.7 us -> 49.2 us  [the longest x6 24.9 us: prefix_attention(): call(functools.partial(prefix_kernel, nq, nkv, used, held, last), name, i...]
    unnamed x35 -> x16, local copies, waits for them, and re-layouts: 12.9 us -> 4.1 us
    reduce_sum x1 -> x0, other arithmetic: 3.84 us -> none  [body(): return jnp.sum(shares.astype(F32), axis=0).astype(BF)]
    ppermute x4, waiting for transfers between devices: 0.01 us -> 2.93 us  [core(): return lax.ppermute(x, 'core', shift(2, 1))]
    ppermute x10 -> x15, starting transfers between devices: 20.5 us -> 20.5 us  [the longest x6 6.51 us: along_z(): return lax.ppermute(x, 'z', shift(4, by))]
  transfers between devices with their start and end apart: 19 -> 24, of which waited for: 5 -> 15; matrix products, arithmetic and copies ran while one was open for 0% -> 0% of each run, Pallas kernels for 29% -> 26%
where the time goes in v2:
time: 153 us
  waiting for transfers between devices  70.9 us (46%)
  Pallas kernels  49.2 us (32%)
  starting transfers between devices  27.8 us (18%)
  local copies, waits for them, and re-layouts  4.1 us (3%)
    pallas_call x6, Pallas kernels, prefix_attention(): call(functools.partial(prefix_kernel, nq, nkv, used, held, last), name, i...  24.9 us
    ppermute x6, waiting for transfers between devices, along_z(): return lax.ppermute(x, 'z', shift(4, by))  23.7 us
    ppermute x3, waiting for transfers between devices, body(): cut = [cut[0]] + [lax.ppermute(cut[d], 'y', shift(4, d)) for d in (1, 2, 3)]  23.2 us
    pallas_call x2, Pallas kernels, project(): call(functools.partial(project_kernel, kinds, LOG2E / math.sqrt(HD), fetc...  11.8 us
    ppermute x3, waiting for transfers between devices, body(): lax.ppermute(left[d], 'y', shift(4, d))  10.3 us
    ppermute x1, waiting for transfers between devices, body(): far_x = lax.ppermute(far, ('xlo', 'xhi'), [(0, 3), (3, 0), (1, 2), (2, 1)])  8.32 us
    ppermute x6, starting transfers between devices, along_z(): return lax.ppermute(x, 'z', shift(4, by))  6.51 us
    ppermute x3, starting transfers between devices, body(): lax.ppermute(sent[d], 'y', shift(4, d))  5.98 us
  transfers between devices with their start and end apart: 24, of which 15 were waited for; matrix products, arithmetic and copies ran while one was open for 0% of the time, Pallas kernels for 26%

profile of v2, /device:TPU:0, one launch (start us, length us, event | category | flops | bytes accessed | tf_op | source)
XLA Modules:
  0.0 152.7 jit_solution(8300000153189393123)
XLA Ops:
  0.0 3.2 %prepare.1 = (bf16[256,512]{1,0:T(8,128)(2,1)}, bf16[256,512]{1,0:T(8,128)(2,1)}, bf16[256,512]{1,0:T(8,128)(2,1)}, bf16[256,512]{1,0:T(8,128)(2,1)}) custom-call(s32[4,128]{1,0:T(4,128)} %bitcast.5, f32[1,128]{1,0:T(1,128)} %constant.8.clone.freq, bf16[64,4096]{1,0:T(8,128)(2,1)} %bitcast.3, bf16[64,4096]{1,0:T(8,128)(2,1)} %bitcast.4), custom_call_target="tpu_custom_call" | custom-call | flops 1 | bytes 1 | tf_op jit(solution)/shard_map/prepare/pallas_call | solution.py:101
  3.2 1.7 %collective-permute-start = (bf16[256,512]{1,0:T(8,128)(2,1)}, bf16[256,512]{1,0:T(8,128)(2,1)S(1)}, u32[]{:S(2)}, u32[]{:S(2)}) collective-permute-start(bf16[256,512]{1,0:T(8,128)(2,1)} %get-tuple-element.63), channel_id=1, source_target_pairs={{0,2},{2,4},{4,6},{6,0},{1,3},{3,5},{5,7},{7,1},{8,10},{10,12},{12... | collective-permute-start | bytes 786440 | tf_op jit(solution)/shard_map/ppermute | solution.py:515
  4.9 2.9 %collective-permute-start.1 = (bf16[256,512]{1,0:T(8,128)(2,1)}, bf16[256,512]{1,0:T(8,128)(2,1)S(1)}, u32[]{:S(2)}, u32[]{:S(2)}) collective-permute-start(bf16[256,512]{1,0:T(8,128)(2,1)} %get-tuple-element.64), channel_id=1, source_target_pairs={{0,4},{2,6},{4,0},{6,2},{1,5},{3,7},{5,1},{7,3},{8,12},{10,14},{12... | collective-permute-start | bytes 786440 | tf_op jit(solution)/shard_map/ppermute | solution.py:515
  7.8 1.3 collective-permute-start.2
  9.2 0.9 copy-done.4
  10.1 0.9 copy-done.6
  11.1 6.2 %project_q.1 = (bf16[512,512]{1,0:T(8,128)(2,1)S(1)}, bf16[512,4096]{1,0:T(8,128)(2,1)}) custom-call(bf16[512,4096]{1,0:T(8,128)(2,1)} %hidden, f32[512,128]{1,0:T(8,128)S(1)} %copy-done.6, f32[512,128]{1,0:T(8,128)S(1)} %copy-done.4, bf16[4096,512]{1,0:T(8,128)(2,1)} %refs_0_.2), custom_call_target="tpu_custom_call" | custom-call | flops 1 | bytes 1 | tf_op jit(solution)/shard_map/project_q/pallas_call | solution.py:164
  17.2 4.1 %collective-permute-start.7 = (bf16[512,512]{1,0:T(8,128)(2,1)S(1)}, bf16[512,512]{1,0:T(8,128)(2,1)S(1)}, u32[]{:S(2)}, u32[]{:S(2)}) collective-permute-start(bf16[512,512]{1,0:T(8,128)(2,1)S(1)} %get-tuple-element.73.q_ref.refs_0_), channel_id=1, source_target_pairs={{0,48},{16,0},{32,16},{48,32},{1,49},{17,1},{33,17},{49,33},{2,50}... | collective-permute-start | bytes 1572872 | tf_op jit(solution)/shard_map/ppermute | solution.py:510
  21.4 2.2 %copy-done.3 = bf16[512,4096]{1,0:T(8,128)(2,1)S(1)} copy-done((bf16[512,4096]{1,0:T(8,128)(2,1)S(1)}, bf16[512,4096]{1,0:T(8,128)(2,1)}, u32[]{:S(2)}) %copy-start.3) | copy-done | bytes 4194328
  23.6 5.6 %project_kv.1 = (bf16[512,512]{1,0:T(8,128)(2,1)S(1)}, bf16[512,512]{1,0:T(8,128)(2,1)S(1)}) custom-call(bf16[512,4096]{1,0:T(8,128)(2,1)S(1)} %copy-done.3, f32[512,128]{1,0:T(8,128)S(1)} %copy-done.6, f32[512,128]{1,0:T(8,128)S(1)} %copy-done.5, bf16[4096,512]{1,0:T(8,128)(2,1)S(1)} %copy-done.1, bf16[4096,512]{1,0:T(8,128)(2,1)S(1)} %copy-done.2), custom_call_target="tpu_custom_call" | custom-call | flops 1 | bytes 1 | tf_op jit(solution)/shard_map/project_kv/pallas_call | solution.py:164
  30.0 2.2 %suffix_attention.1 = (f32[512,1024]{1,0:T(8,128)S(1)}, f32[512,512]{1,0:T(8,128)S(1)}) custom-call(s32[1]{0:T(128)S(6)} %copy.13.length, bf16[512,512]{1,0:T(8,128)(2,1)S(1)} %get-tuple-element.73.q_ref.refs_0_, bf16[512,512]{1,0:T(8,128)(2,1)S(1)} %get-tuple-element.75.k_ref, bf16[512,512]{1,0:T(8,128)(2,1)S(1)} %get-tuple-element.76.v_ref), custom_call_target="tpu_custom_call" | custom-call | flops 20000000000 | bytes 1 | tf_op jit(solution)/shard_map/suffix_attention/pallas_call | solution.py:229
  32.2 2.9 %collective-permute-done.6.refs_1_.refs_0_ = bf16[512,512]{1,0:T(8,128)(2,1)S(1)} collective-permute-done((bf16[512,512]{1,0:T(8,128)(2,1)S(1)}, bf16[512,512]{1,0:T(8,128)(2,1)S(1)}, u32[]{:S(2)}, u32[]{:S(2)}) %collective-permute-start.6) | collective-permute-done | bytes 524320 | tf_op jit(solution)/shard_map/ppermute | solution.py:510
  35.1 2.8 %collective-permute-start.5 = (bf16[512,512]{1,0:T(8,128)(2,1)S(1)}, bf16[512,512]{1,0:T(8,128)(2,1)S(1)}, u32[]{:S(2)}, u32[]{:S(2)}) collective-permute-start(bf16[512,512]{1,0:T(8,128)(2,1)S(1)} %get-tuple-element.74), channel_id=1, source_target_pairs={{0,65},{65,0},{1,64},{64,1},{2,67},{67,2},{3,66},{66,3},{4,69},{69... | collective-permute-start | bytes 1572872 | tf_op jit(solution)/shard_map/ppermute | solution.py:525
  38.1 4.2 %attend_near.1 = (f32[512,1024]{1,0:T(8,128)S(1)}, f32[512,512]{1,0:T(8,128)S(1)}, f32[512,1024]{1,0:T(8,128)S(1)}, f32[512,512]{1,0:T(8,128)S(1)}, f32[512,1024]{1,0:T(8,128)S(1)}, /*index=5*/f32[512,512]{1,0:T(8,128)S(1)}) custom-call(bf16[512,512]{1,0:T(8,128)(2,1)S(1)} %get-tuple-element.73.q_ref.refs_0_, ...), custom_call_target="tpu_custom_call" | custom-call | flops 1 | bytes 1 | tf_op jit(solution)/shard_map/attend_near/pallas_call | solution.py:319
  42.3 8.3 %collective-permute-done.5.refs_5_ = bf16[512,512]{1,0:T(8,128)(2,1)S(1)} collective-permute-done((bf16[512,512]{1,0:T(8,128)(2,1)S(1)}, bf16[512,512]{1,0:T(8,128)(2,1)S(1)}, u32[]{:S(2)}, u32[]{:S(2)}) %collective-permute-start.5) | collective-permute-done | bytes 524320 | tf_op jit(solution)/shard_map/ppermute | solution.py:525
  50.7 1.3 collective-permute-done.4.refs_4_
  51.9 0.5 collective-permute-start.11
  52.7 0.7 collective-permute-done.3.refs_3_.refs_0_
  53.4 0.4 collective-permute-done.10.refs_6_
  53.8 0.7 collective-permute-done.11.refs_7_
  54.6 14.1 %attend_middle.1 = (f32[512,1024]{1,0:T(8,128)S(1)}, f32[512,512]{1,0:T(8,128)S(1)}, f32[512,1024]{1,0:T(8,128)S(1)}, f32[512,512]{1,0:T(8,128)S(1)}, f32[512,10...) custom-call(bf16[512,512]{1,0:T(8,128)(2,1)S(1)} %get-tuple-element.73.q_ref.refs_0_, ...), custom_call_target="tpu_custom_call" | custom-call | flops 1 | bytes 1 | tf_op jit(solution)/shard_map/attend_middle/pallas_call | solution.py:319
  68.9 1.8 %collective-permute-done.12.refs_2_ = bf16[512,512]{1,0:T(8,128)(2,1)S(1)} collective-permute-done((bf16[512,512]{1,0:T(8,128)(2,1)S(1)}, bf16[512,512]{1,0:T(8,128)(2,1)S(1)}, u32[]{:S(2)}, u32[]{:S(2)}) %collective-permute-start.12) | collective-permute-done | bytes 524320 | tf_op jit(solution)/shard_map/ppermute | solution.py:507
  70.7 1.7 %attend_last.4 = bf16[528,512]{1,0:T(8,128)(2,1)S(1)} custom-call(bf16[512,512]{1,0:T(8,128)(2,1)S(1)} %collective-permute-done.3.refs_3_.refs_0_, bf16[512,512]{1,0:T(8,128)(2,1)S(1)} %collective-permute-done.9.refs_1_, bf16[512,512]{1,0:T(8,128)(2,1)S(1)} %collective-permute-done.12.refs_2_, f32[512,1024]{1,0:T(8,128)S(1)} %get-tuple-element.92.refs_3_, ...), custom_call_target="tpu_custom_call" | custom-call | flops 1 | bytes 1 | tf_op jit(solution)/shard_map/attend_last/pallas_call | solution.py:319
  72.4 1.7 %attend_last.5 = bf16[528,512]{1,0:T(8,128)(2,1)S(1)} custom-call(bf16[512,512]{1,0:T(8,128)(2,1)S(1)} %collective-permute-done.6.refs_1_.refs_0_, bf16[512,512]{1,0:T(8,128)(2,1)S(1)} %collective-permute-done.9.refs_1_, bf16[512,512]{1,0:T(8,128)(2,1)S(1)} %collective-permute-done.12.refs_2_, f32[512,1024]{1,0:T(8,128)S(1)} %get-tuple-element.94.refs_3_, ...), custom_call_target="tpu_custom_call" | custom-call | flops 1 | bytes 1 | tf_op jit(solution)/shard_map/attend_last/pallas_call | solution.py:319
  74.1 2.0 %collective-permute-start.14 = (bf16[528,512]{1,0:T(8,128)(2,1)S(1)}, bf16[528,512]{1,0:T(8,128)(2,1)S(1)}, u32[]{:S(2)}, u32[]{:S(2)}) collective-permute-start(bf16[528,512]{1,0:T(8,128)(2,1)S(1)} %attend_last.5), channel_id=1, source_target_pairs={{0,48},{16,0},{32,16},{48,32},{1,49},{17,1},{33,17},{49,33},{2,50}... | collective-permute-start | bytes 1622024 | tf_op jit(solution)/shard_map/ppermute | solution.py:510
  76.1 1.6 %attend_last.6 = bf16[528,512]{1,0:T(8,128)(2,1)S(1)} custom-call(bf16[512,512]{1,0:T(8,128)(2,1)S(1)} %collective-permute-done.7.refs_2_.refs_0_, bf16[512,512]{1,0:T(8,128)(2,1)S(1)} %collective-permute-done.9.refs_1_, bf16[512,512]{1,0:T(8,128)(2,1)S(1)} %collective-permute-done.12.refs_2_, f32[512,1024]{1,0:T(8,128)S(1)} %get-tuple-element.96.refs_3_, ...), custom_call_target="tpu_custom_call" | custom-call | flops 1 | bytes 1 | tf_op jit(solution)/shard_map/attend_last/pallas_call | solution.py:319
  77.7 0.3 collective-permute-start.15
  78.1 1.6 %attend_last.7.refs_3_ = bf16[528,512]{1,0:T(8,128)(2,1)S(1)} custom-call(bf16[512,512]{1,0:T(8,128)(2,1)S(1)} %get-tuple-element.73.q_ref.refs_0_, bf16[512,512]{1,0:T(8,128)(2,1)S(1)} %collective-permute-done.9.refs_1_, bf16[512,512]{1,0:T(8,128)(2,1)S(1)} %collective-permute-done.12.refs_2_, f32[512,1024]{1,0:T(8,128)S(1)} %get-tuple-element.90.refs_3_, ...), custom_call_target="tpu_custom_call" | custom-call | flops 1 | bytes 1 | tf_op jit(solution)/shard_map/attend_last/pallas_call | solution.py:319
  79.7 9.4 %collective-permute-done.13.refs_0_ = bf16[528,512]{1,0:T(8,128)(2,1)S(1)} collective-permute-done((bf16[528,512]{1,0:T(8,128)(2,1)S(1)}, bf16[528,512]{1,0:T(8,128)(2,1)S(1)}, u32[]{:S(2)}, u32[]{:S(2)}) %collective-permute-start.13) | collective-permute-done | bytes 540704 | tf_op jit(solution)/shard_map/ppermute | solution.py:510
  89.1 8.5 %collective-permute-done.14.refs_1_ = bf16[528,512]{1,0:T(8,128)(2,1)S(1)} collective-permute-done((bf16[528,512]{1,0:T(8,128)(2,1)S(1)}, bf16[528,512]{1,0:T(8,128)(2,1)S(1)}, u32[]{:S(2)}, u32[]{:S(2)}) %collective-permute-start.14) | collective-permute-done | bytes 540704 | tf_op jit(solution)/shard_map/ppermute | solution.py:510
  97.6 2.2 %collective-permute-done.15.refs_2_ = bf16[528,512]{1,0:T(8,128)(2,1)S(1)} collective-permute-done((bf16[528,512]{1,0:T(8,128)(2,1)S(1)}, bf16[528,512]{1,0:T(8,128)(2,1)S(1)}, u32[]{:S(2)}, u32[]{:S(2)}) %collective-permute-start.15) | collective-permute-done | bytes 540704 | tf_op jit(solution)/shard_map/ppermute | solution.py:510
  99.8 3.1 %first_half.1 = (bf16[256,2048]{1,0:T(8,128)(2,1)S(1)}, bf16[256,2048]{1,0:T(8,128)(2,1)S(1)}, bf16[512,512]{1,0:T(8,128)(2,1)S(1)}) custom-call(s32[1]{0:T(128)S(6)} %copy.13.length, bf16[528,512]{1,0:T(8,128)(2,1)S(1)} %collective-permute-done.13.refs_0_, bf16[528,512]{1,0:T(8,128)(2,1)S(1)} %collective-permute-done.14.refs_1_, ...), custom_call_target="tpu_custom_call" | custom-call | flops 1 | bytes 1 | tf_op jit(solution)/shard_map/first_half/pallas_call | solution.py:387
  102.9 0.9 collective-permute-start.16
  103.8 1.7 %second_half.1 = (bf16[128,2048]{1,0:T(8,128)(2,1)S(1)}, bf16[128,2048]{1,0:T(8,128)(2,1)S(1)}, bf16[128,2048]{1,0:T(8,128)(2,1)S(1)}, bf16[128,2048]{1,0:T(8,128)(2,1)S(1)}) custom-call(bf16[512,512]{1,0:T(8,128)(2,1)S(1)} %get-tuple-element.108.by_y, bf16[512,4096]{1,0:T(8,128)(2,1)S(1)} %copy-done), custom_call_target="tpu_custom_call" | custom-call | flops 1 | bytes 1 | tf_op jit(solution)/shard_map/second_half/pallas_call | solution.py:412
  105.6 0.7 collective-permute-start.20
  106.3 1.1 collective-permute-start.21
  107.4 1.7 %collective-permute-start.22 = (bf16[128,2048]{1,0:T(8,128)(2,1)S(1)}, bf16[128,2048]{1,0:T(8,128)(2,1)S(1)}, u32[]{:S(2)}, u32[]{:S(2)}) collective-permute-start(bf16[128,2048]{1,0:T(8,128)(2,1)S(1)} %get-tuple-element.112), channel_id=1, source_target_pairs={{0,6},{2,0},{4,2},{6,4},{1,7},{3,1},{5,3},{7,5},{8,14},{10,8},{12,... | collective-permute-start | bytes 1572872 | tf_op jit(solution)/shard_map/ppermute | solution.py:557
  109.1 22.6 %collective-permute-done.20.refs_1_ = bf16[128,2048]{1,0:T(8,128)(2,1)S(1)} collective-permute-done((bf16[128,2048]{1,0:T(8,128)(2,1)S(1)}, bf16[128,2048]{1,0:T(8,128)(2,1)S(1)}, u32[]{:S(2)}, u32[]{:S(2)}) %collective-permute-start.20) | collective-permute-done | bytes 524320 | tf_op jit(solution)/shard_map/ppermute | solution.py:557
  131.7 0.6 collective-permute-done.22.refs_3_
  132.3 0.6 sum_y.1
  132.9 2.8 %collective-permute-start.23 = (bf16[64,2048]{1,0:T(8,128)(2,1)S(1)}, bf16[64,2048]{1,0:T(8,128)(2,1)S(1)}, u32[]{:S(2)}, u32[]{:S(2)}) collective-permute-start(bf16[64,2048]{1,0:T(8,128)(2,1)S(1)} %get-tuple-element.114), channel_id=1, source_target_pairs={{0,1},{1,0},{2,3},{3,2},{4,5},{5,4},{6,7},{7,6},{8,9},{9,8},{10,11... | collective-permute-start | bytes 786440 | tf_op jit(solution)/shard_map/ppermute | solution.py:561
  135.7 0.6 sum_x.1
  136.3 0.5 collective-permute-start.17
  136.8 3.6 %collective-permute-start.18 = (bf16[64,2048]{1,0:T(8,128)(2,1)S(1)}, bf16[64,2048]{1,0:T(8,128)(2,1)S(1)}, u32[]{:S(2)}, u32[]{:S(2)}) collective-permute-start(bf16[64,2048]{1,0:T(8,128)(2,1)S(1)} %get-tuple-element.106), channel_id=1, source_target_pairs={{0,4},{2,6},{4,0},{6,2},{1,5},{3,7},{5,1},{7,3},{8,12},{10,14},{12... | collective-permute-start | bytes 786440 | tf_op jit(solution)/shard_map/ppermute | solution.py:559
  140.3 1.2 collective-permute-done.23.refs_5_
  141.5 3.7 %collective-permute-done.17.refs_1_ = bf16[64,2048]{1,0:T(8,128)(2,1)S(1)} collective-permute-done((bf16[64,2048]{1,0:T(8,128)(2,1)S(1)}, bf16[64,2048]{1,0:T(8,128)(2,1)S(1)}, u32[]{:S(2)}, u32[]{:S(2)}) %collective-permute-start.17) | collective-permute-done | bytes 262176 | tf_op jit(solution)/shard_map/ppermute | solution.py:559
  145.2 6.6 %collective-permute-done.18.refs_2_ = bf16[64,2048]{1,0:T(8,128)(2,1)S(1)} collective-permute-done((bf16[64,2048]{1,0:T(8,128)(2,1)S(1)}, bf16[64,2048]{1,0:T(8,128)(2,1)S(1)}, u32[]{:S(2)}, u32[]{:S(2)}) %collective-permute-start.18) | collective-permute-done | bytes 262176 | tf_op jit(solution)/shard_map/ppermute | solution.py:559
  151.8 1.0 finish.1
  (32 shorter events, 0.9 us)
Async XLA Ops:
  3.2 26.7 %collective-permute-start = (bf16[256,512]{1,0:T(8,128)(2,1)}, bf16[256,512]{1,0:T(8,128)(2,1)S(1)}, u32[]{:S(2)}, u32[]{:S(2)}) collective-permute-start(bf16[256,512]{1,0:T(8,128)(2,1)} %get-tuple-element.63), channel_id=1, source_target_pairs={{0,2},{2,4},{4,6},{6,0},{1,3},{3,5},{5,7},{7,1},{8,10},{10,12},{12... | collective-permute-start | bytes 786440 | tf_op jit(solution)/shard_map/ppermute | solution.py:515
  4.9 25.0 %collective-permute-start.1 = (bf16[256,512]{1,0:T(8,128)(2,1)}, bf16[256,512]{1,0:T(8,128)(2,1)S(1)}, u32[]{:S(2)}, u32[]{:S(2)}) collective-permute-start(bf16[256,512]{1,0:T(8,128)(2,1)} %get-tuple-element.64), channel_id=1, source_target_pairs={{0,4},{2,6},{4,0},{6,2},{1,5},{3,7},{5,1},{7,3},{8,12},{10,14},{12... | collective-permute-start | bytes 786440 | tf_op jit(solution)/shard_map/ppermute | solution.py:515
  7.8 22.1 %collective-permute-start.2 = (bf16[256,512]{1,0:T(8,128)(2,1)}, bf16[256,512]{1,0:T(8,128)(2,1)S(1)}, u32[]{:S(2)}, u32[]{:S(2)}) collective-permute-start(bf16[256,512]{1,0:T(8,128)(2,1)} %get-tuple-element.65), channel_id=1, source_target_pairs={{0,6},{2,0},{4,2},{6,4},{1,7},{3,1},{5,3},{7,5},{8,14},{10,8},{12,... | collective-permute-start | bytes 786440 | tf_op jit(solution)/shard_map/ppermute | solution.py:515
  9.2 0.9 copy-start.4
  10.1 0.9 copy-start.6
  11.1 10.3 %copy-start.1 = (bf16[4096,512]{1,0:T(8,128)(2,1)S(1)}, bf16[4096,512]{1,0:T(8,128)(2,1)}, u32[]{:S(2)}) copy-start(bf16[4096,512]{1,0:T(8,128)(2,1)} %refs_0_.3) | copy-start | bytes 12582916
  11.1 10.3 %copy-start.2 = (bf16[4096,512]{1,0:T(8,128)(2,1)S(1)}, bf16[4096,512]{1,0:T(8,128)(2,1)}, u32[]{:S(2)}) copy-start(bf16[4096,512]{1,0:T(8,128)(2,1)} %refs_1_.1) | copy-start | bytes 12582916
  11.1 10.3 %copy-start.5 = (f32[512,128]{1,0:T(8,128)S(1)}, f32[512,128]{1,0:T(8,128)}, u32[]{:S(2)}) copy-start(f32[512,128]{1,0:T(8,128)} %constant.7.clone.sine) | copy-start | bytes 786436
  17.2 14.9 %collective-permute-start.7 = (bf16[512,512]{1,0:T(8,128)(2,1)S(1)}, bf16[512,512]{1,0:T(8,128)(2,1)S(1)}, u32[]{:S(2)}, u32[]{:S(2)}) collective-permute-start(bf16[512,512]{1,0:T(8,128)(2,1)S(1)} %get-tuple-element.73.q_ref.refs_0_), channel_id=1, source_target_pairs={{0,48},{16,0},{32,16},{48,32},{1,49},{17,1},{33,17},{49,33},{2,50}... | collective-permute-start | bytes 1572872 | tf_op jit(solution)/shard_map/ppermute | solution.py:510
  21.4 13.8 %collective-permute-start.6 = (bf16[512,512]{1,0:T(8,128)(2,1)S(1)}, bf16[512,512]{1,0:T(8,128)(2,1)S(1)}, u32[]{:S(2)}, u32[]{:S(2)}) collective-permute-start(bf16[512,512]{1,0:T(8,128)(2,1)S(1)} %get-tuple-element.73.q_ref.refs_0_), channel_id=1, source_target_pairs={{0,16},{16,32},{32,48},{48,0},{1,17},{17,33},{33,49},{49,1},{2,18}... | collective-permute-start | bytes 1572872 | tf_op jit(solution)/shard_map/ppermute | solution.py:510
  21.4 2.2 %copy-start.3 = (bf16[512,4096]{1,0:T(8,128)(2,1)S(1)}, bf16[512,4096]{1,0:T(8,128)(2,1)}, u32[]{:S(2)}) copy-start(bf16[512,4096]{1,0:T(8,128)(2,1)} %get-tuple-element.66.hidden) | copy-start | bytes 12582916
  23.6 6.3 %copy-start.7 = (bf16[256,512]{1,0:T(8,128)(2,1)S(1)}, bf16[256,512]{1,0:T(8,128)(2,1)}, u32[]{:S(2)}) copy-start(bf16[256,512]{1,0:T(8,128)(2,1)} %get-tuple-element.68.refs_0_) | copy-start | bytes 786436
  35.1 3.0 %collective-permute-start.8 = (bf16[512,512]{1,0:T(8,128)(2,1)S(1)}, bf16[512,512]{1,0:T(8,128)(2,1)S(1)}, u32[]{:S(2)}, u32[]{:S(2)}) collective-permute-start(bf16[512,512]{1,0:T(8,128)(2,1)S(1)} %get-tuple-element.80.refs_3_.refs_8_), channel_id=1, source_target_pairs={{0,8},{8,0},{1,9},{9,1},{2,10},{10,2},{3,11},{11,3},{4,12},{12,4},... | collective-permute-start | bytes 1572872 | tf_op jit(solution)/shard_map/ppermute | solution.py:507
  35.1 15.5 %collective-permute-start.5 = (bf16[512,512]{1,0:T(8,128)(2,1)S(1)}, bf16[512,512]{1,0:T(8,128)(2,1)S(1)}, u32[]{:S(2)}, u32[]{:S(2)}) collective-permute-start(bf16[512,512]{1,0:T(8,128)(2,1)S(1)} %get-tuple-element.74), channel_id=1, source_target_pairs={{0,65},{65,0},{1,64},{64,1},{2,67},{67,2},{3,66},{66,3},{4,69},{69... | collective-permute-start | bytes 1572872 | tf_op jit(solution)/shard_map/ppermute | solution.py:525
  37.9 14.1 %collective-permute-start.4 = (bf16[512,512]{1,0:T(8,128)(2,1)S(1)}, bf16[512,512]{1,0:T(8,128)(2,1)S(1)}, u32[]{:S(2)}, u32[]{:S(2)}) collective-permute-start(bf16[512,512]{1,0:T(8,128)(2,1)S(1)} %get-tuple-element.80.refs_3_.refs_8_), channel_id=1, source_target_pairs={{0,64},{64,0},{1,65},{65,1},{2,66},{66,2},{3,67},{67,3},{4,68},{68... | collective-permute-start | bytes 1572872 | tf_op jit(solution)/shard_map/ppermute | solution.py:524
  38.1 15.3 %collective-permute-start.3 = (bf16[512,512]{1,0:T(8,128)(2,1)S(1)}, bf16[512,512]{1,0:T(8,128)(2,1)S(1)}, u32[]{:S(2)}, u32[]{:S(2)}) collective-permute-start(bf16[512,512]{1,0:T(8,128)(2,1)S(1)} %get-tuple-element.73.q_ref.refs_0_), channel_id=1, source_target_pairs={{0,32},{16,48},{32,0},{48,16},{1,33},{17,49},{33,1},{49,17},{2,34}... | collective-permute-start | bytes 1572872 | tf_op jit(solution)/shard_map/ppermute | solution.py:510
  51.9 1.9 %collective-permute-start.10 = (bf16[512,512]{1,0:T(8,128)(2,1)S(1)}, bf16[512,512]{1,0:T(8,128)(2,1)S(1)}, u32[]{:S(2)}, u32[]{:S(2)}) collective-permute-start(bf16[512,512]{1,0:T(8,128)(2,1)S(1)} %collective-permute-done.4.refs_4_), channel_id=1, source_target_pairs={{0,8},{8,0},{1,9},{9,1},{2,10},{10,2},{3,11},{11,3},{4,12},{12,4},... | collective-permute-start | bytes 1572872 | tf_op jit(solution)/shard_map/ppermute | solution.py:507
  51.9 2.7 %collective-permute-start.11 = (bf16[512,512]{1,0:T(8,128)(2,1)S(1)}, bf16[512,512]{1,0:T(8,128)(2,1)S(1)}, u32[]{:S(2)}, u32[]{:S(2)}) collective-permute-start(bf16[512,512]{1,0:T(8,128)(2,1)S(1)} %collective-permute-done.5.refs_5_), channel_id=1, source_target_pairs={{0,8},{8,0},{1,9},{9,1},{2,10},{10,2},{3,11},{11,3},{4,12},{12,4},... | collective-permute-start | bytes 1572872 | tf_op jit(solution)/shard_map/ppermute | solution.py:507
  52.4 16.3 %collective-permute-start.9 = (bf16[512,512]{1,0:T(8,128)(2,1)S(1)}, bf16[512,512]{1,0:T(8,128)(2,1)S(1)}, u32[]{:S(2)}, u32[]{:S(2)}) collective-permute-start(bf16[512,512]{1,0:T(8,128)(2,1)S(1)} %collective-permute-done.5.refs_5_), channel_id=1, source_target_pairs={{0,64},{64,0},{1,65},{65,1},{2,66},{66,2},{3,67},{67,3},{4,68},{68... | collective-permute-start | bytes 1572872 | tf_op jit(solution)/shard_map/ppermute | solution.py:536
  68.7 2.0 %collective-permute-start.12 = (bf16[512,512]{1,0:T(8,128)(2,1)S(1)}, bf16[512,512]{1,0:T(8,128)(2,1)S(1)}, u32[]{:S(2)}, u32[]{:S(2)}) collective-permute-start(bf16[512,512]{1,0:T(8,128)(2,1)S(1)} %collective-permute-done.9.refs_1_), channel_id=1, source_target_pairs={{0,8},{8,0},{1,9},{9,1},{2,10},{10,2},{3,11},{11,3},{4,12},{12,4},... | collective-permute-start | bytes 1572872 | tf_op jit(solution)/shard_map/ppermute | solution.py:507
  72.4 16.7 %collective-permute-start.13 = (bf16[528,512]{1,0:T(8,128)(2,1)S(1)}, bf16[528,512]{1,0:T(8,128)(2,1)S(1)}, u32[]{:S(2)}, u32[]{:S(2)}) collective-permute-start(bf16[528,512]{1,0:T(8,128)(2,1)S(1)} %attend_last.4), channel_id=1, source_target_pairs={{0,32},{16,48},{32,0},{48,16},{1,33},{17,49},{33,1},{49,17},{2,34}... | collective-permute-start | bytes 1622024 | tf_op jit(solution)/shard_map/ppermute | solution.py:510
  74.1 23.5 %collective-permute-start.14 = (bf16[528,512]{1,0:T(8,128)(2,1)S(1)}, bf16[528,512]{1,0:T(8,128)(2,1)S(1)}, u32[]{:S(2)}, u32[]{:S(2)}) collective-permute-start(bf16[528,512]{1,0:T(8,128)(2,1)S(1)} %attend_last.5), channel_id=1, source_target_pairs={{0,48},{16,0},{32,16},{48,32},{1,49},{17,1},{33,17},{49,33},{2,50}... | collective-permute-start | bytes 1622024 | tf_op jit(solution)/shard_map/ppermute | solution.py:510
  77.7 22.1 %collective-permute-start.15 = (bf16[528,512]{1,0:T(8,128)(2,1)S(1)}, bf16[528,512]{1,0:T(8,128)(2,1)S(1)}, u32[]{:S(2)}, u32[]{:S(2)}) collective-permute-start(bf16[528,512]{1,0:T(8,128)(2,1)S(1)} %attend_last.6), channel_id=1, source_target_pairs={{0,16},{16,32},{32,48},{48,0},{1,17},{17,33},{33,49},{49,1},{2,18}... | collective-permute-start | bytes 1622024 | tf_op jit(solution)/shard_map/ppermute | solution.py:510
  78.1 21.8 %copy-start = (bf16[512,4096]{1,0:T(8,128)(2,1)S(1)}, bf16[512,4096]{1,0:T(8,128)(2,1)}, u32[]{:S(2)}) copy-start(bf16[512,4096]{1,0:T(8,128)(2,1)} %weight.1) | copy-start | bytes 12582916
  102.9 32.7 %collective-permute-start.16 = (bf16[256,2048]{1,0:T(8,128)(2,1)S(1)}, bf16[256,2048]{1,0:T(8,128)(2,1)S(1)}, u32[]{:S(2)}, u32[]{:S(2)}) collective-permute-start(bf16[256,2048]{1,0:T(8,128)(2,1)S(1)} %get-tuple-element.103), channel_id=1, source_target_pairs={{0,1},{1,0},{2,3},{3,2},{4,5},{5,4},{6,7},{7,6},{8,9},{9,8},{10,11... | collective-permute-start | bytes 3145736 | tf_op jit(solution)/shard_map/ppermute | solution.py:555
  105.6 26.1 %collective-permute-start.20 = (bf16[128,2048]{1,0:T(8,128)(2,1)S(1)}, bf16[128,2048]{1,0:T(8,128)(2,1)S(1)}, u32[]{:S(2)}, u32[]{:S(2)}) collective-permute-start(bf16[128,2048]{1,0:T(8,128)(2,1)S(1)} %get-tuple-element.110), channel_id=1, source_target_pairs={{0,2},{2,4},{4,6},{6,0},{1,3},{3,5},{5,7},{7,1},{8,10},{10,12},{12... | collective-permute-start | bytes 1572872 | tf_op jit(solution)/shard_map/ppermute | solution.py:557
  106.3 25.3 %collective-permute-start.21 = (bf16[128,2048]{1,0:T(8,128)(2,1)S(1)}, bf16[128,2048]{1,0:T(8,128)(2,1)S(1)}, u32[]{:S(2)}, u32[]{:S(2)}) collective-permute-start(bf16[128,2048]{1,0:T(8,128)(2,1)S(1)} %get-tuple-element.111), channel_id=1, source_target_pairs={{0,4},{2,6},{4,0},{6,2},{1,5},{3,7},{5,1},{7,3},{8,12},{10,14},{12... | collective-permute-start | bytes 1572872 | tf_op jit(solution)/shard_map/ppermute | solution.py:557
  107.4 24.9 %collective-permute-start.22 = (bf16[128,2048]{1,0:T(8,128)(2,1)S(1)}, bf16[128,2048]{1,0:T(8,128)(2,1)S(1)}, u32[]{:S(2)}, u32[]{:S(2)}) collective-permute-start(bf16[128,2048]{1,0:T(8,128)(2,1)S(1)} %get-tuple-element.112), channel_id=1, source_target_pairs={{0,6},{2,0},{4,2},{6,4},{1,7},{3,1},{5,3},{7,5},{8,14},{10,8},{12,... | collective-permute-start | bytes 1572872 | tf_op jit(solution)/shard_map/ppermute | solution.py:557
  132.9 8.6 %collective-permute-start.23 = (bf16[64,2048]{1,0:T(8,128)(2,1)S(1)}, bf16[64,2048]{1,0:T(8,128)(2,1)S(1)}, u32[]{:S(2)}, u32[]{:S(2)}) collective-permute-start(bf16[64,2048]{1,0:T(8,128)(2,1)S(1)} %get-tuple-element.114), channel_id=1, source_target_pairs={{0,1},{1,0},{2,3},{3,2},{4,5},{5,4},{6,7},{7,6},{8,9},{9,8},{10,11... | collective-permute-start | bytes 786440 | tf_op jit(solution)/shard_map/ppermute | solution.py:561
  136.3 8.9 %collective-permute-start.17 = (bf16[64,2048]{1,0:T(8,128)(2,1)S(1)}, bf16[64,2048]{1,0:T(8,128)(2,1)S(1)}, u32[]{:S(2)}, u32[]{:S(2)}) collective-permute-start(bf16[64,2048]{1,0:T(8,128)(2,1)S(1)} %get-tuple-element.105), channel_id=1, source_target_pairs={{0,2},{2,4},{4,6},{6,0},{1,3},{3,5},{5,7},{7,1},{8,10},{10,12},{12... | collective-permute-start | bytes 786440 | tf_op jit(solution)/shard_map/ppermute | solution.py:559
  136.8 15.0 %collective-permute-start.18 = (bf16[64,2048]{1,0:T(8,128)(2,1)S(1)}, bf16[64,2048]{1,0:T(8,128)(2,1)S(1)}, u32[]{:S(2)}, u32[]{:S(2)}) collective-permute-start(bf16[64,2048]{1,0:T(8,128)(2,1)S(1)} %get-tuple-element.106), channel_id=1, source_target_pairs={{0,4},{2,6},{4,0},{6,2},{1,5},{3,7},{5,1},{7,3},{8,12},{10,14},{12... | collective-permute-start | bytes 786440 | tf_op jit(solution)/shard_map/ppermute | solution.py:559
  140.3 11.4 %collective-permute-start.19 = (bf16[64,2048]{1,0:T(8,128)(2,1)S(1)}, bf16[64,2048]{1,0:T(8,128)(2,1)S(1)}, u32[]{:S(2)}, u32[]{:S(2)}) collective-permute-start(bf16[64,2048]{1,0:T(8,128)(2,1)S(1)} %get-tuple-element.107), channel_id=1, source_target_pairs={{0,6},{2,0},{4,2},{6,4},{1,7},{3,1},{5,3},{7,5},{8,14},{10,8},{12,... | collective-permute-start | bytes 786440 | tf_op jit(solution)/shard_map/ppermute | solution.py:559

commit v3 on v2

v3 whole, which is shorter than its diff:
```python
import functools
import math

import jax
import jax.numpy as jnp
import numpy as np
from jax import lax
from jax.experimental import pallas as pl
from jax.experimental.pallas import tpu as pltpu
from jax.sharding import Mesh, PartitionSpec as P

HD = 128
HQL = 4
BLOCK = 16
SUF = 512
PREFIX = 8192
WIDTH = HQL * HD
LOG2E = 1.4426950408889634
EXTRA = 16
COST = 5 * 10**9
SUFFIX_COST = 1
NEAR_COST = 10**10
PACK_COST = 4 * 10**9
PIECE = 32
SLABS = 8
BF = jnp.bfloat16
F32 = jnp.float32


def frequencies():
    return np.exp(-math.log(10000.0) * np.arange(HD // 2) * 2.0 / HD)


def suffix_tables():
    angle = (PREFIX + np.arange(SUF))[:, None] * frequencies()[None, :]
    cosine, sine = np.cos(angle), np.sin(angle)
    return (
        np.concatenate([cosine, cosine], axis=1).astype(np.float32),
        np.concatenate([-sine, sine], axis=1).astype(np.float32),
    )


def pieces_of_rows():
    count = SUF // PIECE // 2
    return [
        ((half * count + device) * PIECE, (2 * device + half) * PIECE)
        for half in range(2)
        for device in range(count)
    ]


def place_of_row(row):
    half, inside = row // (SUF // 2), row % (SUF // 2)
    return (2 * (inside // PIECE) + half) * PIECE + inside % PIECE


def call(kernel, name, vmem=24, flops=1, **kwargs):
    return pl.pallas_call(
        kernel,
        name=name,
        cost_estimate=pl.CostEstimate(flops=flops, bytes_accessed=1, transcendentals=0),
        compiler_params=pltpu.CompilerParams(vmem_limit_bytes=vmem * 2**20),
        **kwargs,
    )


def turn(values, cosine, sine):
    return values * cosine + pltpu.roll(values, HD // 2, 1) * sine


def prep_kernel(slots, freq, keys_hbm, values_hbm, *refs):
    outs, (keys, values, sems) = refs[:-3], refs[-3:]
    copies = [
        pltpu.make_async_copy(keys_hbm, keys, sems.at[0]),
        pltpu.make_async_copy(values_hbm, values, sems.at[1]),
    ]
    for copy in copies:
        copy.start()
    y, xhi = lax.axis_index("y"), lax.axis_index("xhi")
    chip = lax.axis_index("xlo") * 4 + lax.axis_index("z")
    device = (chip * 2 + lax.axis_index("core")) * 8 + y * 2 + xhi
    slot0 = device * (keys.shape[0] // BLOCK)
    shape = (slots.shape[0], slots.shape[1])
    block = (
        lax.broadcasted_iota(jnp.int32, shape, 0) * shape[1]
        + lax.broadcasted_iota(jnp.int32, shape, 1)
    ).astype(F32)
    rows = keys.shape[0]
    token = lax.broadcasted_iota(jnp.int32, (rows, HD), 0)
    position = jnp.zeros((rows, HD), F32)
    for i in range(rows // BLOCK):
        owner = jnp.sum(jnp.where(slots[...] == slot0 + i, block, 0.0))
        position = jnp.where(token // BLOCK == i, owner * BLOCK, position)
    position = position + (token % BLOCK).astype(F32)
    angle = position * freq[...]
    cosine = jnp.cos(angle)
    lane = lax.broadcasted_iota(jnp.int32, (rows, HD), 1)
    sine = jnp.sin(angle)
    sine = jnp.where(lane < HD // 2, -sine, sine)
    for kind, copy in enumerate(copies):
        copy.wait()
        for d, out in enumerate(outs):
            target = lax.rem(y + d, 4)
            for part in range(2):
                group = 2 * target + (xhi if part == 0 else 1 - xhi)
                to = pl.ds((part * 2 + kind) * rows, rows)
                for h in range(HQL):
                    at = pl.ds(pl.multiple_of(group * WIDTH + h * HD, HD), HD)
                    if kind == 0:
                        value = turn(keys[:, at].astype(F32), cosine, sine).astype(BF)
                    else:
                        value = values[:, at]
                    out[to, pl.ds(h * HD, HD)] = value


def prepare(block_slot, keys, values):
    rows = keys.shape[0]
    freq = np.tile(frequencies(), 2)[None, :].astype(np.float32)
    vmem = pl.BlockSpec(memory_space=pltpu.VMEM)
    return call(
        prep_kernel,
        "prepare",
        60,
        in_specs=[vmem] * 2
        + [pl.BlockSpec(memory_space=pltpu.HBM)] * 2,
        out_specs=[vmem] * 4,
        out_shape=[jax.ShapeDtypeStruct((4 * rows, WIDTH), BF)] * 4,
        scratch_shapes=[
            pltpu.VMEM(keys.shape, BF),
            pltpu.VMEM(values.shape, BF),
            pltpu.SemaphoreType.DMA((2,)),
        ],
    )(block_slot.reshape(4, -1), jnp.asarray(freq), keys, values)


def project_kernel(kinds, scale, *refs):
    n = len(kinds)
    hidden, weights, tables, outs = refs[0], refs[1 : n + 1], refs[n + 1 : n + 3], refs[n + 3 :]
    outs, (rows, *slabs), turns, sems = outs[:n], outs[n : 2 * n + 1], outs[-3:-1], outs[-1]
    depth = hidden.shape[1]
    deep = depth // SLABS
    copies = []
    for i in range(SLABS):
        at = pl.ds(i * deep, deep)
        slab = [(hidden.at[:, at], rows.at[:, at])]
        slab += [(w.at[at, :], v.at[at, :]) for w, v in zip(weights, slabs)]
        copies.append(
            [
                pltpu.make_async_copy(src, dst, sems.at[i, j])
                for j, (src, dst) in enumerate(slab)
            ]
        )
    copies.append(
        [
            pltpu.make_async_copy(src, dst, sems.at[SLABS, j])
            for j, (src, dst) in enumerate(zip(tables, turns))
        ]
    )
    for group in copies:
        for copy in group:
            copy.start()
    totals = [0.0] * n
    for i in range(SLABS):
        for copy in copies[i]:
            copy.wait()
        at = slice(i * deep, (i + 1) * deep)
        for j, slab in enumerate(slabs):
            totals[j] += jnp.dot(rows[:, at], slab[at, :], preferred_element_type=F32)
    for copy in copies[SLABS]:
        copy.wait()
    cosine, sine = turns
    for kind, out, total in zip(kinds, outs, totals):
        for h in range(HQL):
            at = slice(h * HD, (h + 1) * HD)
            value = total[:, at]
            if kind != "v":
                value = turn(value, cosine[...], sine[...])
            if kind == "q":
                for to, origin in pieces_of_rows():
                    rows_to = pl.ds(to, PIECE)
                    out[rows_to, at] = (value[origin : origin + PIECE] * scale).astype(BF)
            else:
                out[:, at] = value.astype(BF)


def project(kinds, hidden, weights, tables):
    rows, depth = hidden.shape
    n = len(kinds)
    hbm = pl.BlockSpec(memory_space=pltpu.HBM)
    return call(
        functools.partial(project_kernel, kinds, LOG2E / math.sqrt(HD)),
        "project_" + kinds,
        60,
        1,
        in_specs=[hbm] * (n + 3),
        out_specs=[pl.BlockSpec(memory_space=pltpu.VMEM)] * n,
        out_shape=[jax.ShapeDtypeStruct((rows, WIDTH), BF)] * n,
        scratch_shapes=[pltpu.VMEM((rows, depth), BF)]
        + [pltpu.VMEM((depth, WIDTH), BF)] * n
        + [pltpu.VMEM((rows, HD), F32)] * 2
        + [pltpu.SemaphoreType.DMA((SLABS + 1, max(n + 1, 2)))],
    )(hidden, *weights, *tables)


def pack_kernel(n, *refs):
    got, outs = refs[:n], refs[n:]
    rows = got[0].shape[0] // 4
    for part, out in enumerate(outs):
        for kind in range(2):
            for i, piece in enumerate(got):
                at = pl.ds((kind * n + i) * rows, rows)
                out[at, :] = piece[pl.ds((2 * part + kind) * rows, rows), :]


def pack(got):
    rows, width = got[0].shape
    vmem = pl.BlockSpec(memory_space=pltpu.VMEM)
    return call(
        functools.partial(pack_kernel, len(got)),
        "pack",
        flops=PACK_COST,
        in_specs=[vmem] * len(got),
        out_specs=[vmem] * 2,
        out_shape=[jax.ShapeDtypeStruct((len(got) * rows // 2, width), BF)] * 2,
    )(*got)


def widen(v):
    return jnp.concatenate([v, jnp.ones_like(v)], axis=1)


def suffix_kernel(length, q_ref, k_ref, v_ref, sum_ref, top_ref):
    tile = 128
    for t in range(SUF // tile):
        rows, keys = pl.ds(t * tile, tile), (t % 2 + 1) * SUF // 2
        row = place_of_row(t * tile + lax.broadcasted_iota(jnp.int32, (tile, keys), 0))
        column = lax.broadcasted_iota(jnp.int32, (tile, keys), 1)
        mask = (column <= row) & (column < length[0])
        for h in range(HQL):
            head = slice(h * HD, (h + 1) * HD)
            s = lax.dot_general(
                q_ref[rows, head],
                k_ref[:keys, head],
                (((1,), (1,)), ((), ())),
                preferred_element_type=F32,
            )
            s = jnp.where(mask, s, -1e30)
            top = jnp.max(s, axis=1, keepdims=True)
            p = jnp.exp2(s - top).astype(BF)
            sum_ref[rows, 2 * h * HD : 2 * (h + 1) * HD] = jnp.dot(
                p, widen(v_ref[:keys, head]), preferred_element_type=F32
            )
            top_ref[rows, head] = jnp.broadcast_to(top, (tile, HD))


def suffix_attention(length, q, k, v):
    vmem = pl.BlockSpec(memory_space=pltpu.VMEM)
    return call(
        suffix_kernel,
        "suffix_attention",
        flops=SUFFIX_COST,
        in_specs=[pl.BlockSpec(memory_space=pltpu.SMEM)] + [vmem] * 3,
        out_specs=[vmem] * 2,
        out_shape=STATE,
    )(length, q, k, v)


def split_log(log):
    high = log.astype(BF)
    rest = log - high.astype(F32)
    middle = rest.astype(BF)
    return high, middle, (rest - middle.astype(F32)).astype(BF)


def prefix_kernel(nq, nkv, used, held, halves, *refs):
    qs, kvs = refs[:nq], refs[nq : nq + nkv]
    old, at = [], nq + nkv
    for has in held:
        old.append(refs[at : at + 2] if has else None)
        at += 2 * has
    outs = refs[at:]
    half = kvs[0].shape[0] // 2
    tile = SUF // 2

    def one_tile(h, r, rows, out=None):
        head = slice(h * HD, (h + 1) * HD)
        wide = slice(2 * h * HD, 2 * (h + 1) * HD)
        n = used[r]
        k = jnp.concatenate([kv[:half, head] for kv in kvs[:n]], axis=0)
        v = jnp.concatenate([kv[half:, head] for kv in kvs[:n]], axis=0)
        s = lax.dot_general(
            qs[r][rows, head],
            k,
            (((1,), (1,)), ((), ())),
            preferred_element_type=F32,
        )
        top = jnp.broadcast_to(jnp.max(s, axis=1, keepdims=True), (tile, HD))
        if old[r] is not None:
            before = old[r][1][rows, head]
            top = jnp.maximum(before, top)
        p = jnp.exp2(s - jnp.concatenate([top] * (n * half // HD), axis=1)).astype(BF)
        both = jnp.dot(p, widen(v), preferred_element_type=F32)
        if old[r] is not None:
            shrink = jnp.exp2(before - top)
            both += jnp.concatenate([shrink] * 2, axis=1) * old[r][0][rows, wide]
        if not halves:
            outs[2 * r][rows, wide] = both
            outs[2 * r + 1][rows, head] = top
            return
        acc, total = both[:, :HD], both[:, HD:]
        out[:tile, head] = (acc / total).astype(BF)
        log = top + jnp.log2(total)
        logs = [log[i : i + HD].T[:1] for i in range(0, tile, HD)]
        rest = jnp.zeros((EXTRA - 3 * len(logs), HD), BF)
        parts = split_log(jnp.concatenate(logs, axis=0))
        out[tile:, head] = jnp.concatenate([*parts, rest], axis=0)

    if not halves:

        @pl.loop(0, SUF // tile)
        def _(t):
            rows = pl.ds(pl.multiple_of(t * tile, tile), tile)
            for h in range(HQL):
                for r in range(nq):
                    one_tile(h, r, rows)

        return
    for h in range(HQL):
        for r in range(nq):
            for i, t in enumerate(halves):
                out = outs[r * len(halves) + i]
                one_tile(h, r, pl.ds(t * tile, tile), out)


STATE = [
    jax.ShapeDtypeStruct((SUF, 2 * WIDTH), F32),
    jax.ShapeDtypeStruct((SUF, WIDTH), F32),
]


def prefix_attention(name, qs, kvs, used, states, halves=(), cost=1):
    nq, nkv = len(qs), len(kvs)
    held = [state is not None for state in states]
    extra = [x for state in states if state is not None for x in state]
    vmem = pl.BlockSpec(memory_space=pltpu.VMEM)
    message = jax.ShapeDtypeStruct((SUF // 2 + EXTRA, WIDTH), BF)
    shapes = [message] * len(halves) * nq if halves else STATE * nq
    out = call(
        functools.partial(prefix_kernel, nq, nkv, used, held, halves),
        name,
        flops=cost,
        in_specs=[vmem] * (nq + nkv + len(extra)),
        out_specs=[vmem] * len(shapes),
        out_shape=shapes,
    )(*qs, *kvs, *extra)
    return list(out) if halves else [out[i : i + 2] for i in range(0, 2 * nq, 2)]


def combine(parts, length, half, attended):
    tile = HD
    count = SUF // 2 // tile
    row = lax.broadcasted_iota(jnp.int32, (tile, HD), 0)
    for h in range(HQL):
        at = pl.ds(h * HD, HD)
        logs = []
        for part in parts:
            tail = part[SUF // 2 :, at].astype(F32)
            logs.append(
                tail[:count] + tail[count : 2 * count] + tail[2 * count : 3 * count]
            )
        top = functools.reduce(jnp.maximum, logs)
        shares = [jnp.exp2(log - top) for log in logs]
        total = functools.reduce(lambda a, b: a + b, shares)
        shares = [share / total for share in shares]
        for t in range(count):
            rows = pl.ds(t * tile, tile)
            acc = jnp.zeros((tile, HD), F32)
            for share, part in zip(shares, parts):
                wide = jnp.broadcast_to(share[t : t + 1, :], (tile, HD)).T
                acc += wide * part[rows, at].astype(F32)
            live = place_of_row(half * (SUF // 2) + t * tile + row) < length[0]
            attended[rows, at] = jnp.where(live, acc, 0.0).astype(BF)


def output_kernel(n, half, length, *refs):
    parts, weight, outs = refs[:n], refs[n], refs[n + 1 : -2]
    attended, ordered = refs[-2:]

    @pl.when(pl.program_id(0) == 0)
    def _():
        combine(parts, length, half, attended)
        if half == 1:
            xhi = lax.axis_index("xhi")
            groups = [2 * y + x for x in (1 - xhi, xhi) for y in range(4)]
        else:
            y = lax.axis_index("y")
            groups = [2 * lax.rem(y + d, 4) + x for d in range(4) for x in range(2)]
        for i, group in enumerate(groups):
            at = pl.ds(pl.multiple_of(group * PIECE, PIECE), PIECE)
            ordered[pl.ds(i * PIECE, PIECE), :] = attended[at, :]

    rows = outs[0].shape[0]
    for i, out in enumerate(outs):
        out[...] = jnp.dot(
            ordered[pl.ds(i * rows, rows), :], weight[...], preferred_element_type=F32
        ).astype(BF)


def output_half(length, half, parts, weight):
    n = len(parts)
    width = weight.shape[1]
    wide = 1024
    count = 4 if half == 0 else 2
    rows = SUF // 2 // count
    whole = pl.BlockSpec((SUF // 2 + EXTRA, WIDTH), lambda i: (0, 0))
    return call(
        functools.partial(output_kernel, n, half),
        "output_half",
        flops=1 + half * COST,
        grid=(width // wide,),
        in_specs=[pl.BlockSpec(memory_space=pltpu.SMEM)]
        + [whole] * n
        + [pl.BlockSpec((WIDTH, wide), lambda i: (0, i))],
        out_specs=[pl.BlockSpec((rows, wide), lambda i: (0, i))] * count,
        out_shape=[jax.ShapeDtypeStruct((rows, width), BF)] * count,
        scratch_shapes=[pltpu.VMEM((SUF // 2, WIDTH), BF)] * 2,
    )(length, *parts, weight)


def add_up(refs, at=slice(None)):
    return functools.reduce(lambda a, b: a + b, [r[at, :].astype(F32) for r in refs])


def sum_x_kernel(ours, theirs, *outs):
    y = lax.axis_index("y")
    rows = outs[0].shape[0]
    for d, out in enumerate(outs):
        at = pl.ds(pl.multiple_of(lax.rem(y + d, 4) * rows, rows), rows)
        out[...] = add_up([ours, theirs], at).astype(BF)


def sum_x(ours, theirs):
    rows, width = ours.shape
    wide = 1024
    return call(
        sum_x_kernel,
        "sum_x",
        grid=(width // wide,),
        in_specs=[pl.BlockSpec((rows, wide), lambda i: (0, i))] * 2,
        out_specs=[pl.BlockSpec((rows // 4, wide), lambda i: (0, i))] * 4,
        out_shape=[jax.ShapeDtypeStruct((rows // 4, width), BF)] * 4,
    )(ours, theirs)


def sum_y_kernel(n, *refs):
    parts, (theirs, ours) = refs[:n], refs[n:]
    xhi = lax.axis_index("xhi")
    rows = ours.shape[0]
    for part, out in ((1 - xhi, theirs), (xhi, ours)):
        at = pl.ds(pl.multiple_of(part * rows, rows), rows)
        out[...] = add_up(parts, at).astype(BF)


def sum_y(parts):
    rows, width = parts[0].shape
    wide = 1024
    return call(
        functools.partial(sum_y_kernel, len(parts)),
        "sum_y",
        flops=2 * 10**10,
        grid=(width // wide,),
        in_specs=[pl.BlockSpec((rows, wide), lambda i: (0, i))] * len(parts),
        out_specs=[pl.BlockSpec((rows // 2, wide), lambda i: (0, i))] * 2,
        out_shape=[jax.ShapeDtypeStruct((rows // 2, width), BF)] * 2,
    )(*parts)


def finish_kernel(n, *refs):
    upper, lower, out = refs[:n], refs[n:-1], refs[-1]
    rows = upper[0].shape[0]
    out[:rows, :] = add_up(upper).astype(BF)
    out[rows:, :] = add_up(lower).astype(BF)


def finish(upper, lower):
    rows, width = upper[0].shape
    vmem = pl.BlockSpec(memory_space=pltpu.VMEM)
    return call(
        functools.partial(finish_kernel, len(upper)),
        "finish",
        in_specs=[vmem] * (len(upper) + len(lower)),
        out_specs=vmem,
        out_shape=jax.ShapeDtypeStruct((2 * rows, width), BF),
    )(*upper, *lower)


def shift(n, by):
    return [(i, (i + by) % n) for i in range(n)]


def in_order(values, *others):
    return list(lax.optimization_barrier((*values, *others)))[: len(values)]


def body(
    hidden, w_query, w_key, w_value, w_output, prefix_keys, prefix_values, block_slot, suffix_len
):
    slots, block, feats = prefix_keys.shape
    rows = slots * block
    tables = [jnp.asarray(t) for t in suffix_tables()]

    def core(x):
        return lax.ppermute(x, "core", shift(2, 1))

    def along_z(x, by):
        return lax.ppermute(x, "z", shift(4, by))

    sent = prepare(
        block_slot, prefix_keys.reshape(rows, feats), prefix_values.reshape(rows, feats)
    )
    got = [sent[0]] + [lax.ppermute(sent[d], "y", shift(4, d)) for d in (1, 2, 3)]

    (hidden,) = in_order([hidden], sent[0])
    (q,) = project("q", hidden, [w_query], tables)
    q2, q1, q3 = [along_z(q, by) for by in (2, 1, -1)]
    got = in_order(got, q)
    near, far = pack(got)
    near_x = lax.ppermute(near, "xlo", shift(2, 1))
    far_x = lax.ppermute(far, ("xlo", "xhi"), [(0, 3), (3, 0), (1, 2), (2, 1)])
    (hidden,) = in_order([hidden], near)
    k_suffix, v_suffix = project("kv", hidden, [w_key, w_value], tables)
    begun = suffix_attention(suffix_len, q, k_suffix, v_suffix)
    queries = in_order([q2, q1, q3], begun[0])
    near_c = core(in_order([near], *queries)[0])

    near_x, far_x = in_order([near_x, far_x], begun[0])
    far_xx = lax.ppermute(far_x, "xlo", shift(2, 1))
    middle = [near_x, far_x, core(near_x), core(far_x)]
    states = prefix_attention(
        "attend_near",
        in_order(queries, near_x, far_x),
        [near, near_c],
        [2] * 3,
        [None] * 3,
        cost=NEAR_COST,
    )
    states = prefix_attention("attend_middle", queries, middle, [4] * 3, states)
    (far_xx,) = in_order([far_xx], states[0][0])
    final = [far_xx, core(far_xx)]
    sums = []
    for half in range(2):
        sent = prefix_attention("attend_last", queries, final, [2] * 3, states, [half])
        sums.append([along_z(m, back) for m, back in zip(sent, [2, -1, 1])])
        final = in_order(final, sent[0])
    every = [near, near_c, *middle, *final]
    own = prefix_attention("attend_own", [q], every, [8], [begun], [0, 1])
    cut = output_half(suffix_len, 0, in_order(sums[0], own[0]) + [own[0]], w_output)
    sums[1] = in_order(sums[1], cut[0])
    cut = [cut[0]] + [lax.ppermute(cut[d], "y", shift(4, d)) for d in (1, 2, 3)]
    theirs, ours = output_half(suffix_len, 1, sums[1] + [own[1]], w_output)
    theirs = lax.ppermute(theirs, "xhi", shift(2, 1))
    cut = in_order(cut, ours)
    upper_theirs, upper_ours = sum_y(cut)
    upper = [upper_ours, lax.ppermute(upper_theirs, "xhi", shift(2, 1))]
    (theirs,) = in_order([theirs], upper_ours)
    lower = sum_x(ours, theirs)
    lower = [lower[0]] + [lax.ppermute(lower[d], "y", shift(4, d)) for d in (1, 2, 3)]
    return finish(upper, lower)


def solution(mesh):
    fine = Mesh(
        mesh.devices.reshape(2, 4, 2, 4, 2), ("xlo", "z", "core", "y", "xhi")
    )
    pool, head = ("xlo", "z", "core"), ("y", "xhi")
    placed = (
        P(pool, None),
        P(None, head),
        P(None, head),
        P(None, head),
        P(head, None),
        P(pool + head, None, None),
        P(pool + head, None, None),
        P(),
        P(pool),
    )
    return jax.shard_map(
        body, mesh=fine, in_specs=placed, out_specs=P(pool + head, None), check_vma=False
    )
```

time: 153 us -> 136 us (0.89)
  waiting for transfers between devices: 70.9 us -> 38.9 us
  starting transfers between devices: 27.8 us -> 41.6 us
  Pallas kernels: 49.2 us -> 51.9 us
  local copies, waits for them, and re-layouts: 4.1 us -> 2.09 us
    ppermute x6 -> x9, waiting for transfers between devices: 23.7 us -> 5.38 us  [along_z(): return lax.ppermute(x, 'z', shift(4, by))]
    ppermute x6 -> x9, starting transfers between devices: 6.51 us -> 16.7 us  [along_z(): return lax.ppermute(x, 'z', shift(4, by))]
    ppermute x3, waiting for transfers between devices: 23.2 us -> 14.2 us  [body(): cut = [cut[0]] + [lax.ppermute(cut[d], 'y', shift(4, d)) for d in (1, 2, 3)]]
    ppermute x1, waiting for transfers between devices: 8.32 us -> 0.01 us  [body(): far_x = lax.ppermute(far, ('xlo', 'xhi'), [(0, 3), (3, 0), (1, 2), (2, 1)])]
    ppermute x1, waiting for transfers between devices: 0.01 us -> 6.66 us  [body(): theirs = lax.ppermute(theirs, 'xhi', shift(2, 1))]
    pallas_call x14 -> x13, Pallas kernels: 45.4 us -> 48.1 us  [the longest x5 22.5 us: prefix_attention(): call(functools.partial(prefix_kernel, nq, nkv, used, held, halves), name,...]
    ppermute x1, starting transfers between devices: 0.93 us -> 3.1 us  [body(): theirs = lax.ppermute(theirs, 'xhi', shift(2, 1))]
    unnamed x16 -> x10, local copies, waits for them, and re-layouts: 4.1 us -> 2.09 us
  transfers between devices with their start and end apart: 24 -> 27, of which waited for: 15 -> 12; matrix products, arithmetic and copies ran while one was open for 0% -> 0% of each run, Pallas kernels for 26% -> 34%
where the time goes in v3:
time: 136 us; the launch traced here: 135 us
  Pallas kernels  51.9 us (38%)
  starting transfers between devices  41.6 us (31%)
  waiting for transfers between devices  38.9 us (29%)
  local copies, waits for them, and re-layouts  2.09 us (2%)
    pallas_call x5, Pallas kernels, prefix_attention(): call(functools.partial(prefix_kernel, nq, nkv, used, held, halves), name,...  22.5 us
    ppermute x9, starting transfers between devices, along_z(): return lax.ppermute(x, 'z', shift(4, by))  16.7 us
    ppermute x3, waiting for transfers between devices, body(): cut = [cut[0]] + [lax.ppermute(cut[d], 'y', shift(4, d)) for d in (1, 2, 3)]  14.2 us
    pallas_call x2, Pallas kernels, project(): call(functools.partial(project_kernel, kinds, LOG2E / math.sqrt(HD)), 'pr...  13.8 us
    ppermute x3, waiting for transfers between devices, body(): lax.ppermute(lower[d], 'y', shift(4, d))  9.83 us
    pallas_call x2, Pallas kernels, output_half(): call(functools.partial(output_kernel, n, half), 'output_half', flops=1 +...  7.54 us
    ppermute x1, waiting for transfers between devices, body(): theirs = lax.ppermute(theirs, 'xhi', shift(2, 1))  6.66 us
    ppermute x3, starting transfers between devices, body(): lax.ppermute(sent[d], 'y', shift(4, d))  5.98 us
  transfers between devices with their start and end apart: 27, of which 12 were waited for; matrix products, arithmetic and copies ran while one was open for 0% of the time, Pallas kernels for 34%

profile of v3, /device:TPU:0, one launch (start us, length us, event | category | flops | bytes accessed | tf_op | source)
XLA Modules:
  0.0 135.3 jit_solution(922645385228668158)
XLA Ops:
  0.0 3.2 %prepare.1 = (bf16[256,512]{1,0:T(8,128)(2,1)}, bf16[256,512]{1,0:T(8,128)(2,1)}, bf16[256,512]{1,0:T(8,128)(2,1)}, bf16[256,512]{1,0:T(8,128)(2,1)}) custom-call(s32[4,128]{1,0:T(4,128)} %bitcast.5, f32[1,128]{1,0:T(1,128)} %constant.8.clone.freq, bf16[64,4096]{1,0:T(8,128)(2,1)} %bitcast.3, bf16[64,4096]{1,0:T(8,128)(2,1)} %bitcast.4), custom_call_target="tpu_custom_call" | custom-call | flops 1 | bytes 1 | tf_op jit(solution)/shard_map/prepare/pallas_call | solution.py:120
  3.2 1.7 %collective-permute-start.3 = (bf16[256,512]{1,0:T(8,128)(2,1)}, bf16[256,512]{1,0:T(8,128)(2,1)S(1)}, u32[]{:S(2)}, u32[]{:S(2)}) collective-permute-start(bf16[256,512]{1,0:T(8,128)(2,1)} %get-tuple-element.80), channel_id=1, source_target_pairs={{0,2},{2,4},{4,6},{6,0},{1,3},{3,5},{5,7},{7,1},{8,10},{10,12},{12... | collective-permute-start | bytes 786440 | tf_op jit(solution)/shard_map/ppermute | solution.py:521
  4.9 2.9 %collective-permute-start.4 = (bf16[256,512]{1,0:T(8,128)(2,1)}, bf16[256,512]{1,0:T(8,128)(2,1)S(1)}, u32[]{:S(2)}, u32[]{:S(2)}) collective-permute-start(bf16[256,512]{1,0:T(8,128)(2,1)} %get-tuple-element.81), channel_id=1, source_target_pairs={{0,4},{2,6},{4,0},{6,2},{1,5},{3,7},{5,1},{7,3},{8,12},{10,14},{12... | collective-permute-start | bytes 786440 | tf_op jit(solution)/shard_map/ppermute | solution.py:521
  7.8 1.3 collective-permute-start.5
  9.2 5.5 %project_q.1.q_ref.refs_0_ = bf16[512,512]{1,0:T(8,128)(2,1)} custom-call(bf16[512,4096]{1,0:T(8,128)(2,1)} %refs_0_.1, bf16[4096,512]{1,0:T(8,128)(2,1)} %refs_1_.2, f32[512,128]{1,0:T(8,128)} %constant.6.clone.refs_2_.refs_3_, f32[512,128]{1,0:T(8,128)} %constant.7.clone.refs_3_.refs_4_), custom_call_target="tpu_custom_call" | custom-call | flops 1 | bytes 1 | tf_op jit(solution)/shard_map/project_q/pallas_call | solution.py:190
  14.7 4.0 %collective-permute-start = (bf16[512,512]{1,0:T(8,128)(2,1)}, bf16[512,512]{1,0:T(8,128)(2,1)S(1)}, u32[]{:S(2)}, u32[]{:S(2)}) collective-permute-start(bf16[512,512]{1,0:T(8,128)(2,1)} %project_q.1.q_ref.refs_0_), channel_id=1, source_target_pairs={{0,32},{16,48},{32,0},{48,16},{1,33},{17,49},{33,1},{49,17},{2,34}... | collective-permute-start | bytes 1572872 | tf_op jit(solution)/shard_map/ppermute | solution.py:516
  18.6 1.0 collective-permute-start.1
  19.7 2.2 %collective-permute-start.2 = (bf16[512,512]{1,0:T(8,128)(2,1)}, bf16[512,512]{1,0:T(8,128)(2,1)S(1)}, u32[]{:S(2)}, u32[]{:S(2)}) collective-permute-start(bf16[512,512]{1,0:T(8,128)(2,1)} %project_q.1.q_ref.refs_0_), channel_id=1, source_target_pairs={{0,48},{16,0},{32,16},{48,32},{1,49},{17,1},{33,17},{49,33},{2,50}... | collective-permute-start | bytes 1572872 | tf_op jit(solution)/shard_map/ppermute | solution.py:516
  22.6 0.9 pack.1
  23.4 1.5 %collective-permute-start.6 = (bf16[512,512]{1,0:T(8,128)(2,1)S(1)}, bf16[512,512]{1,0:T(8,128)(2,1)S(1)}, u32[]{:S(2)}, u32[]{:S(2)}) collective-permute-start(bf16[512,512]{1,0:T(8,128)(2,1)S(1)} %get-tuple-element.101.refs_3_.refs_1_), channel_id=1, source_target_pairs={{0,64},{64,0},{1,65},{65,1},{2,66},{66,2},{3,67},{67,3},{4,68},{68... | collective-permute-start | bytes 1572872 | tf_op jit(solution)/shard_map/ppermute | solution.py:528
  24.9 2.1 %collective-permute-start.7 = (bf16[512,512]{1,0:T(8,128)(2,1)}, bf16[512,512]{1,0:T(8,128)(2,1)S(1)}, u32[]{:S(2)}, u32[]{:S(2)}) collective-permute-start(bf16[512,512]{1,0:T(8,128)(2,1)} %get-tuple-element.95), channel_id=1, source_target_pairs={{0,65},{65,0},{1,64},{64,1},{2,67},{67,2},{3,66},{66,3},{4,69},{69... | collective-permute-start | bytes 1572872 | tf_op jit(solution)/shard_map/ppermute | solution.py:529
  27.0 8.3 %project_kv.1 = (bf16[512,512]{1,0:T(8,128)(2,1)}, bf16[512,512]{1,0:T(8,128)(2,1)}) custom-call(bf16[512,4096]{1,0:T(8,128)(2,1)} %refs_0_.1, bf16[4096,512]{1,0:T(8,128)(2,1)} %refs_1_.3, bf16[4096,512]{1,0:T(8,128)(2,1)} %refs_2_.2, f32[512,128]{1,0:T(8,128)} %constant.6.clone.refs_2_.refs_3_, f32[512,128]{1,0:T(8,128)} %constant.7.clone.refs_3_.refs_4_), custom_call_target="tpu_custom_call" | custom-call | flops 1 | bytes 1 | tf_op jit(solution)/shard_map/project_kv/pallas_call | solution.py:190
  35.3 1.0 copy-done.2
  36.4 1.0 copy-done.3
  37.4 1.8 %suffix_attention.1 = (f32[512,1024]{1,0:T(8,128)S(1)}, f32[512,512]{1,0:T(8,128)S(1)}) custom-call(s32[1]{0:T(128)S(6)} %copy.13.length, bf16[512,512]{1,0:T(8,128)(2,1)S(1)} %copy-done, bf16[512,512]{1,0:T(8,128)(2,1)S(1)} %copy-done.2, bf16[512,512]{1,0:T(8,128)(2,1)S(1)} %copy-done.3), custom_call_target="tpu_custom_call" | custom-call | flops 1 | bytes 1 | tf_op jit(solution)/shard_map/suffix_attention/pallas_call | solution.py:258
  39.3 1.9 %collective-permute-done.1.refs_1_ = bf16[512,512]{1,0:T(8,128)(2,1)S(1)} collective-permute-done((bf16[512,512]{1,0:T(8,128)(2,1)}, bf16[512,512]{1,0:T(8,128)(2,1)S(1)}, u32[]{:S(2)}, u32[]{:S(2)}) %collective-permute-start.1) | collective-permute-done | bytes 524320 | tf_op jit(solution)/shard_map/ppermute | solution.py:516
  41.2 0.8 collective-permute-done.2.refs_2_
  42.6 1.5 %collective-permute-start.8 = (bf16[512,512]{1,0:T(8,128)(2,1)S(1)}, bf16[512,512]{1,0:T(8,128)(2,1)S(1)}, u32[]{:S(2)}, u32[]{:S(2)}) collective-permute-start(bf16[512,512]{1,0:T(8,128)(2,1)S(1)} %collective-permute-done.7.refs_4_), channel_id=1, source_target_pairs={{0,64},{64,0},{1,65},{65,1},{2,66},{66,2},{3,67},{67,3},{4,68},{68... | collective-permute-start | bytes 1572872 | tf_op jit(solution)/shard_map/ppermute | solution.py:537
  44.1 4.1 %attend_near.1 = (f32[512,1024]{1,0:T(8,128)S(1)}, f32[512,512]{1,0:T(8,128)S(1)}, f32[512,1024]{1,0:T(8,128)S(1)}, f32[512,512]{1,0:T(8,128)S(1)}, f32[512,1024]{1,0:T(8,128)S(1)}, /*index=5*/f32[512,512]{1,0:T(8,128)S(1)}) custom-call(bf16[512,512]{1,0:T(8,128)(2,1)S(1)} %collective-permute-done.refs_0_, ...), custom_call_target="tpu_custom_call" | custom-call | flops 10000000000 | bytes 1 | tf_op jit(solution)/shard_map/attend_near/pallas_call | solution.py:348
  48.2 8.2 %attend_middle.1 = (f32[512,1024]{1,0:T(8,128)S(1)}, f32[512,512]{1,0:T(8,128)S(1)}, f32[512,1024]{1,0:T(8,128)S(1)}, f32[512,512]{1,0:T(8,128)S(1)}, f32[512,1024]{1,0:T(8,128)S(1)}, /*index=5*/f32[512,512]{1,0:T(8,128)S(1)}) custom-call(bf16[512,512]{1,0:T(8,128)(2,1)S(1)} %collective-permute-done.refs_0_, ...), custom_call_target="tpu_custom_call" | custom-call | flops 1 | bytes 1 | tf_op jit(solution)/shard_map/attend_middle/pallas_call | solution.py:348
  56.8 1.9 %collective-permute-done.12.refs_4_.refs_8_ = bf16[512,512]{1,0:T(8,128)(2,1)S(1)} collective-permute-done((bf16[512,512]{1,0:T(8,128)(2,1)S(1)}, bf16[512,512]{1,0:T(8,128)(2,1)S(1)}, u32[]{:S(2)}, u32[]{:S(2)}) %collective-permute-start.12) | collective-permute-done | bytes 524320 | tf_op jit(solution)/shard_map/ppermute | solution.py:513
  58.7 2.4 %attend_last.2 = (bf16[272,512]{1,0:T(8,128)(2,1)S(1)}, bf16[272,512]{1,0:T(8,128)(2,1)S(1)}, bf16[272,512]{1,0:T(8,128)(2,1)S(1)}) custom-call(bf16[512,512]{1,0:T(8,128)(2,1)S(1)} %collective-permute-done.refs_0_, bf16[512,512]{1,0:T(8,128)(2,1)S(1)} %collective-permute-done.1.refs_1_, bf16[512,512]{1,0:T(8,128)(2,1)S(1)} %collective-permute-done.2.refs_2_, ...), custom_call_target="tpu_custom_call" | custom-call | flops 1 | bytes 1 | tf_op jit(solution)/shard_map/attend_last/pallas_call | solution.py:348
  61.1 2.1 %collective-permute-start.13 = (bf16[272,512]{1,0:T(8,128)(2,1)S(1)}, bf16[272,512]{1,0:T(8,128)(2,1)S(1)}, u32[]{:S(2)}, u32[]{:S(2)}) collective-permute-start(bf16[272,512]{1,0:T(8,128)(2,1)S(1)} %get-tuple-element.115), channel_id=1, source_target_pairs={{0,32},{16,48},{32,0},{48,16},{1,33},{17,49},{33,1},{49,17},{2,34}... | collective-permute-start | bytes 835592 | tf_op jit(solution)/shard_map/ppermute | solution.py:516
  63.2 1.6 %collective-permute-start.14 = (bf16[272,512]{1,0:T(8,128)(2,1)S(1)}, bf16[272,512]{1,0:T(8,128)(2,1)S(1)}, u32[]{:S(2)}, u32[]{:S(2)}) collective-permute-start(bf16[272,512]{1,0:T(8,128)(2,1)S(1)} %get-tuple-element.116), channel_id=1, source_target_pairs={{0,48},{16,0},{32,16},{48,32},{1,49},{17,1},{33,17},{49,33},{2,50}... | collective-permute-start | bytes 835592 | tf_op jit(solution)/shard_map/ppermute | solution.py:516
  65.3 2.4 %attend_last.3 = (bf16[272,512]{1,0:T(8,128)(2,1)S(1)}, bf16[272,512]{1,0:T(8,128)(2,1)S(1)}, bf16[272,512]{1,0:T(8,128)(2,1)S(1)}) custom-call(bf16[512,512]{1,0:T(8,128)(2,1)S(1)} %collective-permute-done.refs_0_, bf16[512,512]{1,0:T(8,128)(2,1)S(1)} %collective-permute-done.1.refs_1_, bf16[512,512]{1,0:T(8,128)(2,1)S(1)} %collective-permute-done.2.refs_2_, ...), custom_call_target="tpu_custom_call" | custom-call | flops 1 | bytes 1 | tf_op jit(solution)/shard_map/attend_last/pallas_call | solution.py:348
  67.6 1.7 %collective-permute-start.19 = (bf16[272,512]{1,0:T(8,128)(2,1)S(1)}, bf16[272,512]{1,0:T(8,128)(2,1)S(1)}, u32[]{:S(2)}, u32[]{:S(2)}) collective-permute-start(bf16[272,512]{1,0:T(8,128)(2,1)S(1)} %get-tuple-element.120), channel_id=1, source_target_pairs={{0,32},{16,48},{32,0},{48,16},{1,33},{17,49},{33,1},{49,17},{2,34}... | collective-permute-start | bytes 835592 | tf_op jit(solution)/shard_map/ppermute | solution.py:516
  69.4 2.6 %collective-permute-start.20 = (bf16[272,512]{1,0:T(8,128)(2,1)S(1)}, bf16[272,512]{1,0:T(8,128)(2,1)S(1)}, u32[]{:S(2)}, u32[]{:S(2)}) collective-permute-start(bf16[272,512]{1,0:T(8,128)(2,1)S(1)} %get-tuple-element.132), channel_id=1, source_target_pairs={{0,48},{16,0},{32,16},{48,32},{1,49},{17,1},{33,17},{49,33},{2,50}... | collective-permute-start | bytes 835592 | tf_op jit(solution)/shard_map/ppermute | solution.py:516
  72.2 1.0 collective-permute-start.21
  73.2 5.5 %attend_own.1 = (bf16[272,512]{1,0:T(8,128)(2,1)S(1)}, bf16[272,512]{1,0:T(8,128)(2,1)S(1)}) custom-call(bf16[512,512]{1,0:T(8,128)(2,1)S(1)} %copy-done, bf16[512,512]{1,0:T(8,128)(2,1)S(1)} %get-tuple-element.101.refs_3_.refs_1_, bf16[512,512]{1,0:T(8,128)(2,1)S(1)} %collective-permute-done.11.refs_4_.refs_2_, ...), custom_call_target="tpu_custom_call" | custom-call | flops 1 | bytes 1 | tf_op jit(solution)/shard_map/attend_own/pallas_call | solution.py:348
  78.7 4.6 %output_half.2 = (bf16[64,4096]{1,0:T(8,128)(2,1)S(1)}, bf16[64,4096]{1,0:T(8,128)(2,1)S(1)}, bf16[64,4096]{1,0:T(8,128)(2,1)S(1)}, bf16[64,4096]{1,0:T(8,128)(2,1)S(1)}) custom-call(s32[1]{0:T(128)S(6)} %copy.13.length, bf16[272,512]{1,0:T(8,128)(2,1)S(1)} %collective-permute-done.13.refs_0_, bf16[272,512]{1,0:T(8,128)(2,1)S(1)} %collective-permute-done.14.refs_1_, ...), custom_call_target="tpu_custom_call" | custom-call | flops 1 | bytes 1 | tf_op jit(solution)/shard_map/output_half/pallas_call | solution.py:416
  83.3 0.7 collective-permute-start.16
  84.1 1.1 collective-permute-start.17
  85.2 1.7 %collective-permute-start.18 = (bf16[64,4096]{1,0:T(8,128)(2,1)S(1)}, bf16[64,4096]{1,0:T(8,128)(2,1)S(1)}, u32[]{:S(2)}, u32[]{:S(2)}) collective-permute-start(bf16[64,4096]{1,0:T(8,128)(2,1)S(1)} %get-tuple-element.131), channel_id=1, source_target_pairs={{0,6},{2,0},{4,2},{6,4},{1,7},{3,1},{5,3},{7,5},{8,14},{10,8},{12,... | collective-permute-start | bytes 1572872 | tf_op jit(solution)/shard_map/ppermute | solution.py:559
  86.9 2.5 %collective-permute-done.20.refs_1_ = bf16[272,512]{1,0:T(8,128)(2,1)S(1)} collective-permute-done((bf16[272,512]{1,0:T(8,128)(2,1)S(1)}, bf16[272,512]{1,0:T(8,128)(2,1)S(1)}, u32[]{:S(2)}, u32[]{:S(2)}) %collective-permute-start.20) | collective-permute-done | bytes 278560 | tf_op jit(solution)/shard_map/ppermute | solution.py:516
  89.3 3.0 %output_half.3 = (bf16[128,4096]{1,0:T(8,128)(2,1)S(1)}, bf16[128,4096]{1,0:T(8,128)(2,1)S(1)}) custom-call(s32[1]{0:T(128)S(6)} %copy.13.length, bf16[272,512]{1,0:T(8,128)(2,1)S(1)} %collective-permute-done.19.refs_0_, bf16[272,512]{1,0:T(8,128)(2,1)S(1)} %collective-permute-done.20.refs_1_, bf16[272,512]{1,0:T(8,128)(2,1)S(1)} %collective-permute-done.21.refs_2_, ...), custom_call_target="tpu_custom_call" | custom-call | flops 5000000000 | bytes 1 | tf_op jit(solution)/shard_map/output_half/pallas_call | solution.py:416
  92.3 3.1 %collective-permute-start.23 = (bf16[128,4096]{1,0:T(8,128)(2,1)S(1)}, bf16[128,4096]{1,0:T(8,128)(2,1)S(1)}, u32[]{:S(2)}, u32[]{:S(2)}) collective-permute-start(bf16[128,4096]{1,0:T(8,128)(2,1)S(1)} %get-tuple-element.145), channel_id=1, source_target_pairs={{0,1},{1,0},{2,3},{3,2},{4,5},{5,4},{6,7},{7,6},{8,9},{9,8},{10,11... | collective-permute-start | bytes 3145736 | tf_op jit(solution)/shard_map/ppermute | solution.py:561
  95.4 13.6 %collective-permute-done.16.refs_1_ = bf16[64,4096]{1,0:T(8,128)(2,1)S(1)} collective-permute-done((bf16[64,4096]{1,0:T(8,128)(2,1)S(1)}, bf16[64,4096]{1,0:T(8,128)(2,1)S(1)}, u32[]{:S(2)}, u32[]{:S(2)}) %collective-permute-start.16) | collective-permute-done | bytes 524320 | tf_op jit(solution)/shard_map/ppermute | solution.py:559
  108.9 0.6 collective-permute-done.18.refs_3_
  109.6 0.6 sum_y.1
  110.1 3.1 %collective-permute-start.22 = (bf16[32,4096]{1,0:T(8,128)(2,1)S(1)}, bf16[32,4096]{1,0:T(8,128)(2,1)S(1)}, u32[]{:S(2)}, u32[]{:S(2)}) collective-permute-start(bf16[32,4096]{1,0:T(8,128)(2,1)S(1)} %get-tuple-element.144), channel_id=1, source_target_pairs={{0,1},{1,0},{2,3},{3,2},{4,5},{5,4},{6,7},{7,6},{8,9},{9,8},{10,11... | collective-permute-start | bytes 786440 | tf_op jit(solution)/shard_map/ppermute | solution.py:564
  113.2 6.7 %collective-permute-done.23.theirs = bf16[128,4096]{1,0:T(8,128)(2,1)S(1)} collective-permute-done((bf16[128,4096]{1,0:T(8,128)(2,1)S(1)}, bf16[128,4096]{1,0:T(8,128)(2,1)S(1)}, u32[]{:S(2)}, u32[]{:S(2)}) %collective-permute-start.23) | collective-permute-done | bytes 1048608 | tf_op jit(solution)/shard_map/ppermute | solution.py:561
  119.9 0.6 sum_x.1
  120.5 0.8 collective-permute-start.24
  121.2 1.1 collective-permute-start.25
  122.3 1.7 %collective-permute-start.26 = (bf16[32,4096]{1,0:T(8,128)(2,1)S(1)}, bf16[32,4096]{1,0:T(8,128)(2,1)S(1)}, u32[]{:S(2)}, u32[]{:S(2)}) collective-permute-start(bf16[32,4096]{1,0:T(8,128)(2,1)S(1)} %get-tuple-element.150), channel_id=1, source_target_pairs={{0,6},{2,0},{4,2},{6,4},{1,7},{3,1},{5,3},{7,5},{8,14},{10,8},{12,... | collective-permute-start | bytes 786440 | tf_op jit(solution)/shard_map/ppermute | solution.py:567
  124.5 9.2 %collective-permute-done.24.refs_3_ = bf16[32,4096]{1,0:T(8,128)(2,1)S(1)} collective-permute-done((bf16[32,4096]{1,0:T(8,128)(2,1)S(1)}, bf16[32,4096]{1,0:T(8,128)(2,1)S(1)}, u32[]{:S(2)}, u32[]{:S(2)}) %collective-permute-start.24) | collective-permute-done | bytes 262176 | tf_op jit(solution)/shard_map/ppermute | solution.py:567
  133.7 0.6 collective-permute-done.26.refs_5_
  134.3 1.0 finish.1
  (31 shorter events, 2.2 us)
Async XLA Ops:
  3.2 16.5 %collective-permute-start.3 = (bf16[256,512]{1,0:T(8,128)(2,1)}, bf16[256,512]{1,0:T(8,128)(2,1)S(1)}, u32[]{:S(2)}, u32[]{:S(2)}) collective-permute-start(bf16[256,512]{1,0:T(8,128)(2,1)} %get-tuple-element.80), channel_id=1, source_target_pairs={{0,2},{2,4},{4,6},{6,0},{1,3},{3,5},{5,7},{7,1},{8,10},{10,12},{12... | collective-permute-start | bytes 786440 | tf_op jit(solution)/shard_map/ppermute | solution.py:521
  4.9 17.6 %collective-permute-start.4 = (bf16[256,512]{1,0:T(8,128)(2,1)}, bf16[256,512]{1,0:T(8,128)(2,1)S(1)}, u32[]{:S(2)}, u32[]{:S(2)}) collective-permute-start(bf16[256,512]{1,0:T(8,128)(2,1)} %get-tuple-element.81), channel_id=1, source_target_pairs={{0,4},{2,6},{4,0},{6,2},{1,5},{3,7},{5,1},{7,3},{8,12},{10,14},{12... | collective-permute-start | bytes 786440 | tf_op jit(solution)/shard_map/ppermute | solution.py:521
  7.8 14.7 %collective-permute-start.5 = (bf16[256,512]{1,0:T(8,128)(2,1)}, bf16[256,512]{1,0:T(8,128)(2,1)S(1)}, u32[]{:S(2)}, u32[]{:S(2)}) collective-permute-start(bf16[256,512]{1,0:T(8,128)(2,1)} %get-tuple-element.82), channel_id=1, source_target_pairs={{0,6},{2,0},{4,2},{6,4},{1,7},{3,1},{5,3},{7,5},{8,14},{10,8},{12,... | collective-permute-start | bytes 786440 | tf_op jit(solution)/shard_map/ppermute | solution.py:521
  9.2 13.4 %copy-start.4 = (bf16[256,512]{1,0:T(8,128)(2,1)S(1)}, bf16[256,512]{1,0:T(8,128)(2,1)}, u32[]{:S(2)}) copy-start(bf16[256,512]{1,0:T(8,128)(2,1)} %get-tuple-element.83.refs_0_) | copy-start | bytes 786436
  14.7 24.6 %collective-permute-start = (bf16[512,512]{1,0:T(8,128)(2,1)}, bf16[512,512]{1,0:T(8,128)(2,1)S(1)}, u32[]{:S(2)}, u32[]{:S(2)}) collective-permute-start(bf16[512,512]{1,0:T(8,128)(2,1)} %project_q.1.q_ref.refs_0_), channel_id=1, source_target_pairs={{0,32},{16,48},{32,0},{48,16},{1,33},{17,49},{33,1},{49,17},{2,34}... | collective-permute-start | bytes 1572872 | tf_op jit(solution)/shard_map/ppermute | solution.py:516
  18.6 22.5 %collective-permute-start.1 = (bf16[512,512]{1,0:T(8,128)(2,1)}, bf16[512,512]{1,0:T(8,128)(2,1)S(1)}, u32[]{:S(2)}, u32[]{:S(2)}) collective-permute-start(bf16[512,512]{1,0:T(8,128)(2,1)} %project_q.1.q_ref.refs_0_), channel_id=1, source_target_pairs={{0,16},{16,32},{32,48},{48,0},{1,17},{17,33},{33,49},{49,1},{2,18}... | collective-permute-start | bytes 1572872 | tf_op jit(solution)/shard_map/ppermute | solution.py:516
  19.7 22.3 %collective-permute-start.2 = (bf16[512,512]{1,0:T(8,128)(2,1)}, bf16[512,512]{1,0:T(8,128)(2,1)S(1)}, u32[]{:S(2)}, u32[]{:S(2)}) collective-permute-start(bf16[512,512]{1,0:T(8,128)(2,1)} %project_q.1.q_ref.refs_0_), channel_id=1, source_target_pairs={{0,48},{16,0},{32,16},{48,32},{1,49},{17,1},{33,17},{49,33},{2,50}... | collective-permute-start | bytes 1572872 | tf_op jit(solution)/shard_map/ppermute | solution.py:516
  23.4 18.5 %collective-permute-start.6 = (bf16[512,512]{1,0:T(8,128)(2,1)S(1)}, bf16[512,512]{1,0:T(8,128)(2,1)S(1)}, u32[]{:S(2)}, u32[]{:S(2)}) collective-permute-start(bf16[512,512]{1,0:T(8,128)(2,1)S(1)} %get-tuple-element.101.refs_3_.refs_1_), channel_id=1, source_target_pairs={{0,64},{64,0},{1,65},{65,1},{2,66},{66,2},{3,67},{67,3},{4,68},{68... | collective-permute-start | bytes 1572872 | tf_op jit(solution)/shard_map/ppermute | solution.py:528
  24.9 10.4 %copy-start = (bf16[512,512]{1,0:T(8,128)(2,1)S(1)}, bf16[512,512]{1,0:T(8,128)(2,1)}, u32[]{:S(2)}) copy-start(bf16[512,512]{1,0:T(8,128)(2,1)} %project_q.1.q_ref.refs_0_) | copy-start | bytes 1572868
  24.9 17.0 %collective-permute-start.7 = (bf16[512,512]{1,0:T(8,128)(2,1)}, bf16[512,512]{1,0:T(8,128)(2,1)S(1)}, u32[]{:S(2)}, u32[]{:S(2)}) collective-permute-start(bf16[512,512]{1,0:T(8,128)(2,1)} %get-tuple-element.95), channel_id=1, source_target_pairs={{0,65},{65,0},{1,64},{64,1},{2,67},{67,2},{3,66},{66,3},{4,69},{69... | collective-permute-start | bytes 1572872 | tf_op jit(solution)/shard_map/ppermute | solution.py:529
  35.3 1.0 copy-start.2
  36.4 1.0 copy-start.3
  42.0 2.1 %collective-permute-start.11 = (bf16[512,512]{1,0:T(8,128)(2,1)S(1)}, bf16[512,512]{1,0:T(8,128)(2,1)S(1)}, u32[]{:S(2)}, u32[]{:S(2)}) collective-permute-start(bf16[512,512]{1,0:T(8,128)(2,1)S(1)} %get-tuple-element.101.refs_3_.refs_1_), channel_id=1, source_target_pairs={{0,8},{8,0},{1,9},{9,1},{2,10},{10,2},{3,11},{11,3},{4,12},{12,4},... | collective-permute-start | bytes 1572872 | tf_op jit(solution)/shard_map/ppermute | solution.py:513
  42.0 6.2 %collective-permute-start.10 = (bf16[512,512]{1,0:T(8,128)(2,1)S(1)}, bf16[512,512]{1,0:T(8,128)(2,1)S(1)}, u32[]{:S(2)}, u32[]{:S(2)}) collective-permute-start(bf16[512,512]{1,0:T(8,128)(2,1)S(1)} %collective-permute-done.7.refs_4_), channel_id=1, source_target_pairs={{0,8},{8,0},{1,9},{9,1},{2,10},{10,2},{3,11},{11,3},{4,12},{12,4},... | collective-permute-start | bytes 1572872 | tf_op jit(solution)/shard_map/ppermute | solution.py:513
  42.5 5.7 %collective-permute-start.9 = (bf16[512,512]{1,0:T(8,128)(2,1)S(1)}, bf16[512,512]{1,0:T(8,128)(2,1)S(1)}, u32[]{:S(2)}, u32[]{:S(2)}) collective-permute-start(bf16[512,512]{1,0:T(8,128)(2,1)S(1)} %collective-permute-done.6.refs_3_), channel_id=1, source_target_pairs={{0,8},{8,0},{1,9},{9,1},{2,10},{10,2},{3,11},{11,3},{4,12},{12,4},... | collective-permute-start | bytes 1572872 | tf_op jit(solution)/shard_map/ppermute | solution.py:513
  42.6 14.3 %collective-permute-start.8 = (bf16[512,512]{1,0:T(8,128)(2,1)S(1)}, bf16[512,512]{1,0:T(8,128)(2,1)S(1)}, u32[]{:S(2)}, u32[]{:S(2)}) collective-permute-start(bf16[512,512]{1,0:T(8,128)(2,1)S(1)} %collective-permute-done.7.refs_4_), channel_id=1, source_target_pairs={{0,64},{64,0},{1,65},{65,1},{2,66},{66,2},{3,67},{67,3},{4,68},{68... | collective-permute-start | bytes 1572872 | tf_op jit(solution)/shard_map/ppermute | solution.py:537
  56.8 1.9 %collective-permute-start.12 = (bf16[512,512]{1,0:T(8,128)(2,1)S(1)}, bf16[512,512]{1,0:T(8,128)(2,1)S(1)}, u32[]{:S(2)}, u32[]{:S(2)}) collective-permute-start(bf16[512,512]{1,0:T(8,128)(2,1)S(1)} %collective-permute-done.8.refs_3_.refs_7_), channel_id=1, source_target_pairs={{0,8},{8,0},{1,9},{9,1},{2,10},{10,2},{3,11},{11,3},{4,12},{12,4},... | collective-permute-start | bytes 1572872 | tf_op jit(solution)/shard_map/ppermute | solution.py:513
  61.1 11.1 %collective-permute-start.13 = (bf16[272,512]{1,0:T(8,128)(2,1)S(1)}, bf16[272,512]{1,0:T(8,128)(2,1)S(1)}, u32[]{:S(2)}, u32[]{:S(2)}) collective-permute-start(bf16[272,512]{1,0:T(8,128)(2,1)S(1)} %get-tuple-element.115), channel_id=1, source_target_pairs={{0,32},{16,48},{32,0},{48,16},{1,33},{17,49},{33,1},{49,17},{2,34}... | collective-permute-start | bytes 835592 | tf_op jit(solution)/shard_map/ppermute | solution.py:516
  63.2 15.5 %collective-permute-start.14 = (bf16[272,512]{1,0:T(8,128)(2,1)S(1)}, bf16[272,512]{1,0:T(8,128)(2,1)S(1)}, u32[]{:S(2)}, u32[]{:S(2)}) collective-permute-start(bf16[272,512]{1,0:T(8,128)(2,1)S(1)} %get-tuple-element.116), channel_id=1, source_target_pairs={{0,48},{16,0},{32,16},{48,32},{1,49},{17,1},{33,17},{49,33},{2,50}... | collective-permute-start | bytes 835592 | tf_op jit(solution)/shard_map/ppermute | solution.py:516
  64.8 13.9 %collective-permute-start.15 = (bf16[272,512]{1,0:T(8,128)(2,1)S(1)}, bf16[272,512]{1,0:T(8,128)(2,1)S(1)}, u32[]{:S(2)}, u32[]{:S(2)}) collective-permute-start(bf16[272,512]{1,0:T(8,128)(2,1)S(1)} %get-tuple-element.117), channel_id=1, source_target_pairs={{0,16},{16,32},{32,48},{48,0},{1,17},{17,33},{33,49},{49,1},{2,18}... | collective-permute-start | bytes 835592 | tf_op jit(solution)/shard_map/ppermute | solution.py:516
  67.6 17.5 %collective-permute-start.19 = (bf16[272,512]{1,0:T(8,128)(2,1)S(1)}, bf16[272,512]{1,0:T(8,128)(2,1)S(1)}, u32[]{:S(2)}, u32[]{:S(2)}) collective-permute-start(bf16[272,512]{1,0:T(8,128)(2,1)S(1)} %get-tuple-element.120), channel_id=1, source_target_pairs={{0,32},{16,48},{32,0},{48,16},{1,33},{17,49},{33,1},{49,17},{2,34}... | collective-permute-start | bytes 835592 | tf_op jit(solution)/shard_map/ppermute | solution.py:516
  69.4 19.9 %collective-permute-start.20 = (bf16[272,512]{1,0:T(8,128)(2,1)S(1)}, bf16[272,512]{1,0:T(8,128)(2,1)S(1)}, u32[]{:S(2)}, u32[]{:S(2)}) collective-permute-start(bf16[272,512]{1,0:T(8,128)(2,1)S(1)} %get-tuple-element.132), channel_id=1, source_target_pairs={{0,48},{16,0},{32,16},{48,32},{1,49},{17,1},{33,17},{49,33},{2,50}... | collective-permute-start | bytes 835592 | tf_op jit(solution)/shard_map/ppermute | solution.py:516
  72.2 17.1 %collective-permute-start.21 = (bf16[272,512]{1,0:T(8,128)(2,1)S(1)}, bf16[272,512]{1,0:T(8,128)(2,1)S(1)}, u32[]{:S(2)}, u32[]{:S(2)}) collective-permute-start(bf16[272,512]{1,0:T(8,128)(2,1)S(1)} %get-tuple-element.133), channel_id=1, source_target_pairs={{0,16},{16,32},{32,48},{48,0},{1,17},{17,33},{33,49},{49,1},{2,18}... | collective-permute-start | bytes 835592 | tf_op jit(solution)/shard_map/ppermute | solution.py:516
  73.2 5.5 %copy-start.1 = (bf16[512,4096]{1,0:T(8,128)(2,1)S(1)}, bf16[512,4096]{1,0:T(8,128)(2,1)}, u32[]{:S(2)}) copy-start(bf16[512,4096]{1,0:T(8,128)(2,1)} %refs_4_.4) | copy-start | bytes 12582916
  83.3 25.6 %collective-permute-start.16 = (bf16[64,4096]{1,0:T(8,128)(2,1)S(1)}, bf16[64,4096]{1,0:T(8,128)(2,1)S(1)}, u32[]{:S(2)}, u32[]{:S(2)}) collective-permute-start(bf16[64,4096]{1,0:T(8,128)(2,1)S(1)} %get-tuple-element.129), channel_id=1, source_target_pairs={{0,2},{2,4},{4,6},{6,0},{1,3},{3,5},{5,7},{7,1},{8,10},{10,12},{12... | collective-permute-start | bytes 1572872 | tf_op jit(solution)/shard_map/ppermute | solution.py:559
  84.1 24.9 %collective-permute-start.17 = (bf16[64,4096]{1,0:T(8,128)(2,1)S(1)}, bf16[64,4096]{1,0:T(8,128)(2,1)S(1)}, u32[]{:S(2)}, u32[]{:S(2)}) collective-permute-start(bf16[64,4096]{1,0:T(8,128)(2,1)S(1)} %get-tuple-element.130), channel_id=1, source_target_pairs={{0,4},{2,6},{4,0},{6,2},{1,5},{3,7},{5,1},{7,3},{8,12},{10,14},{12... | collective-permute-start | bytes 1572872 | tf_op jit(solution)/shard_map/ppermute | solution.py:559
  85.2 24.4 %collective-permute-start.18 = (bf16[64,4096]{1,0:T(8,128)(2,1)S(1)}, bf16[64,4096]{1,0:T(8,128)(2,1)S(1)}, u32[]{:S(2)}, u32[]{:S(2)}) collective-permute-start(bf16[64,4096]{1,0:T(8,128)(2,1)S(1)} %get-tuple-element.131), channel_id=1, source_target_pairs={{0,6},{2,0},{4,2},{6,4},{1,7},{3,1},{5,3},{7,5},{8,14},{10,8},{12,... | collective-permute-start | bytes 1572872 | tf_op jit(solution)/shard_map/ppermute | solution.py:559
  92.3 27.6 %collective-permute-start.23 = (bf16[128,4096]{1,0:T(8,128)(2,1)S(1)}, bf16[128,4096]{1,0:T(8,128)(2,1)S(1)}, u32[]{:S(2)}, u32[]{:S(2)}) collective-permute-start(bf16[128,4096]{1,0:T(8,128)(2,1)S(1)} %get-tuple-element.145), channel_id=1, source_target_pairs={{0,1},{1,0},{2,3},{3,2},{4,5},{5,4},{6,7},{7,6},{8,9},{9,8},{10,11... | collective-permute-start | bytes 3145736 | tf_op jit(solution)/shard_map/ppermute | solution.py:561
  110.1 14.4 %collective-permute-start.22 = (bf16[32,4096]{1,0:T(8,128)(2,1)S(1)}, bf16[32,4096]{1,0:T(8,128)(2,1)S(1)}, u32[]{:S(2)}, u32[]{:S(2)}) collective-permute-start(bf16[32,4096]{1,0:T(8,128)(2,1)S(1)} %get-tuple-element.144), channel_id=1, source_target_pairs={{0,1},{1,0},{2,3},{3,2},{4,5},{5,4},{6,7},{7,6},{8,9},{9,8},{10,11... | collective-permute-start | bytes 786440 | tf_op jit(solution)/shard_map/ppermute | solution.py:564
  120.5 13.2 %collective-permute-start.24 = (bf16[32,4096]{1,0:T(8,128)(2,1)S(1)}, bf16[32,4096]{1,0:T(8,128)(2,1)S(1)}, u32[]{:S(2)}, u32[]{:S(2)}) collective-permute-start(bf16[32,4096]{1,0:T(8,128)(2,1)S(1)} %get-tuple-element.148), channel_id=1, source_target_pairs={{0,2},{2,4},{4,6},{6,0},{1,3},{3,5},{5,7},{7,1},{8,10},{10,12},{12... | collective-permute-start | bytes 786440 | tf_op jit(solution)/shard_map/ppermute | solution.py:567
  121.2 12.5 %collective-permute-start.25 = (bf16[32,4096]{1,0:T(8,128)(2,1)S(1)}, bf16[32,4096]{1,0:T(8,128)(2,1)S(1)}, u32[]{:S(2)}, u32[]{:S(2)}) collective-permute-start(bf16[32,4096]{1,0:T(8,128)(2,1)S(1)} %get-tuple-element.149), channel_id=1, source_target_pairs={{0,4},{2,6},{4,0},{6,2},{1,5},{3,7},{5,1},{7,3},{8,12},{10,14},{12... | collective-permute-start | bytes 786440 | tf_op jit(solution)/shard_map/ppermute | solution.py:567
  122.3 12.0 %collective-permute-start.26 = (bf16[32,4096]{1,0:T(8,128)(2,1)S(1)}, bf16[32,4096]{1,0:T(8,128)(2,1)S(1)}, u32[]{:S(2)}, u32[]{:S(2)}) collective-permute-start(bf16[32,4096]{1,0:T(8,128)(2,1)S(1)} %get-tuple-element.150), channel_id=1, source_target_pairs={{0,6},{2,0},{4,2},{6,4},{1,7},{3,1},{5,3},{7,5},{8,14},{10,8},{12,... | collective-permute-start | bytes 786440 | tf_op jit(solution)/shard_map/ppermute | solution.py:567

commit v4 on v3

--- a/solution.py
+++ b/solution.py
@@ -522,36 +522,44 @@
 
     (hidden,) = in_order([hidden], sent[0])
     (q,) = project("q", hidden, [w_query], tables)
-    q2, q1, q3 = [along_z(q, by) for by in (2, 1, -1)]
+    q1, q3, q2 = [along_z(q, by) for by in (1, -1, 2)]
     got = in_order(got, q)
     near, far = pack(got)
     near_x = lax.ppermute(near, "xlo", shift(2, 1))
     far_x = lax.ppermute(far, ("xlo", "xhi"), [(0, 3), (3, 0), (1, 2), (2, 1)])
     (hidden,) = in_order([hidden], near)
     k_suffix, v_suffix = project("kv", hidden, [w_key, w_value], tables)
-    begun = suffix_attention(suffix_len, q, k_suffix, v_suffix)
-    queries = in_order([q2, q1, q3], begun[0])
-    near_c = core(in_order([near], *queries)[0])
-
-    near_x, far_x = in_order([near_x, far_x], begun[0])
+    q1, q3 = in_order([q1, q3], k_suffix)
+    near_c = core(in_order([near], q1, q3)[0])
+
+    near_x, far_x = in_order([near_x, far_x], k_suffix)
     far_xx = lax.ppermute(far_x, "xlo", shift(2, 1))
     middle = [near_x, far_x, core(near_x), core(far_x)]
-    states = prefix_attention(
+    state1, state3 = prefix_attention(
         "attend_near",
-        in_order(queries, near_x, far_x),
+        in_order([q1, q3], near_x, far_x),
         [near, near_c],
-        [2] * 3,
-        [None] * 3,
+        [2] * 2,
+        [None] * 2,
         cost=NEAR_COST,
     )
-    states = prefix_attention("attend_middle", queries, middle, [4] * 3, states)
-    (far_xx,) = in_order([far_xx], states[0][0])
+    state1, state3 = prefix_attention(
+        "attend_middle", [q1, q3], middle, [4] * 2, [state1, state3]
+    )
+    (q2,) = in_order([q2], state1[0])
+    (state2,) = prefix_attention(
+        "attend_two", [q2], [near, near_c, *middle], [6], [None]
+    )
+    queries, states = [q2, q1, q3], [state2, state1, state3]
+    (far_xx,) = in_order([far_xx], state2[0])
     final = [far_xx, core(far_xx)]
     sums = []
     for half in range(2):
         sent = prefix_attention("attend_last", queries, final, [2] * 3, states, [half])
         sums.append([along_z(m, back) for m, back in zip(sent, [2, -1, 1])])
         final = in_order(final, sent[0])
+    (k_suffix,) = in_order([k_suffix], final[0])
+    begun = suffix_attention(suffix_len, q, k_suffix, v_suffix)
     every = [near, near_c, *middle, *final]
     own = prefix_attention("attend_own", [q], every, [8], [begun], [0, 1])
     cut = output_half(suffix_len, 0, in_order(sums[0], own[0]) + [own[0]], w_output)

time: 136 us -> 131 us (0.963)
  local copies, waits for them, and re-layouts: 2.09 us -> 0.02 us
  waiting for transfers between devices: 38.9 us -> 37 us
    ppermute x9, waiting for transfers between devices: 5.38 us -> 2.56 us  [along_z(): return lax.ppermute(x, 'z', shift(4, by))]
    ppermute x3, waiting for transfers between devices: 9.83 us -> 7.23 us  [body(): lax.ppermute(lower[d], 'y', shift(4, d))]
    ppermute x1, starting transfers between devices: 3.1 us -> 0.79 us  [body(): theirs = lax.ppermute(theirs, 'xhi', shift(2, 1))]
    unnamed x10, local copies, waits for them, and re-layouts: 2.09 us -> 0.02 us
    ppermute x3, starting transfers between devices: 3.51 us -> 5.53 us  [body(): cut = [cut[0]] + [lax.ppermute(cut[d], 'y', shift(4, d)) for d in (1, 2, 3)]]
    ppermute x3, waiting for transfers between devices: 14.2 us -> 16.2 us  [body(): cut = [cut[0]] + [lax.ppermute(cut[d], 'y', shift(4, d)) for d in (1, 2, 3)]]
    ppermute x1, starting transfers between devices: 3.1 us -> 1.26 us  [body(): upper = [upper_ours, lax.ppermute(upper_theirs, 'xhi', shift(2, 1))]]
    ppermute x1, waiting for transfers between devices: 6.66 us -> 8.39 us  [body(): theirs = lax.ppermute(theirs, 'xhi', shift(2, 1))]
  transfers between devices with their start and end apart: 27 -> 27, of which waited for: 12 -> 8; matrix products, arithmetic and copies ran while one was open for 0% -> 0% of each run, Pallas kernels for 34% -> 35%
where the time goes in v4:
time: 131 us
  Pallas kernels  52.3 us (40%)
  starting transfers between devices  40.8 us (31%)
  waiting for transfers between devices  37 us (28%)
    pallas_call x6, Pallas kernels, prefix_attention(): call(functools.partial(prefix_kernel, nq, nkv, used, held, halves), name,...  23.8 us
    ppermute x9, starting transfers between devices, along_z(): return lax.ppermute(x, 'z', shift(4, by))  18.2 us
    ppermute x3, waiting for transfers between devices, body(): cut = [cut[0]] + [lax.ppermute(cut[d], 'y', shift(4, d)) for d in (1, 2, 3)]  16.2 us
    pallas_call x2, Pallas kernels, project(): call(functools.partial(project_kernel, kinds, LOG2E / math.sqrt(HD)), 'pr...  13.8 us
    ppermute x1, waiting for transfers between devices, body(): theirs = lax.ppermute(theirs, 'xhi', shift(2, 1))  8.39 us
    pallas_call x2, Pallas kernels, output_half(): call(functools.partial(output_kernel, n, half), 'output_half', flops=1 +...  7.54 us
    ppermute x3, waiting for transfers between devices, body(): lax.ppermute(lower[d], 'y', shift(4, d))  7.23 us
    ppermute x3, starting transfers between devices, body(): lax.ppermute(sent[d], 'y', shift(4, d))  5.98 us
  transfers between devices with their start and end apart: 27, of which 8 were waited for; matrix products, arithmetic and copies ran while one was open for 0% of the time, Pallas kernels for 35%

profile of v4, /device:TPU:0, one launch (start us, length us, event | category | flops | bytes accessed | tf_op | source)
XLA Modules:
  0.0 131.1 jit_solution(10806321155469400231)
XLA Ops:
  0.0 3.2 %prepare.1 = (bf16[256,512]{1,0:T(8,128)(2,1)}, bf16[256,512]{1,0:T(8,128)(2,1)}, bf16[256,512]{1,0:T(8,128)(2,1)}, bf16[256,512]{1,0:T(8,128)(2,1)}) custom-call(s32[4,128]{1,0:T(4,128)} %bitcast.5, f32[1,128]{1,0:T(1,128)} %constant.8.clone.freq, bf16[64,4096]{1,0:T(8,128)(2,1)} %bitcast.3, bf16[64,4096]{1,0:T(8,128)(2,1)} %bitcast.4), custom_call_target="tpu_custom_call" | custom-call | flops 1 | bytes 1 | tf_op jit(solution)/shard_map/prepare/pallas_call | solution.py:120
  3.2 1.7 %collective-permute-start.3 = (bf16[256,512]{1,0:T(8,128)(2,1)}, bf16[256,512]{1,0:T(8,128)(2,1)S(1)}, u32[]{:S(2)}, u32[]{:S(2)}) collective-permute-start(bf16[256,512]{1,0:T(8,128)(2,1)} %get-tuple-element.78), channel_id=1, source_target_pairs={{0,2},{2,4},{4,6},{6,0},{1,3},{3,5},{5,7},{7,1},{8,10},{10,12},{12... | collective-permute-start | bytes 786440 | tf_op jit(solution)/shard_map/ppermute | solution.py:521
  4.9 2.9 %collective-permute-start.4 = (bf16[256,512]{1,0:T(8,128)(2,1)}, bf16[256,512]{1,0:T(8,128)(2,1)S(1)}, u32[]{:S(2)}, u32[]{:S(2)}) collective-permute-start(bf16[256,512]{1,0:T(8,128)(2,1)} %get-tuple-element.79), channel_id=1, source_target_pairs={{0,4},{2,6},{4,0},{6,2},{1,5},{3,7},{5,1},{7,3},{8,12},{10,14},{12... | collective-permute-start | bytes 786440 | tf_op jit(solution)/shard_map/ppermute | solution.py:521
  7.8 1.3 %collective-permute-start.5 = (bf16[256,512]{1,0:T(8,128)(2,1)}, bf16[256,512]{1,0:T(8,128)(2,1)S(1)}, u32[]{:S(2)}, u32[]{:S(2)}) collective-permute-start(bf16[256,512]{1,0:T(8,128)(2,1)} %get-tuple-element.80), channel_id=1, source_target_pairs={{0,6},{2,0},{4,2},{6,4},{1,7},{3,1},{5,3},{7,5},{8,14},{10,8},{12,... | collective-permute-start | bytes 786440 | tf_op jit(solution)/shard_map/ppermute | solution.py:521
  9.2 5.5 %project_q.1.q_ref.refs_0_ = bf16[512,512]{1,0:T(8,128)(2,1)} custom-call(bf16[512,4096]{1,0:T(8,128)(2,1)} %refs_0_.1, bf16[4096,512]{1,0:T(8,128)(2,1)} %refs_1_.2, f32[512,128]{1,0:T(8,128)} %constant.6.clone.refs_2_.refs_3_, f32[512,128]{1,0:T(8,128)} %constant.7.clone.refs_3_.refs_4_), custom_call_target="tpu_custom_call" | custom-call | flops 1 | bytes 1 | tf_op jit(solution)/shard_map/project_q/pallas_call | solution.py:190
  14.7 2.0 %collective-permute-start.1 = (bf16[512,512]{1,0:T(8,128)(2,1)}, bf16[512,512]{1,0:T(8,128)(2,1)S(1)}, u32[]{:S(2)}, u32[]{:S(2)}) collective-permute-start(bf16[512,512]{1,0:T(8,128)(2,1)} %project_q.1.q_ref.refs_0_), channel_id=1, source_target_pairs={{0,16},{16,32},{32,48},{48,0},{1,17},{17,33},{33,49},{49,1},{2,18}... | collective-permute-start | bytes 1572872 | tf_op jit(solution)/shard_map/ppermute | solution.py:516
  16.7 2.2 %collective-permute-start.2 = (bf16[512,512]{1,0:T(8,128)(2,1)}, bf16[512,512]{1,0:T(8,128)(2,1)S(1)}, u32[]{:S(2)}, u32[]{:S(2)}) collective-permute-start(bf16[512,512]{1,0:T(8,128)(2,1)} %project_q.1.q_ref.refs_0_), channel_id=1, source_target_pairs={{0,48},{16,0},{32,16},{48,32},{1,49},{17,1},{33,17},{49,33},{2,50}... | collective-permute-start | bytes 1572872 | tf_op jit(solution)/shard_map/ppermute | solution.py:516
  18.9 0.8 collective-permute-done.4.refs_2_
  19.8 1.6 %collective-permute-start.6 = (bf16[512,512]{1,0:T(8,128)(2,1)S(1)}, bf16[512,512]{1,0:T(8,128)(2,1)S(1)}, u32[]{:S(2)}, u32[]{:S(2)}) collective-permute-start(bf16[512,512]{1,0:T(8,128)(2,1)S(1)} %get-tuple-element.95.refs_2_.refs_1_), channel_id=1, source_target_pairs={{0,64},{64,0},{1,65},{65,1},{2,66},{66,2},{3,67},{67,3},{4,68},{68... | collective-permute-start | bytes 1572872 | tf_op jit(solution)/shard_map/ppermute | solution.py:528
  21.3 2.1 %collective-permute-start.7 = (bf16[512,512]{1,0:T(8,128)(2,1)S(1)}, bf16[512,512]{1,0:T(8,128)(2,1)S(1)}, u32[]{:S(2)}, u32[]{:S(2)}) collective-permute-start(bf16[512,512]{1,0:T(8,128)(2,1)S(1)} %get-tuple-element.90), channel_id=1, source_target_pairs={{0,65},{65,0},{1,64},{64,1},{2,67},{67,2},{3,66},{66,3},{4,69},{69... | collective-permute-start | bytes 1572872 | tf_op jit(solution)/shard_map/ppermute | solution.py:529
  23.4 8.3 %project_kv.1 = (bf16[512,512]{1,0:T(8,128)(2,1)}, bf16[512,512]{1,0:T(8,128)(2,1)}) custom-call(bf16[512,4096]{1,0:T(8,128)(2,1)} %refs_0_.1, bf16[4096,512]{1,0:T(8,128)(2,1)} %refs_1_.3, bf16[4096,512]{1,0:T(8,128)(2,1)} %refs_2_.2, f32[512,128]{1,0:T(8,128)} %constant.6.clone.refs_2_.refs_3_, f32[512,128]{1,0:T(8,128)} %constant.7.clone.refs_3_.refs_4_), custom_call_target="tpu_custom_call" | custom-call | flops 1 | bytes 1 | tf_op jit(solution)/shard_map/project_kv/pallas_call | solution.py:190
  31.8 3.9 %collective-permute-start = (bf16[512,512]{1,0:T(8,128)(2,1)S(1)}, bf16[512,512]{1,0:T(8,128)(2,1)S(1)}, u32[]{:S(2)}, u32[]{:S(2)}) collective-permute-start(bf16[512,512]{1,0:T(8,128)(2,1)S(1)} %copy-done), channel_id=1, source_target_pairs={{0,32},{16,48},{32,0},{48,16},{1,33},{17,49},{33,1},{49,17},{2,34}... | collective-permute-start | bytes 1572872 | tf_op jit(solution)/shard_map/ppermute | solution.py:516
  35.8 0.2 collective-permute-start.8
  35.9 0.4 collective-permute-start.9
  36.3 0.6 collective-permute-start.11
  36.9 3.0 %attend_near.1 = (f32[512,1024]{1,0:T(8,128)S(1)}, f32[512,512]{1,0:T(8,128)S(1)}, f32[512,1024]{1,0:T(8,128)S(1)}, f32[512,512]{1,0:T(8,128)S(1)}) custom-call(bf16[512,512]{1,0:T(8,128)(2,1)S(1)} %collective-permute-done.1.refs_0_.refs_1_, bf16[512,512]{1,0:T(8,128)(2,1)S(1)} %collective-permute-done.2.refs_1_.refs_2_, ...), custom_call_target="tpu_custom_call" | custom-call | flops 10000000000 | bytes 1 | tf_op jit(solution)/shard_map/attend_near/pallas_call | solution.py:348
  39.9 5.8 %attend_middle.1 = (f32[512,1024]{1,0:T(8,128)S(1)}, f32[512,512]{1,0:T(8,128)S(1)}, f32[512,1024]{1,0:T(8,128)S(1)}, f32[512,512]{1,0:T(8,128)S(1)}) custom-call(bf16[512,512]{1,0:T(8,128)(2,1)S(1)} %collective-permute-done.1.refs_0_.refs_1_, bf16[512,512]{1,0:T(8,128)(2,1)S(1)} %collective-permute-done.2.refs_1_.refs_2_, ...), custom_call_target="tpu_custom_call" | custom-call | flops 1 | bytes 1 | tf_op jit(solution)/shard_map/attend_middle/pallas_call | solution.py:348
  45.7 2.5 %collective-permute-done.refs_0_ = bf16[512,512]{1,0:T(8,128)(2,1)S(1)} collective-permute-done((bf16[512,512]{1,0:T(8,128)(2,1)S(1)}, bf16[512,512]{1,0:T(8,128)(2,1)S(1)}, u32[]{:S(2)}, u32[]{:S(2)}) %collective-permute-start) | collective-permute-done | bytes 524320 | tf_op jit(solution)/shard_map/ppermute | solution.py:516
  48.3 4.7 %attend_two.1 = (f32[512,1024]{1,0:T(8,128)S(1)}, f32[512,512]{1,0:T(8,128)S(1)}) custom-call(bf16[512,512]{1,0:T(8,128)(2,1)S(1)} %collective-permute-done.refs_0_, bf16[512,512]{1,0:T(8,128)(2,1)S(1)} %get-tuple-element.95.refs_2_.refs_1_, bf16[512,512]{1,0:T(8,128)(2,1)S(1)} %collective-permute-done.10.refs_3_.refs_2_, ...), custom_call_target="tpu_custom_call" | custom-call | flops 1 | bytes 1 | tf_op jit(solution)/shard_map/attend_two/pallas_call | solution.py:348
  53.1 1.9 %collective-permute-done.12.refs_4_.refs_8_ = bf16[512,512]{1,0:T(8,128)(2,1)S(1)} collective-permute-done((bf16[512,512]{1,0:T(8,128)(2,1)S(1)}, bf16[512,512]{1,0:T(8,128)(2,1)S(1)}, u32[]{:S(2)}, u32[]{:S(2)}) %collective-permute-start.12) | collective-permute-done | bytes 524320 | tf_op jit(solution)/shard_map/ppermute | solution.py:513
  55.0 2.4 %attend_last.2 = (bf16[272,512]{1,0:T(8,128)(2,1)S(1)}, bf16[272,512]{1,0:T(8,128)(2,1)S(1)}, bf16[272,512]{1,0:T(8,128)(2,1)S(1)}) custom-call(bf16[512,512]{1,0:T(8,128)(2,1)S(1)} %collective-permute-done.refs_0_, bf16[512,512]{1,0:T(8,128)(2,1)S(1)} %collective-permute-done.1.refs_0_.refs_1_, bf16[512,512]{1,0:T(8,128)(2,1)S(1)} %collective-permute-done.2.refs_1_.refs_2_, ...), custom_call_target="tpu_custom_call" | custom-call | flops 1 | bytes 1 | tf_op jit(solution)/shard_map/attend_last/pallas_call | solution.py:348
  57.4 3.3 %collective-permute-start.13 = (bf16[272,512]{1,0:T(8,128)(2,1)S(1)}, bf16[272,512]{1,0:T(8,128)(2,1)S(1)}, u32[]{:S(2)}, u32[]{:S(2)}) collective-permute-start(bf16[272,512]{1,0:T(8,128)(2,1)S(1)} %get-tuple-element.108), channel_id=1, source_target_pairs={{0,32},{16,48},{32,0},{48,16},{1,33},{17,49},{33,1},{49,17},{2,34}... | collective-permute-start | bytes 835592 | tf_op jit(solution)/shard_map/ppermute | solution.py:516
  60.7 0.7 collective-permute-start.14
  61.4 1.3 %collective-permute-start.15 = (bf16[272,512]{1,0:T(8,128)(2,1)S(1)}, bf16[272,512]{1,0:T(8,128)(2,1)S(1)}, u32[]{:S(2)}, u32[]{:S(2)}) collective-permute-start(bf16[272,512]{1,0:T(8,128)(2,1)S(1)} %get-tuple-element.110), channel_id=1, source_target_pairs={{0,16},{16,32},{32,48},{48,0},{1,17},{17,33},{33,49},{49,1},{2,18}... | collective-permute-start | bytes 835592 | tf_op jit(solution)/shard_map/ppermute | solution.py:516
  62.7 2.4 %attend_last.3 = (bf16[272,512]{1,0:T(8,128)(2,1)S(1)}, bf16[272,512]{1,0:T(8,128)(2,1)S(1)}, bf16[272,512]{1,0:T(8,128)(2,1)S(1)}) custom-call(bf16[512,512]{1,0:T(8,128)(2,1)S(1)} %collective-permute-done.refs_0_, bf16[512,512]{1,0:T(8,128)(2,1)S(1)} %collective-permute-done.1.refs_0_.refs_1_, bf16[512,512]{1,0:T(8,128)(2,1)S(1)} %collective-permute-done.2.refs_1_.refs_2_, ...), custom_call_target="tpu_custom_call" | custom-call | flops 1 | bytes 1 | tf_op jit(solution)/shard_map/attend_last/pallas_call | solution.py:348
  65.1 1.1 collective-permute-start.19
  66.2 2.6 %collective-permute-start.20 = (bf16[272,512]{1,0:T(8,128)(2,1)S(1)}, bf16[272,512]{1,0:T(8,128)(2,1)S(1)}, u32[]{:S(2)}, u32[]{:S(2)}) collective-permute-start(bf16[272,512]{1,0:T(8,128)(2,1)S(1)} %get-tuple-element.128), channel_id=1, source_target_pairs={{0,48},{16,0},{32,16},{48,32},{1,49},{17,1},{33,17},{49,33},{2,50}... | collective-permute-start | bytes 835592 | tf_op jit(solution)/shard_map/ppermute | solution.py:516
  68.9 0.9 collective-permute-start.21
  70.5 1.8 %suffix_attention.1 = (f32[512,1024]{1,0:T(8,128)S(1)}, f32[512,512]{1,0:T(8,128)S(1)}) custom-call(s32[1]{0:T(128)S(6)} %copy.13.length, bf16[512,512]{1,0:T(8,128)(2,1)S(1)} %copy-done, bf16[512,512]{1,0:T(8,128)(2,1)S(1)} %copy-done.2, bf16[512,512]{1,0:T(8,128)(2,1)S(1)} %copy-done.3), custom_call_target="tpu_custom_call" | custom-call | flops 1 | bytes 1 | tf_op jit(solution)/shard_map/suffix_attention/pallas_call | solution.py:258
  72.3 5.5 %attend_own.1 = (bf16[272,512]{1,0:T(8,128)(2,1)S(1)}, bf16[272,512]{1,0:T(8,128)(2,1)S(1)}) custom-call(bf16[512,512]{1,0:T(8,128)(2,1)S(1)} %copy-done, bf16[512,512]{1,0:T(8,128)(2,1)S(1)} %get-tuple-element.95.refs_2_.refs_1_, bf16[512,512]{1,0:T(8,128)(2,1)S(1)} %collective-permute-done.10.refs_3_.refs_2_, ...), custom_call_target="tpu_custom_call" | custom-call | flops 1 | bytes 1 | tf_op jit(solution)/shard_map/attend_own/pallas_call | solution.py:348
  77.8 4.6 %output_half.2 = (bf16[64,4096]{1,0:T(8,128)(2,1)S(1)}, bf16[64,4096]{1,0:T(8,128)(2,1)S(1)}, bf16[64,4096]{1,0:T(8,128)(2,1)S(1)}, bf16[64,4096]{1,0:T(8,128)(2,1)S(1)}) custom-call(s32[1]{0:T(128)S(6)} %copy.13.length, bf16[272,512]{1,0:T(8,128)(2,1)S(1)} %collective-permute-done.13.refs_0_, bf16[272,512]{1,0:T(8,128)(2,1)S(1)} %collective-permute-done.14.refs_1_, ...), custom_call_target="tpu_custom_call" | custom-call | flops 1 | bytes 1 | tf_op jit(solution)/shard_map/output_half/pallas_call | solution.py:416
  82.4 1.6 %collective-permute-start.16 = (bf16[64,4096]{1,0:T(8,128)(2,1)S(1)}, bf16[64,4096]{1,0:T(8,128)(2,1)S(1)}, u32[]{:S(2)}, u32[]{:S(2)}) collective-permute-start(bf16[64,4096]{1,0:T(8,128)(2,1)S(1)} %get-tuple-element.125), channel_id=1, source_target_pairs={{0,2},{2,4},{4,6},{6,0},{1,3},{3,5},{5,7},{7,1},{8,10},{10,12},{12... | collective-permute-start | bytes 1572872 | tf_op jit(solution)/shard_map/ppermute | solution.py:567
  84.0 2.4 %collective-permute-start.17 = (bf16[64,4096]{1,0:T(8,128)(2,1)S(1)}, bf16[64,4096]{1,0:T(8,128)(2,1)S(1)}, u32[]{:S(2)}, u32[]{:S(2)}) collective-permute-start(bf16[64,4096]{1,0:T(8,128)(2,1)S(1)} %get-tuple-element.126), channel_id=1, source_target_pairs={{0,4},{2,6},{4,0},{6,2},{1,5},{3,7},{5,1},{7,3},{8,12},{10,14},{12... | collective-permute-start | bytes 1572872 | tf_op jit(solution)/shard_map/ppermute | solution.py:567
  86.4 1.6 %collective-permute-start.18 = (bf16[64,4096]{1,0:T(8,128)(2,1)S(1)}, bf16[64,4096]{1,0:T(8,128)(2,1)S(1)}, u32[]{:S(2)}, u32[]{:S(2)}) collective-permute-start(bf16[64,4096]{1,0:T(8,128)(2,1)S(1)} %get-tuple-element.127), channel_id=1, source_target_pairs={{0,6},{2,0},{4,2},{6,4},{1,7},{3,1},{5,3},{7,5},{8,14},{10,8},{12,... | collective-permute-start | bytes 1572872 | tf_op jit(solution)/shard_map/ppermute | solution.py:567
  88.0 3.0 %output_half.3 = (bf16[128,4096]{1,0:T(8,128)(2,1)S(1)}, bf16[128,4096]{1,0:T(8,128)(2,1)S(1)}) custom-call(s32[1]{0:T(128)S(6)} %copy.13.length, bf16[272,512]{1,0:T(8,128)(2,1)S(1)} %collective-permute-done.19.refs_0_, bf16[272,512]{1,0:T(8,128)(2,1)S(1)} %collective-permute-done.20.refs_1_, bf16[272,512]{1,0:T(8,128)(2,1)S(1)} %collective-permute-done.21.refs_2_, ...), custom_call_target="tpu_custom_call" | custom-call | flops 5000000000 | bytes 1 | tf_op jit(solution)/shard_map/output_half/pallas_call | solution.py:416
  90.9 0.8 collective-permute-start.23
  91.7 6.7 %collective-permute-done.16.refs_1_ = bf16[64,4096]{1,0:T(8,128)(2,1)S(1)} collective-permute-done((bf16[64,4096]{1,0:T(8,128)(2,1)S(1)}, bf16[64,4096]{1,0:T(8,128)(2,1)S(1)}, u32[]{:S(2)}, u32[]{:S(2)}) %collective-permute-start.16) | collective-permute-done | bytes 524320 | tf_op jit(solution)/shard_map/ppermute | solution.py:567
  98.4 9.2 %collective-permute-done.17.refs_2_ = bf16[64,4096]{1,0:T(8,128)(2,1)S(1)} collective-permute-done((bf16[64,4096]{1,0:T(8,128)(2,1)S(1)}, bf16[64,4096]{1,0:T(8,128)(2,1)S(1)}, u32[]{:S(2)}, u32[]{:S(2)}) %collective-permute-start.17) | collective-permute-done | bytes 524320 | tf_op jit(solution)/shard_map/ppermute | solution.py:567
  107.6 0.2 collective-permute-done.18.refs_3_
  107.9 0.6 sum_y.1
  108.5 1.3 collective-permute-start.22
  109.7 8.4 %collective-permute-done.23.theirs = bf16[128,4096]{1,0:T(8,128)(2,1)S(1)} collective-permute-done((bf16[128,4096]{1,0:T(8,128)(2,1)S(1)}, bf16[128,4096]{1,0:T(8,128)(2,1)S(1)}, u32[]{:S(2)}, u32[]{:S(2)}) %collective-permute-start.23) | collective-permute-done | bytes 1048608 | tf_op jit(solution)/shard_map/ppermute | solution.py:569
  118.1 0.6 sum_x.1
  118.7 0.8 collective-permute-start.24
  119.5 1.8 %collective-permute-start.25 = (bf16[32,4096]{1,0:T(8,128)(2,1)S(1)}, bf16[32,4096]{1,0:T(8,128)(2,1)S(1)}, u32[]{:S(2)}, u32[]{:S(2)}) collective-permute-start(bf16[32,4096]{1,0:T(8,128)(2,1)S(1)} %get-tuple-element.145), channel_id=1, source_target_pairs={{0,4},{2,6},{4,0},{6,2},{1,5},{3,7},{5,1},{7,3},{8,12},{10,14},{12... | collective-permute-start | bytes 786440 | tf_op jit(solution)/shard_map/ppermute | solution.py:575
  121.3 1.6 %collective-permute-start.26 = (bf16[32,4096]{1,0:T(8,128)(2,1)S(1)}, bf16[32,4096]{1,0:T(8,128)(2,1)S(1)}, u32[]{:S(2)}, u32[]{:S(2)}) collective-permute-start(bf16[32,4096]{1,0:T(8,128)(2,1)S(1)} %get-tuple-element.146), channel_id=1, source_target_pairs={{0,6},{2,0},{4,2},{6,4},{1,7},{3,1},{5,3},{7,5},{8,14},{10,8},{12,... | collective-permute-start | bytes 786440 | tf_op jit(solution)/shard_map/ppermute | solution.py:575
  122.9 7.2 %collective-permute-done.24.refs_3_ = bf16[32,4096]{1,0:T(8,128)(2,1)S(1)} collective-permute-done((bf16[32,4096]{1,0:T(8,128)(2,1)S(1)}, bf16[32,4096]{1,0:T(8,128)(2,1)S(1)}, u32[]{:S(2)}, u32[]{:S(2)}) %collective-permute-start.24) | collective-permute-done | bytes 262176 | tf_op jit(solution)/shard_map/ppermute | solution.py:575
  130.1 1.0 finish.1
  (32 shorter events, 0.3 us)
Async XLA Ops:
  3.2 15.7 %collective-permute-start.3 = (bf16[256,512]{1,0:T(8,128)(2,1)}, bf16[256,512]{1,0:T(8,128)(2,1)S(1)}, u32[]{:S(2)}, u32[]{:S(2)}) collective-permute-start(bf16[256,512]{1,0:T(8,128)(2,1)} %get-tuple-element.78), channel_id=1, source_target_pairs={{0,2},{2,4},{4,6},{6,0},{1,3},{3,5},{5,7},{7,1},{8,10},{10,12},{12... | collective-permute-start | bytes 786440 | tf_op jit(solution)/shard_map/ppermute | solution.py:521
  4.9 14.7 %collective-permute-start.4 = (bf16[256,512]{1,0:T(8,128)(2,1)}, bf16[256,512]{1,0:T(8,128)(2,1)S(1)}, u32[]{:S(2)}, u32[]{:S(2)}) collective-permute-start(bf16[256,512]{1,0:T(8,128)(2,1)} %get-tuple-element.79), channel_id=1, source_target_pairs={{0,4},{2,6},{4,0},{6,2},{1,5},{3,7},{5,1},{7,3},{8,12},{10,14},{12... | collective-permute-start | bytes 786440 | tf_op jit(solution)/shard_map/ppermute | solution.py:521
  7.8 11.9 %collective-permute-start.5 = (bf16[256,512]{1,0:T(8,128)(2,1)}, bf16[256,512]{1,0:T(8,128)(2,1)S(1)}, u32[]{:S(2)}, u32[]{:S(2)}) collective-permute-start(bf16[256,512]{1,0:T(8,128)(2,1)} %get-tuple-element.80), channel_id=1, source_target_pairs={{0,6},{2,0},{4,2},{6,4},{1,7},{3,1},{5,3},{7,5},{8,14},{10,8},{12,... | collective-permute-start | bytes 786440 | tf_op jit(solution)/shard_map/ppermute | solution.py:521
  9.2 10.5 %copy-start.4 = (bf16[256,512]{1,0:T(8,128)(2,1)S(1)}, bf16[256,512]{1,0:T(8,128)(2,1)}, u32[]{:S(2)}) copy-start(bf16[256,512]{1,0:T(8,128)(2,1)} %get-tuple-element.81.refs_0_) | copy-start | bytes 786436
  14.7 17.0 %collective-permute-start.1 = (bf16[512,512]{1,0:T(8,128)(2,1)}, bf16[512,512]{1,0:T(8,128)(2,1)S(1)}, u32[]{:S(2)}, u32[]{:S(2)}) collective-permute-start(bf16[512,512]{1,0:T(8,128)(2,1)} %project_q.1.q_ref.refs_0_), channel_id=1, source_target_pairs={{0,16},{16,32},{32,48},{48,0},{1,17},{17,33},{33,49},{49,1},{2,18}... | collective-permute-start | bytes 1572872 | tf_op jit(solution)/shard_map/ppermute | solution.py:516
  16.7 15.0 %collective-permute-start.2 = (bf16[512,512]{1,0:T(8,128)(2,1)}, bf16[512,512]{1,0:T(8,128)(2,1)S(1)}, u32[]{:S(2)}, u32[]{:S(2)}) collective-permute-start(bf16[512,512]{1,0:T(8,128)(2,1)} %project_q.1.q_ref.refs_0_), channel_id=1, source_target_pairs={{0,48},{16,0},{32,16},{48,32},{1,49},{17,1},{33,17},{49,33},{2,50}... | collective-permute-start | bytes 1572872 | tf_op jit(solution)/shard_map/ppermute | solution.py:516
  19.8 16.0 %collective-permute-start.6 = (bf16[512,512]{1,0:T(8,128)(2,1)S(1)}, bf16[512,512]{1,0:T(8,128)(2,1)S(1)}, u32[]{:S(2)}, u32[]{:S(2)}) collective-permute-start(bf16[512,512]{1,0:T(8,128)(2,1)S(1)} %get-tuple-element.95.refs_2_.refs_1_), channel_id=1, source_target_pairs={{0,64},{64,0},{1,65},{65,1},{2,66},{66,2},{3,67},{67,3},{4,68},{68... | collective-permute-start | bytes 1572872 | tf_op jit(solution)/shard_map/ppermute | solution.py:528
  21.3 10.5 %copy-start = (bf16[512,512]{1,0:T(8,128)(2,1)S(1)}, bf16[512,512]{1,0:T(8,128)(2,1)}, u32[]{:S(2)}) copy-start(bf16[512,512]{1,0:T(8,128)(2,1)} %project_q.1.q_ref.refs_0_) | copy-start | bytes 1572868
  21.3 14.4 %collective-permute-start.7 = (bf16[512,512]{1,0:T(8,128)(2,1)S(1)}, bf16[512,512]{1,0:T(8,128)(2,1)S(1)}, u32[]{:S(2)}, u32[]{:S(2)}) collective-permute-start(bf16[512,512]{1,0:T(8,128)(2,1)S(1)} %get-tuple-element.90), channel_id=1, source_target_pairs={{0,65},{65,0},{1,64},{64,1},{2,67},{67,2},{3,66},{66,3},{4,69},{69... | collective-permute-start | bytes 1572872 | tf_op jit(solution)/shard_map/ppermute | solution.py:529
  31.7 5.2 %collective-permute-start.10 = (bf16[512,512]{1,0:T(8,128)(2,1)S(1)}, bf16[512,512]{1,0:T(8,128)(2,1)S(1)}, u32[]{:S(2)}, u32[]{:S(2)}) collective-permute-start(bf16[512,512]{1,0:T(8,128)(2,1)S(1)} %get-tuple-element.95.refs_2_.refs_1_), channel_id=1, source_target_pairs={{0,8},{8,0},{1,9},{9,1},{2,10},{10,2},{3,11},{11,3},{4,12},{12,4},... | collective-permute-start | bytes 1572872 | tf_op jit(solution)/shard_map/ppermute | solution.py:513
  31.8 16.4 %collective-permute-start = (bf16[512,512]{1,0:T(8,128)(2,1)S(1)}, bf16[512,512]{1,0:T(8,128)(2,1)S(1)}, u32[]{:S(2)}, u32[]{:S(2)}) collective-permute-start(bf16[512,512]{1,0:T(8,128)(2,1)S(1)} %copy-done), channel_id=1, source_target_pairs={{0,32},{16,48},{32,0},{48,16},{1,33},{17,49},{33,1},{49,17},{2,34}... | collective-permute-start | bytes 1572872 | tf_op jit(solution)/shard_map/ppermute | solution.py:516
  35.8 4.2 %collective-permute-start.8 = (bf16[512,512]{1,0:T(8,128)(2,1)S(1)}, bf16[512,512]{1,0:T(8,128)(2,1)S(1)}, u32[]{:S(2)}, u32[]{:S(2)}) collective-permute-start(bf16[512,512]{1,0:T(8,128)(2,1)S(1)} %collective-permute-done.6.refs_2_.refs_3_), channel_id=1, source_target_pairs={{0,8},{8,0},{1,9},{9,1},{2,10},{10,2},{3,11},{11,3},{4,12},{12,4},... | collective-permute-start | bytes 1572872 | tf_op jit(solution)/shard_map/ppermute | solution.py:513
  35.9 4.0 %collective-permute-start.9 = (bf16[512,512]{1,0:T(8,128)(2,1)S(1)}, bf16[512,512]{1,0:T(8,128)(2,1)S(1)}, u32[]{:S(2)}, u32[]{:S(2)}) collective-permute-start(bf16[512,512]{1,0:T(8,128)(2,1)S(1)} %collective-permute-done.7.refs_3_.refs_4_), channel_id=1, source_target_pairs={{0,8},{8,0},{1,9},{9,1},{2,10},{10,2},{3,11},{11,3},{4,12},{12,4},... | collective-permute-start | bytes 1572872 | tf_op jit(solution)/shard_map/ppermute | solution.py:513
  36.3 16.7 %collective-permute-start.11 = (bf16[512,512]{1,0:T(8,128)(2,1)S(1)}, bf16[512,512]{1,0:T(8,128)(2,1)S(1)}, u32[]{:S(2)}, u32[]{:S(2)}) collective-permute-start(bf16[512,512]{1,0:T(8,128)(2,1)S(1)} %collective-permute-done.7.refs_3_.refs_4_), channel_id=1, source_target_pairs={{0,64},{64,0},{1,65},{65,1},{2,66},{66,2},{3,67},{67,3},{4,68},{68... | collective-permute-start | bytes 1572872 | tf_op jit(solution)/shard_map/ppermute | solution.py:536
  53.0 2.0 %collective-permute-start.12 = (bf16[512,512]{1,0:T(8,128)(2,1)S(1)}, bf16[512,512]{1,0:T(8,128)(2,1)S(1)}, u32[]{:S(2)}, u32[]{:S(2)}) collective-permute-start(bf16[512,512]{1,0:T(8,128)(2,1)S(1)} %collective-permute-done.11.refs_3_.refs_7_), channel_id=1, source_target_pairs={{0,8},{8,0},{1,9},{9,1},{2,10},{10,2},{3,11},{11,3},{4,12},{12,4},... | collective-permute-start | bytes 1572872 | tf_op jit(solution)/shard_map/ppermute | solution.py:513
  57.4 11.5 %collective-permute-start.13 = (bf16[272,512]{1,0:T(8,128)(2,1)S(1)}, bf16[272,512]{1,0:T(8,128)(2,1)S(1)}, u32[]{:S(2)}, u32[]{:S(2)}) collective-permute-start(bf16[272,512]{1,0:T(8,128)(2,1)S(1)} %get-tuple-element.108), channel_id=1, source_target_pairs={{0,32},{16,48},{32,0},{48,16},{1,33},{17,49},{33,1},{49,17},{2,34}... | collective-permute-start | bytes 835592 | tf_op jit(solution)/shard_map/ppermute | solution.py:516
  60.7 17.1 %collective-permute-start.14 = (bf16[272,512]{1,0:T(8,128)(2,1)S(1)}, bf16[272,512]{1,0:T(8,128)(2,1)S(1)}, u32[]{:S(2)}, u32[]{:S(2)}) collective-permute-start(bf16[272,512]{1,0:T(8,128)(2,1)S(1)} %get-tuple-element.109), channel_id=1, source_target_pairs={{0,48},{16,0},{32,16},{48,32},{1,49},{17,1},{33,17},{49,33},{2,50}... | collective-permute-start | bytes 835592 | tf_op jit(solution)/shard_map/ppermute | solution.py:516
  61.4 9.0 %copy-start.2 = (bf16[512,512]{1,0:T(8,128)(2,1)S(1)}, bf16[512,512]{1,0:T(8,128)(2,1)}, u32[]{:S(2)}) copy-start(bf16[512,512]{1,0:T(8,128)(2,1)} %get-tuple-element.116.k_ref) | copy-start | bytes 1572868
  61.4 9.0 %copy-start.3 = (bf16[512,512]{1,0:T(8,128)(2,1)S(1)}, bf16[512,512]{1,0:T(8,128)(2,1)}, u32[]{:S(2)}) copy-start(bf16[512,512]{1,0:T(8,128)(2,1)} %get-tuple-element.117.v_ref) | copy-start | bytes 1572868
  61.4 16.4 %collective-permute-start.15 = (bf16[272,512]{1,0:T(8,128)(2,1)S(1)}, bf16[272,512]{1,0:T(8,128)(2,1)S(1)}, u32[]{:S(2)}, u32[]{:S(2)}) collective-permute-start(bf16[272,512]{1,0:T(8,128)(2,1)S(1)} %get-tuple-element.110), channel_id=1, source_target_pairs={{0,16},{16,32},{32,48},{48,0},{1,17},{17,33},{33,49},{49,1},{2,18}... | collective-permute-start | bytes 835592 | tf_op jit(solution)/shard_map/ppermute | solution.py:516
  65.1 21.3 %collective-permute-start.19 = (bf16[272,512]{1,0:T(8,128)(2,1)S(1)}, bf16[272,512]{1,0:T(8,128)(2,1)S(1)}, u32[]{:S(2)}, u32[]{:S(2)}) collective-permute-start(bf16[272,512]{1,0:T(8,128)(2,1)S(1)} %get-tuple-element.113), channel_id=1, source_target_pairs={{0,32},{16,48},{32,0},{48,16},{1,33},{17,49},{33,1},{49,17},{2,34}... | collective-permute-start | bytes 835592 | tf_op jit(solution)/shard_map/ppermute | solution.py:516
  66.2 21.7 %collective-permute-start.20 = (bf16[272,512]{1,0:T(8,128)(2,1)S(1)}, bf16[272,512]{1,0:T(8,128)(2,1)S(1)}, u32[]{:S(2)}, u32[]{:S(2)}) collective-permute-start(bf16[272,512]{1,0:T(8,128)(2,1)S(1)} %get-tuple-element.128), channel_id=1, source_target_pairs={{0,48},{16,0},{32,16},{48,32},{1,49},{17,1},{33,17},{49,33},{2,50}... | collective-permute-start | bytes 835592 | tf_op jit(solution)/shard_map/ppermute | solution.py:516
  68.9 19.1 %collective-permute-start.21 = (bf16[272,512]{1,0:T(8,128)(2,1)S(1)}, bf16[272,512]{1,0:T(8,128)(2,1)S(1)}, u32[]{:S(2)}, u32[]{:S(2)}) collective-permute-start(bf16[272,512]{1,0:T(8,128)(2,1)S(1)} %get-tuple-element.129), channel_id=1, source_target_pairs={{0,16},{16,32},{32,48},{48,0},{1,17},{17,33},{33,49},{49,1},{2,18}... | collective-permute-start | bytes 835592 | tf_op jit(solution)/shard_map/ppermute | solution.py:516
  72.3 5.5 %copy-start.1 = (bf16[512,4096]{1,0:T(8,128)(2,1)S(1)}, bf16[512,4096]{1,0:T(8,128)(2,1)}, u32[]{:S(2)}) copy-start(bf16[512,4096]{1,0:T(8,128)(2,1)} %refs_4_.4) | copy-start | bytes 12582916
  82.4 16.0 %collective-permute-start.16 = (bf16[64,4096]{1,0:T(8,128)(2,1)S(1)}, bf16[64,4096]{1,0:T(8,128)(2,1)S(1)}, u32[]{:S(2)}, u32[]{:S(2)}) collective-permute-start(bf16[64,4096]{1,0:T(8,128)(2,1)S(1)} %get-tuple-element.125), channel_id=1, source_target_pairs={{0,2},{2,4},{4,6},{6,0},{1,3},{3,5},{5,7},{7,1},{8,10},{10,12},{12... | collective-permute-start | bytes 1572872 | tf_op jit(solution)/shard_map/ppermute | solution.py:567
  84.0 23.7 %collective-permute-start.17 = (bf16[64,4096]{1,0:T(8,128)(2,1)S(1)}, bf16[64,4096]{1,0:T(8,128)(2,1)S(1)}, u32[]{:S(2)}, u32[]{:S(2)}) collective-permute-start(bf16[64,4096]{1,0:T(8,128)(2,1)S(1)} %get-tuple-element.126), channel_id=1, source_target_pairs={{0,4},{2,6},{4,0},{6,2},{1,5},{3,7},{5,1},{7,3},{8,12},{10,14},{12... | collective-permute-start | bytes 1572872 | tf_op jit(solution)/shard_map/ppermute | solution.py:567
  86.4 21.5 %collective-permute-start.18 = (bf16[64,4096]{1,0:T(8,128)(2,1)S(1)}, bf16[64,4096]{1,0:T(8,128)(2,1)S(1)}, u32[]{:S(2)}, u32[]{:S(2)}) collective-permute-start(bf16[64,4096]{1,0:T(8,128)(2,1)S(1)} %get-tuple-element.127), channel_id=1, source_target_pairs={{0,6},{2,0},{4,2},{6,4},{1,7},{3,1},{5,3},{7,5},{8,14},{10,8},{12,... | collective-permute-start | bytes 1572872 | tf_op jit(solution)/shard_map/ppermute | solution.py:567
  90.9 27.2 %collective-permute-start.23 = (bf16[128,4096]{1,0:T(8,128)(2,1)S(1)}, bf16[128,4096]{1,0:T(8,128)(2,1)S(1)}, u32[]{:S(2)}, u32[]{:S(2)}) collective-permute-start(bf16[128,4096]{1,0:T(8,128)(2,1)S(1)} %get-tuple-element.141), channel_id=1, source_target_pairs={{0,1},{1,0},{2,3},{3,2},{4,5},{5,4},{6,7},{7,6},{8,9},{9,8},{10,11... | collective-permute-start | bytes 3145736 | tf_op jit(solution)/shard_map/ppermute | solution.py:569
  108.5 14.4 %collective-permute-start.22 = (bf16[32,4096]{1,0:T(8,128)(2,1)S(1)}, bf16[32,4096]{1,0:T(8,128)(2,1)S(1)}, u32[]{:S(2)}, u32[]{:S(2)}) collective-permute-start(bf16[32,4096]{1,0:T(8,128)(2,1)S(1)} %get-tuple-element.140), channel_id=1, source_target_pairs={{0,1},{1,0},{2,3},{3,2},{4,5},{5,4},{6,7},{7,6},{8,9},{9,8},{10,11... | collective-permute-start | bytes 786440 | tf_op jit(solution)/shard_map/ppermute | solution.py:572
  118.7 11.4 %collective-permute-start.24 = (bf16[32,4096]{1,0:T(8,128)(2,1)S(1)}, bf16[32,4096]{1,0:T(8,128)(2,1)S(1)}, u32[]{:S(2)}, u32[]{:S(2)}) collective-permute-start(bf16[32,4096]{1,0:T(8,128)(2,1)S(1)} %get-tuple-element.144), channel_id=1, source_target_pairs={{0,2},{2,4},{4,6},{6,0},{1,3},{3,5},{5,7},{7,1},{8,10},{10,12},{12... | collective-permute-start | bytes 786440 | tf_op jit(solution)/shard_map/ppermute | solution.py:575
  119.5 10.6 %collective-permute-start.25 = (bf16[32,4096]{1,0:T(8,128)(2,1)S(1)}, bf16[32,4096]{1,0:T(8,128)(2,1)S(1)}, u32[]{:S(2)}, u32[]{:S(2)}) collective-permute-start(bf16[32,4096]{1,0:T(8,128)(2,1)S(1)} %get-tuple-element.145), channel_id=1, source_target_pairs={{0,4},{2,6},{4,0},{6,2},{1,5},{3,7},{5,1},{7,3},{8,12},{10,14},{12... | collective-permute-start | bytes 786440 | tf_op jit(solution)/shard_map/ppermute | solution.py:575
  121.3 8.8 %collective-permute-start.26 = (bf16[32,4096]{1,0:T(8,128)(2,1)S(1)}, bf16[32,4096]{1,0:T(8,128)(2,1)S(1)}, u32[]{:S(2)}, u32[]{:S(2)}) collective-permute-start(bf16[32,4096]{1,0:T(8,128)(2,1)S(1)} %get-tuple-element.146), channel_id=1, source_target_pairs={{0,6},{2,0},{4,2},{6,4},{1,7},{3,1},{5,3},{7,5},{8,14},{10,8},{12,... | collective-permute-start | bytes 786440 | tf_op jit(solution)/shard_map/ppermute | solution.py:575

commit v5 on v4

--- a/solution.py
+++ b/solution.py
@@ -550,16 +550,17 @@
     (state2,) = prefix_attention(
         "attend_two", [q2], [near, near_c, *middle], [6], [None]
     )
-    queries, states = [q2, q1, q3], [state2, state1, state3]
+    queries, states = [q1, q2, q3], [state1, state2, state3]
     (far_xx,) = in_order([far_xx], state2[0])
     final = [far_xx, core(far_xx)]
+    (k_suffix,) = in_order([k_suffix], far_xx)
+    begun = suffix_attention(suffix_len, q, k_suffix, v_suffix)
+    final[1:] = in_order(final[1:], begun[0])
     sums = []
     for half in range(2):
         sent = prefix_attention("attend_last", queries, final, [2] * 3, states, [half])
-        sums.append([along_z(m, back) for m, back in zip(sent, [2, -1, 1])])
+        sums.append([along_z(m, back) for m, back in zip(sent, [-1, 2, 1])])
         final = in_order(final, sent[0])
-    (k_suffix,) = in_order([k_suffix], final[0])
-    begun = suffix_attention(suffix_len, q, k_suffix, v_suffix)
     every = [near, near_c, *middle, *final]
     own = prefix_attention("attend_own", [q], every, [8], [begun], [0, 1])
     cut = output_half(suffix_len, 0, in_order(sums[0], own[0]) + [own[0]], w_output)

time: 131 us -> 133 us (1.015)
    ppermute x9, waiting for transfers between devices: 2.56 us -> 5.83 us  [along_z(): return lax.ppermute(x, 'z', shift(4, by))]
    ppermute x4, waiting for transfers between devices: 1.9 us -> 0.01 us  [core(): return lax.ppermute(x, 'core', shift(2, 1))]
    ppermute x1, starting transfers between devices: 0.79 us -> 2.12 us  [body(): theirs = lax.ppermute(theirs, 'xhi', shift(2, 1))]
  transfers between devices with their start and end apart: 27 -> 27, of which waited for: 8 -> 10; matrix products, arithmetic and copies ran while one was open for 0% -> 0% of each run, Pallas kernels for 35% -> 35%
where the time goes in v5:
time: 133 us
  Pallas kernels  52.3 us (39%)
  starting transfers between devices  41.2 us (31%)
  waiting for transfers between devices  38.3 us (29%)
    pallas_call x6, Pallas kernels, prefix_attention(): call(functools.partial(prefix_kernel, nq, nkv, used, held, halves), name,...  23.8 us
    ppermute x9, starting transfers between devices, along_z(): return lax.ppermute(x, 'z', shift(4, by))  17.2 us
    ppermute x3, waiting for transfers between devices, body(): cut = [cut[0]] + [lax.ppermute(cut[d], 'y', shift(4, d)) for d in (1, 2, 3)]  15.6 us
    pallas_call x2, Pallas kernels, project(): call(functools.partial(project_kernel, kinds, LOG2E / math.sqrt(HD)), 'pr...  13.8 us
    ppermute x1, waiting for transfers between devices, body(): theirs = lax.ppermute(theirs, 'xhi', shift(2, 1))  8.09 us
    ppermute x3, waiting for transfers between devices, body(): lax.ppermute(lower[d], 'y', shift(4, d))  7.82 us
    pallas_call x2, Pallas kernels, output_half(): call(functools.partial(output_kernel, n, half), 'output_half', flops=1 +...  7.54 us
    ppermute x3, starting transfers between devices, body(): lax.ppermute(sent[d], 'y', shift(4, d))  5.98 us
  transfers between devices with their start and end apart: 27, of which 10 were waited for; matrix products, arithmetic and copies ran while one was open for 0% of the time, Pallas kernels for 35%

profile of v5, /device:TPU:0, one launch (start us, length us, event | category | flops | bytes accessed | tf_op | source)
XLA Modules:
  0.0 132.7 jit_solution(3788667891245901145)
XLA Ops:
  0.0 3.2 %prepare.1 = (bf16[256,512]{1,0:T(8,128)(2,1)}, bf16[256,512]{1,0:T(8,128)(2,1)}, bf16[256,512]{1,0:T(8,128)(2,1)}, bf16[256,512]{1,0:T(8,128)(2,1)}) custom-call(s32[4,128]{1,0:T(4,128)} %bitcast.5, f32[1,128]{1,0:T(1,128)} %constant.8.clone.freq, bf16[64,4096]{1,0:T(8,128)(2,1)} %bitcast.3, bf16[64,4096]{1,0:T(8,128)(2,1)} %bitcast.4), custom_call_target="tpu_custom_call" | custom-call | flops 1 | bytes 1 | tf_op jit(solution)/shard_map/prepare/pallas_call | solution.py:120
  3.2 1.7 %collective-permute-start.2 = (bf16[256,512]{1,0:T(8,128)(2,1)}, bf16[256,512]{1,0:T(8,128)(2,1)S(1)}, u32[]{:S(2)}, u32[]{:S(2)}) collective-permute-start(bf16[256,512]{1,0:T(8,128)(2,1)} %get-tuple-element.79), channel_id=1, source_target_pairs={{0,2},{2,4},{4,6},{6,0},{1,3},{3,5},{5,7},{7,1},{8,10},{10,12},{12... | collective-permute-start | bytes 786440 | tf_op jit(solution)/shard_map/ppermute | solution.py:521
  4.9 2.9 %collective-permute-start.3 = (bf16[256,512]{1,0:T(8,128)(2,1)}, bf16[256,512]{1,0:T(8,128)(2,1)S(1)}, u32[]{:S(2)}, u32[]{:S(2)}) collective-permute-start(bf16[256,512]{1,0:T(8,128)(2,1)} %get-tuple-element.80), channel_id=1, source_target_pairs={{0,4},{2,6},{4,0},{6,2},{1,5},{3,7},{5,1},{7,3},{8,12},{10,14},{12... | collective-permute-start | bytes 786440 | tf_op jit(solution)/shard_map/ppermute | solution.py:521
  7.8 1.3 %collective-permute-start.4 = (bf16[256,512]{1,0:T(8,128)(2,1)}, bf16[256,512]{1,0:T(8,128)(2,1)S(1)}, u32[]{:S(2)}, u32[]{:S(2)}) collective-permute-start(bf16[256,512]{1,0:T(8,128)(2,1)} %get-tuple-element.81), channel_id=1, source_target_pairs={{0,6},{2,0},{4,2},{6,4},{1,7},{3,1},{5,3},{7,5},{8,14},{10,8},{12,... | collective-permute-start | bytes 786440 | tf_op jit(solution)/shard_map/ppermute | solution.py:521
  9.2 5.5 %project_q.1.q_ref.refs_0_ = bf16[512,512]{1,0:T(8,128)(2,1)} custom-call(bf16[512,4096]{1,0:T(8,128)(2,1)} %refs_0_.1, bf16[4096,512]{1,0:T(8,128)(2,1)} %refs_1_.2, f32[512,128]{1,0:T(8,128)} %constant.6.clone.refs_2_.refs_3_, f32[512,128]{1,0:T(8,128)} %constant.7.clone.refs_3_.refs_4_), custom_call_target="tpu_custom_call" | custom-call | flops 1 | bytes 1 | tf_op jit(solution)/shard_map/project_q/pallas_call | solution.py:190
  14.7 4.1 %collective-permute-start.1 = (bf16[512,512]{1,0:T(8,128)(2,1)}, bf16[512,512]{1,0:T(8,128)(2,1)S(1)}, u32[]{:S(2)}, u32[]{:S(2)}) collective-permute-start(bf16[512,512]{1,0:T(8,128)(2,1)} %project_q.1.q_ref.refs_0_), channel_id=1, source_target_pairs={{0,48},{16,0},{32,16},{48,32},{1,49},{17,1},{33,17},{49,33},{2,50}... | collective-permute-start | bytes 1572872 | tf_op jit(solution)/shard_map/ppermute | solution.py:516
  18.8 0.9 collective-permute-done.3.refs_2_
  19.8 1.6 %collective-permute-start.6 = (bf16[512,512]{1,0:T(8,128)(2,1)S(1)}, bf16[512,512]{1,0:T(8,128)(2,1)S(1)}, u32[]{:S(2)}, u32[]{:S(2)}) collective-permute-start(bf16[512,512]{1,0:T(8,128)(2,1)S(1)} %get-tuple-element.96.refs_2_.refs_1_), channel_id=1, source_target_pairs={{0,64},{64,0},{1,65},{65,1},{2,66},{66,2},{3,67},{67,3},{4,68},{68... | collective-permute-start | bytes 1572872 | tf_op jit(solution)/shard_map/ppermute | solution.py:528
  21.3 2.1 %collective-permute-start.7 = (bf16[512,512]{1,0:T(8,128)(2,1)S(1)}, bf16[512,512]{1,0:T(8,128)(2,1)S(1)}, u32[]{:S(2)}, u32[]{:S(2)}) collective-permute-start(bf16[512,512]{1,0:T(8,128)(2,1)S(1)} %get-tuple-element.91), channel_id=1, source_target_pairs={{0,65},{65,0},{1,64},{64,1},{2,67},{67,2},{3,66},{66,3},{4,69},{69... | collective-permute-start | bytes 1572872 | tf_op jit(solution)/shard_map/ppermute | solution.py:529
  23.4 8.3 %project_kv.1 = (bf16[512,512]{1,0:T(8,128)(2,1)}, bf16[512,512]{1,0:T(8,128)(2,1)}) custom-call(bf16[512,4096]{1,0:T(8,128)(2,1)} %refs_0_.1, bf16[4096,512]{1,0:T(8,128)(2,1)} %refs_1_.3, bf16[4096,512]{1,0:T(8,128)(2,1)} %refs_2_.2, f32[512,128]{1,0:T(8,128)} %constant.6.clone.refs_2_.refs_3_, f32[512,128]{1,0:T(8,128)} %constant.7.clone.refs_3_.refs_4_), custom_call_target="tpu_custom_call" | custom-call | flops 1 | bytes 1 | tf_op jit(solution)/shard_map/project_kv/pallas_call | solution.py:190
  31.7 1.1 collective-permute-done.refs_0_
  32.8 3.0 %collective-permute-start.5 = (bf16[512,512]{1,0:T(8,128)(2,1)S(1)}, bf16[512,512]{1,0:T(8,128)(2,1)S(1)}, u32[]{:S(2)}, u32[]{:S(2)}) collective-permute-start(bf16[512,512]{1,0:T(8,128)(2,1)S(1)} %copy-done), channel_id=1, source_target_pairs={{0,32},{16,48},{32,0},{48,16},{1,33},{17,49},{33,1},{49,17},{2,34}... | collective-permute-start | bytes 1572872 | tf_op jit(solution)/shard_map/ppermute | solution.py:516
  35.8 0.2 collective-permute-start.8
  35.9 0.6 collective-permute-start.11
  36.6 3.0 %attend_near.1 = (f32[512,1024]{1,0:T(8,128)S(1)}, f32[512,512]{1,0:T(8,128)S(1)}, f32[512,1024]{1,0:T(8,128)S(1)}, f32[512,512]{1,0:T(8,128)S(1)}) custom-call(bf16[512,512]{1,0:T(8,128)(2,1)S(1)} %collective-permute-done.refs_0_, bf16[512,512]{1,0:T(8,128)(2,1)S(1)} %collective-permute-done.1.refs_1_.refs_2_, ...), custom_call_target="tpu_custom_call" | custom-call | flops 10000000000 | bytes 1 | tf_op jit(solution)/shard_map/attend_near/pallas_call | solution.py:348
  39.7 5.8 %attend_middle.1 = (f32[512,1024]{1,0:T(8,128)S(1)}, f32[512,512]{1,0:T(8,128)S(1)}, f32[512,1024]{1,0:T(8,128)S(1)}, f32[512,512]{1,0:T(8,128)S(1)}) custom-call(bf16[512,512]{1,0:T(8,128)(2,1)S(1)} %collective-permute-done.refs_0_, bf16[512,512]{1,0:T(8,128)(2,1)S(1)} %collective-permute-done.1.refs_1_.refs_2_, ...), custom_call_target="tpu_custom_call" | custom-call | flops 1 | bytes 1 | tf_op jit(solution)/shard_map/attend_middle/pallas_call | solution.py:348
  45.5 3.2 %collective-permute-done.5.refs_0_.refs_1_ = bf16[512,512]{1,0:T(8,128)(2,1)S(1)} collective-permute-done((bf16[512,512]{1,0:T(8,128)(2,1)S(1)}, bf16[512,512]{1,0:T(8,128)(2,1)S(1)}, u32[]{:S(2)}, u32[]{:S(2)}) %collective-permute-start.5) | collective-permute-done | bytes 524320 | tf_op jit(solution)/shard_map/ppermute | solution.py:516
  48.6 4.7 %attend_two.1 = (f32[512,1024]{1,0:T(8,128)S(1)}, f32[512,512]{1,0:T(8,128)S(1)}) custom-call(bf16[512,512]{1,0:T(8,128)(2,1)S(1)} %collective-permute-done.5.refs_0_.refs_1_, bf16[512,512]{1,0:T(8,128)(2,1)S(1)} %get-tuple-element.96.refs_2_.refs_1_, bf16[512,512]{1,0:T(8,128)(2,1)S(1)} %collective-permute-done.10.refs_3_.refs_2_, ...), custom_call_target="tpu_custom_call" | custom-call | flops 1 | bytes 1 | tf_op jit(solution)/shard_map/attend_two/pallas_call | solution.py:348
  53.4 0.1 collective-permute-start.12
  54.1 1.8 %suffix_attention.1 = (f32[512,1024]{1,0:T(8,128)S(1)}, f32[512,512]{1,0:T(8,128)S(1)}) custom-call(s32[1]{0:T(128)S(6)} %copy.13.length, bf16[512,512]{1,0:T(8,128)(2,1)S(1)} %copy-done, bf16[512,512]{1,0:T(8,128)(2,1)S(1)} %copy-done.2, bf16[512,512]{1,0:T(8,128)(2,1)S(1)} %copy-done.3), custom_call_target="tpu_custom_call" | custom-call | flops 1 | bytes 1 | tf_op jit(solution)/shard_map/suffix_attention/pallas_call | solution.py:258
  56.0 2.4 %attend_last.2 = (bf16[272,512]{1,0:T(8,128)(2,1)S(1)}, bf16[272,512]{1,0:T(8,128)(2,1)S(1)}, bf16[272,512]{1,0:T(8,128)(2,1)S(1)}) custom-call(bf16[512,512]{1,0:T(8,128)(2,1)S(1)} %collective-permute-done.refs_0_, bf16[512,512]{1,0:T(8,128)(2,1)S(1)} %collective-permute-done.5.refs_0_.refs_1_, bf16[512,512]{1,0:T(8,128)(2,1)S(1)} %collective-permute-done.1.refs_1_.refs_2_, ...), custom_call_target="tpu_custom_call" | custom-call | flops 1 | bytes 1 | tf_op jit(solution)/shard_map/attend_last/pallas_call | solution.py:348
  58.4 3.0 %collective-permute-start.14 = (bf16[272,512]{1,0:T(8,128)(2,1)S(1)}, bf16[272,512]{1,0:T(8,128)(2,1)S(1)}, u32[]{:S(2)}, u32[]{:S(2)}) collective-permute-start(bf16[272,512]{1,0:T(8,128)(2,1)S(1)} %get-tuple-element.114), channel_id=1, source_target_pairs={{0,32},{16,48},{32,0},{48,16},{1,33},{17,49},{33,1},{49,17},{2,34}... | collective-permute-start | bytes 835592 | tf_op jit(solution)/shard_map/ppermute | solution.py:516
  61.3 1.0 collective-permute-start.15
  62.3 2.2 %collective-permute-start.13 = (bf16[272,512]{1,0:T(8,128)(2,1)S(1)}, bf16[272,512]{1,0:T(8,128)(2,1)S(1)}, u32[]{:S(2)}, u32[]{:S(2)}) collective-permute-start(bf16[272,512]{1,0:T(8,128)(2,1)S(1)} %get-tuple-element.113), channel_id=1, source_target_pairs={{0,48},{16,0},{32,16},{48,32},{1,49},{17,1},{33,17},{49,33},{2,50}... | collective-permute-start | bytes 835592 | tf_op jit(solution)/shard_map/ppermute | solution.py:516
  64.6 2.4 %attend_last.3 = (bf16[272,512]{1,0:T(8,128)(2,1)S(1)}, bf16[272,512]{1,0:T(8,128)(2,1)S(1)}, bf16[272,512]{1,0:T(8,128)(2,1)S(1)}) custom-call(bf16[512,512]{1,0:T(8,128)(2,1)S(1)} %collective-permute-done.refs_0_, bf16[512,512]{1,0:T(8,128)(2,1)S(1)} %collective-permute-done.5.refs_0_.refs_1_, bf16[512,512]{1,0:T(8,128)(2,1)S(1)} %collective-permute-done.1.refs_1_.refs_2_, ...), custom_call_target="tpu_custom_call" | custom-call | flops 1 | bytes 1 | tf_op jit(solution)/shard_map/attend_last/pallas_call | solution.py:348
  67.0 0.8 collective-permute-start.21
  67.9 1.6 %collective-permute-done.14.refs_1_ = bf16[272,512]{1,0:T(8,128)(2,1)S(1)} collective-permute-done((bf16[272,512]{1,0:T(8,128)(2,1)S(1)}, bf16[272,512]{1,0:T(8,128)(2,1)S(1)}, u32[]{:S(2)}, u32[]{:S(2)}) %collective-permute-start.14) | collective-permute-done | bytes 278560 | tf_op jit(solution)/shard_map/ppermute | solution.py:516
  69.4 3.1 %collective-permute-start.19 = (bf16[272,512]{1,0:T(8,128)(2,1)S(1)}, bf16[272,512]{1,0:T(8,128)(2,1)S(1)}, u32[]{:S(2)}, u32[]{:S(2)}) collective-permute-start(bf16[272,512]{1,0:T(8,128)(2,1)S(1)} %get-tuple-element.118), channel_id=1, source_target_pairs={{0,48},{16,0},{32,16},{48,32},{1,49},{17,1},{33,17},{49,33},{2,50}... | collective-permute-start | bytes 835592 | tf_op jit(solution)/shard_map/ppermute | solution.py:516
  72.5 5.5 %attend_own.1 = (bf16[272,512]{1,0:T(8,128)(2,1)S(1)}, bf16[272,512]{1,0:T(8,128)(2,1)S(1)}) custom-call(bf16[512,512]{1,0:T(8,128)(2,1)S(1)} %copy-done, bf16[512,512]{1,0:T(8,128)(2,1)S(1)} %get-tuple-element.96.refs_2_.refs_1_, bf16[512,512]{1,0:T(8,128)(2,1)S(1)} %collective-permute-done.10.refs_3_.refs_2_, ...), custom_call_target="tpu_custom_call" | custom-call | flops 1 | bytes 1 | tf_op jit(solution)/shard_map/attend_own/pallas_call | solution.py:348
  78.0 4.6 %output_half.2 = (bf16[64,4096]{1,0:T(8,128)(2,1)S(1)}, bf16[64,4096]{1,0:T(8,128)(2,1)S(1)}, bf16[64,4096]{1,0:T(8,128)(2,1)S(1)}, bf16[64,4096]{1,0:T(8,128)(2,1)S(1)}) custom-call(s32[1]{0:T(128)S(6)} %copy.13.length, bf16[272,512]{1,0:T(8,128)(2,1)S(1)} %collective-permute-done.13.refs_0_, bf16[272,512]{1,0:T(8,128)(2,1)S(1)} %collective-permute-done.14.refs_1_, ...), custom_call_target="tpu_custom_call" | custom-call | flops 1 | bytes 1 | tf_op jit(solution)/shard_map/output_half/pallas_call | solution.py:416
  82.6 1.3 collective-permute-start.16
  83.9 2.4 %collective-permute-start.17 = (bf16[64,4096]{1,0:T(8,128)(2,1)S(1)}, bf16[64,4096]{1,0:T(8,128)(2,1)S(1)}, u32[]{:S(2)}, u32[]{:S(2)}) collective-permute-start(bf16[64,4096]{1,0:T(8,128)(2,1)S(1)} %get-tuple-element.128), channel_id=1, source_target_pairs={{0,4},{2,6},{4,0},{6,2},{1,5},{3,7},{5,1},{7,3},{8,12},{10,14},{12... | collective-permute-start | bytes 1572872 | tf_op jit(solution)/shard_map/ppermute | solution.py:568
  86.3 1.6 %collective-permute-start.18 = (bf16[64,4096]{1,0:T(8,128)(2,1)S(1)}, bf16[64,4096]{1,0:T(8,128)(2,1)S(1)}, u32[]{:S(2)}, u32[]{:S(2)}) collective-permute-start(bf16[64,4096]{1,0:T(8,128)(2,1)S(1)} %get-tuple-element.129), channel_id=1, source_target_pairs={{0,6},{2,0},{4,2},{6,4},{1,7},{3,1},{5,3},{7,5},{8,14},{10,8},{12,... | collective-permute-start | bytes 1572872 | tf_op jit(solution)/shard_map/ppermute | solution.py:568
  87.9 3.0 %output_half.3 = (bf16[128,4096]{1,0:T(8,128)(2,1)S(1)}, bf16[128,4096]{1,0:T(8,128)(2,1)S(1)}) custom-call(s32[1]{0:T(128)S(6)} %copy.13.length, bf16[272,512]{1,0:T(8,128)(2,1)S(1)} %collective-permute-done.19.refs_0_, bf16[272,512]{1,0:T(8,128)(2,1)S(1)} %collective-permute-done.20.refs_1_, bf16[272,512]{1,0:T(8,128)(2,1)S(1)} %collective-permute-done.21.refs_2_, ...), custom_call_target="tpu_custom_call" | custom-call | flops 5000000000 | bytes 1 | tf_op jit(solution)/shard_map/output_half/pallas_call | solution.py:416
  90.8 2.1 %collective-permute-start.23 = (bf16[128,4096]{1,0:T(8,128)(2,1)S(1)}, bf16[128,4096]{1,0:T(8,128)(2,1)S(1)}, u32[]{:S(2)}, u32[]{:S(2)}) collective-permute-start(bf16[128,4096]{1,0:T(8,128)(2,1)S(1)} %get-tuple-element.143), channel_id=1, source_target_pairs={{0,1},{1,0},{2,3},{3,2},{4,5},{5,4},{6,7},{7,6},{8,9},{9,8},{10,11... | collective-permute-start | bytes 3145736 | tf_op jit(solution)/shard_map/ppermute | solution.py:570
  93.0 5.4 %collective-permute-done.16.refs_1_ = bf16[64,4096]{1,0:T(8,128)(2,1)S(1)} collective-permute-done((bf16[64,4096]{1,0:T(8,128)(2,1)S(1)}, bf16[64,4096]{1,0:T(8,128)(2,1)S(1)}, u32[]{:S(2)}, u32[]{:S(2)}) %collective-permute-start.16) | collective-permute-done | bytes 524320 | tf_op jit(solution)/shard_map/ppermute | solution.py:568
  98.3 10.0 %collective-permute-done.17.refs_2_ = bf16[64,4096]{1,0:T(8,128)(2,1)S(1)} collective-permute-done((bf16[64,4096]{1,0:T(8,128)(2,1)S(1)}, bf16[64,4096]{1,0:T(8,128)(2,1)S(1)}, u32[]{:S(2)}, u32[]{:S(2)}) %collective-permute-start.17) | collective-permute-done | bytes 524320 | tf_op jit(solution)/shard_map/ppermute | solution.py:568
  108.4 0.2 collective-permute-done.18.refs_3_
  108.6 0.6 sum_y.1
  109.2 1.2 collective-permute-start.22
  110.4 8.1 %collective-permute-done.23.theirs = bf16[128,4096]{1,0:T(8,128)(2,1)S(1)} collective-permute-done((bf16[128,4096]{1,0:T(8,128)(2,1)S(1)}, bf16[128,4096]{1,0:T(8,128)(2,1)S(1)}, u32[]{:S(2)}, u32[]{:S(2)}) %collective-permute-start.23) | collective-permute-done | bytes 1048608 | tf_op jit(solution)/shard_map/ppermute | solution.py:570
  118.5 0.6 sum_x.1
  119.1 0.8 collective-permute-start.24
  119.9 2.4 %collective-permute-start.25 = (bf16[32,4096]{1,0:T(8,128)(2,1)S(1)}, bf16[32,4096]{1,0:T(8,128)(2,1)S(1)}, u32[]{:S(2)}, u32[]{:S(2)}) collective-permute-start(bf16[32,4096]{1,0:T(8,128)(2,1)S(1)} %get-tuple-element.147), channel_id=1, source_target_pairs={{0,4},{2,6},{4,0},{6,2},{1,5},{3,7},{5,1},{7,3},{8,12},{10,14},{12... | collective-permute-start | bytes 786440 | tf_op jit(solution)/shard_map/ppermute | solution.py:576
  122.3 1.6 %collective-permute-start.26 = (bf16[32,4096]{1,0:T(8,128)(2,1)S(1)}, bf16[32,4096]{1,0:T(8,128)(2,1)S(1)}, u32[]{:S(2)}, u32[]{:S(2)}) collective-permute-start(bf16[32,4096]{1,0:T(8,128)(2,1)S(1)} %get-tuple-element.148), channel_id=1, source_target_pairs={{0,6},{2,0},{4,2},{6,4},{1,7},{3,1},{5,3},{7,5},{8,14},{10,8},{12,... | collective-permute-start | bytes 786440 | tf_op jit(solution)/shard_map/ppermute | solution.py:576
  123.9 5.0 %collective-permute-done.24.refs_3_ = bf16[32,4096]{1,0:T(8,128)(2,1)S(1)} collective-permute-done((bf16[32,4096]{1,0:T(8,128)(2,1)S(1)}, bf16[32,4096]{1,0:T(8,128)(2,1)S(1)}, u32[]{:S(2)}, u32[]{:S(2)}) %collective-permute-start.24) | collective-permute-done | bytes 262176 | tf_op jit(solution)/shard_map/ppermute | solution.py:576
  128.9 2.8 %collective-permute-done.25.refs_4_ = bf16[32,4096]{1,0:T(8,128)(2,1)S(1)} collective-permute-done((bf16[32,4096]{1,0:T(8,128)(2,1)S(1)}, bf16[32,4096]{1,0:T(8,128)(2,1)S(1)}, u32[]{:S(2)}, u32[]{:S(2)}) %collective-permute-start.25) | collective-permute-done | bytes 262176 | tf_op jit(solution)/shard_map/ppermute | solution.py:576
  131.7 1.0 finish.1
  (32 shorter events, 0.3 us)
Async XLA Ops:
  3.2 15.6 %collective-permute-start.2 = (bf16[256,512]{1,0:T(8,128)(2,1)}, bf16[256,512]{1,0:T(8,128)(2,1)S(1)}, u32[]{:S(2)}, u32[]{:S(2)}) collective-permute-start(bf16[256,512]{1,0:T(8,128)(2,1)} %get-tuple-element.79), channel_id=1, source_target_pairs={{0,2},{2,4},{4,6},{6,0},{1,3},{3,5},{5,7},{7,1},{8,10},{10,12},{12... | collective-permute-start | bytes 786440 | tf_op jit(solution)/shard_map/ppermute | solution.py:521
  4.9 14.7 %collective-permute-start.3 = (bf16[256,512]{1,0:T(8,128)(2,1)}, bf16[256,512]{1,0:T(8,128)(2,1)S(1)}, u32[]{:S(2)}, u32[]{:S(2)}) collective-permute-start(bf16[256,512]{1,0:T(8,128)(2,1)} %get-tuple-element.80), channel_id=1, source_target_pairs={{0,4},{2,6},{4,0},{6,2},{1,5},{3,7},{5,1},{7,3},{8,12},{10,14},{12... | collective-permute-start | bytes 786440 | tf_op jit(solution)/shard_map/ppermute | solution.py:521
  7.8 11.9 %collective-permute-start.4 = (bf16[256,512]{1,0:T(8,128)(2,1)}, bf16[256,512]{1,0:T(8,128)(2,1)S(1)}, u32[]{:S(2)}, u32[]{:S(2)}) collective-permute-start(bf16[256,512]{1,0:T(8,128)(2,1)} %get-tuple-element.81), channel_id=1, source_target_pairs={{0,6},{2,0},{4,2},{6,4},{1,7},{3,1},{5,3},{7,5},{8,14},{10,8},{12,... | collective-permute-start | bytes 786440 | tf_op jit(solution)/shard_map/ppermute | solution.py:521
  9.2 10.5 %copy-start.4 = (bf16[256,512]{1,0:T(8,128)(2,1)S(1)}, bf16[256,512]{1,0:T(8,128)(2,1)}, u32[]{:S(2)}) copy-start(bf16[256,512]{1,0:T(8,128)(2,1)} %get-tuple-element.82.refs_0_) | copy-start | bytes 786436
  14.7 17.0 %collective-permute-start.1 = (bf16[512,512]{1,0:T(8,128)(2,1)}, bf16[512,512]{1,0:T(8,128)(2,1)S(1)}, u32[]{:S(2)}, u32[]{:S(2)}) collective-permute-start(bf16[512,512]{1,0:T(8,128)(2,1)} %project_q.1.q_ref.refs_0_), channel_id=1, source_target_pairs={{0,48},{16,0},{32,16},{48,32},{1,49},{17,1},{33,17},{49,33},{2,50}... | collective-permute-start | bytes 1572872 | tf_op jit(solution)/shard_map/ppermute | solution.py:516
  18.8 14.0 %collective-permute-start = (bf16[512,512]{1,0:T(8,128)(2,1)}, bf16[512,512]{1,0:T(8,128)(2,1)S(1)}, u32[]{:S(2)}, u32[]{:S(2)}) collective-permute-start(bf16[512,512]{1,0:T(8,128)(2,1)} %project_q.1.q_ref.refs_0_), channel_id=1, source_target_pairs={{0,16},{16,32},{32,48},{48,0},{1,17},{17,33},{33,49},{49,1},{2,18}... | collective-permute-start | bytes 1572872 | tf_op jit(solution)/shard_map/ppermute | solution.py:516
  19.8 16.0 %collective-permute-start.6 = (bf16[512,512]{1,0:T(8,128)(2,1)S(1)}, bf16[512,512]{1,0:T(8,128)(2,1)S(1)}, u32[]{:S(2)}, u32[]{:S(2)}) collective-permute-start(bf16[512,512]{1,0:T(8,128)(2,1)S(1)} %get-tuple-element.96.refs_2_.refs_1_), channel_id=1, source_target_pairs={{0,64},{64,0},{1,65},{65,1},{2,66},{66,2},{3,67},{67,3},{4,68},{68... | collective-permute-start | bytes 1572872 | tf_op jit(solution)/shard_map/ppermute | solution.py:528
  21.3 11.5 %copy-start = (bf16[512,512]{1,0:T(8,128)(2,1)S(1)}, bf16[512,512]{1,0:T(8,128)(2,1)}, u32[]{:S(2)}) copy-start(bf16[512,512]{1,0:T(8,128)(2,1)} %project_q.1.q_ref.refs_0_) | copy-start | bytes 1572868
  21.3 14.4 %collective-permute-start.7 = (bf16[512,512]{1,0:T(8,128)(2,1)S(1)}, bf16[512,512]{1,0:T(8,128)(2,1)S(1)}, u32[]{:S(2)}, u32[]{:S(2)}) collective-permute-start(bf16[512,512]{1,0:T(8,128)(2,1)S(1)} %get-tuple-element.91), channel_id=1, source_target_pairs={{0,65},{65,0},{1,64},{64,1},{2,67},{67,2},{3,66},{66,3},{4,69},{69... | collective-permute-start | bytes 1572872 | tf_op jit(solution)/shard_map/ppermute | solution.py:529
  32.8 3.8 %collective-permute-start.10 = (bf16[512,512]{1,0:T(8,128)(2,1)S(1)}, bf16[512,512]{1,0:T(8,128)(2,1)S(1)}, u32[]{:S(2)}, u32[]{:S(2)}) collective-permute-start(bf16[512,512]{1,0:T(8,128)(2,1)S(1)} %get-tuple-element.96.refs_2_.refs_1_), channel_id=1, source_target_pairs={{0,8},{8,0},{1,9},{9,1},{2,10},{10,2},{3,11},{11,3},{4,12},{12,4},... | collective-permute-start | bytes 1572872 | tf_op jit(solution)/shard_map/ppermute | solution.py:513
  32.8 15.8 %collective-permute-start.5 = (bf16[512,512]{1,0:T(8,128)(2,1)S(1)}, bf16[512,512]{1,0:T(8,128)(2,1)S(1)}, u32[]{:S(2)}, u32[]{:S(2)}) collective-permute-start(bf16[512,512]{1,0:T(8,128)(2,1)S(1)} %copy-done), channel_id=1, source_target_pairs={{0,32},{16,48},{32,0},{48,16},{1,33},{17,49},{33,1},{49,17},{2,34}... | collective-permute-start | bytes 1572872 | tf_op jit(solution)/shard_map/ppermute | solution.py:516
  35.8 3.9 %collective-permute-start.8 = (bf16[512,512]{1,0:T(8,128)(2,1)S(1)}, bf16[512,512]{1,0:T(8,128)(2,1)S(1)}, u32[]{:S(2)}, u32[]{:S(2)}) collective-permute-start(bf16[512,512]{1,0:T(8,128)(2,1)S(1)} %collective-permute-done.6.refs_2_.refs_3_), channel_id=1, source_target_pairs={{0,8},{8,0},{1,9},{9,1},{2,10},{10,2},{3,11},{11,3},{4,12},{12,4},... | collective-permute-start | bytes 1572872 | tf_op jit(solution)/shard_map/ppermute | solution.py:513
  35.9 17.5 %collective-permute-start.11 = (bf16[512,512]{1,0:T(8,128)(2,1)S(1)}, bf16[512,512]{1,0:T(8,128)(2,1)S(1)}, u32[]{:S(2)}, u32[]{:S(2)}) collective-permute-start(bf16[512,512]{1,0:T(8,128)(2,1)S(1)} %collective-permute-done.7.refs_3_.refs_4_), channel_id=1, source_target_pairs={{0,64},{64,0},{1,65},{65,1},{2,66},{66,2},{3,67},{67,3},{4,68},{68... | collective-permute-start | bytes 1572872 | tf_op jit(solution)/shard_map/ppermute | solution.py:536
  36.5 3.1 %collective-permute-start.9 = (bf16[512,512]{1,0:T(8,128)(2,1)S(1)}, bf16[512,512]{1,0:T(8,128)(2,1)S(1)}, u32[]{:S(2)}, u32[]{:S(2)}) collective-permute-start(bf16[512,512]{1,0:T(8,128)(2,1)S(1)} %collective-permute-done.7.refs_3_.refs_4_), channel_id=1, source_target_pairs={{0,8},{8,0},{1,9},{9,1},{2,10},{10,2},{3,11},{11,3},{4,12},{12,4},... | collective-permute-start | bytes 1572872 | tf_op jit(solution)/shard_map/ppermute | solution.py:513
  45.5 8.7 %copy-start.2 = (bf16[512,512]{1,0:T(8,128)(2,1)S(1)}, bf16[512,512]{1,0:T(8,128)(2,1)}, u32[]{:S(2)}) copy-start(bf16[512,512]{1,0:T(8,128)(2,1)} %get-tuple-element.105.k_ref) | copy-start | bytes 1572868
  45.5 8.7 %copy-start.3 = (bf16[512,512]{1,0:T(8,128)(2,1)S(1)}, bf16[512,512]{1,0:T(8,128)(2,1)}, u32[]{:S(2)}) copy-start(bf16[512,512]{1,0:T(8,128)(2,1)} %get-tuple-element.106.v_ref) | copy-start | bytes 1572868
  53.4 2.6 %collective-permute-start.12 = (bf16[512,512]{1,0:T(8,128)(2,1)S(1)}, bf16[512,512]{1,0:T(8,128)(2,1)S(1)}, u32[]{:S(2)}, u32[]{:S(2)}) collective-permute-start(bf16[512,512]{1,0:T(8,128)(2,1)S(1)} %collective-permute-done.11.refs_3_.refs_7_), channel_id=1, source_target_pairs={{0,8},{8,0},{1,9},{9,1},{2,10},{10,2},{3,11},{11,3},{4,12},{12,4},... | collective-permute-start | bytes 1572872 | tf_op jit(solution)/shard_map/ppermute | solution.py:513
  58.4 11.1 %collective-permute-start.14 = (bf16[272,512]{1,0:T(8,128)(2,1)S(1)}, bf16[272,512]{1,0:T(8,128)(2,1)S(1)}, u32[]{:S(2)}, u32[]{:S(2)}) collective-permute-start(bf16[272,512]{1,0:T(8,128)(2,1)S(1)} %get-tuple-element.114), channel_id=1, source_target_pairs={{0,32},{16,48},{32,0},{48,16},{1,33},{17,49},{33,1},{49,17},{2,34}... | collective-permute-start | bytes 835592 | tf_op jit(solution)/shard_map/ppermute | solution.py:516
  61.3 16.6 %collective-permute-start.15 = (bf16[272,512]{1,0:T(8,128)(2,1)S(1)}, bf16[272,512]{1,0:T(8,128)(2,1)S(1)}, u32[]{:S(2)}, u32[]{:S(2)}) collective-permute-start(bf16[272,512]{1,0:T(8,128)(2,1)S(1)} %get-tuple-element.115), channel_id=1, source_target_pairs={{0,16},{16,32},{32,48},{48,0},{1,17},{17,33},{33,49},{49,1},{2,18}... | collective-permute-start | bytes 835592 | tf_op jit(solution)/shard_map/ppermute | solution.py:516
  62.3 15.6 %collective-permute-start.13 = (bf16[272,512]{1,0:T(8,128)(2,1)S(1)}, bf16[272,512]{1,0:T(8,128)(2,1)S(1)}, u32[]{:S(2)}, u32[]{:S(2)}) collective-permute-start(bf16[272,512]{1,0:T(8,128)(2,1)S(1)} %get-tuple-element.113), channel_id=1, source_target_pairs={{0,48},{16,0},{32,16},{48,32},{1,49},{17,1},{33,17},{49,33},{2,50}... | collective-permute-start | bytes 835592 | tf_op jit(solution)/shard_map/ppermute | solution.py:516
  66.9 19.4 %collective-permute-start.20 = (bf16[272,512]{1,0:T(8,128)(2,1)S(1)}, bf16[272,512]{1,0:T(8,128)(2,1)S(1)}, u32[]{:S(2)}, u32[]{:S(2)}) collective-permute-start(bf16[272,512]{1,0:T(8,128)(2,1)S(1)} %get-tuple-element.130), channel_id=1, source_target_pairs={{0,32},{16,48},{32,0},{48,16},{1,33},{17,49},{33,1},{49,17},{2,34}... | collective-permute-start | bytes 835592 | tf_op jit(solution)/shard_map/ppermute | solution.py:516
  67.0 20.9 %collective-permute-start.21 = (bf16[272,512]{1,0:T(8,128)(2,1)S(1)}, bf16[272,512]{1,0:T(8,128)(2,1)S(1)}, u32[]{:S(2)}, u32[]{:S(2)}) collective-permute-start(bf16[272,512]{1,0:T(8,128)(2,1)S(1)} %get-tuple-element.131), channel_id=1, source_target_pairs={{0,16},{16,32},{32,48},{48,0},{1,17},{17,33},{33,49},{49,1},{2,18}... | collective-permute-start | bytes 835592 | tf_op jit(solution)/shard_map/ppermute | solution.py:516
  69.4 18.4 %collective-permute-start.19 = (bf16[272,512]{1,0:T(8,128)(2,1)S(1)}, bf16[272,512]{1,0:T(8,128)(2,1)S(1)}, u32[]{:S(2)}, u32[]{:S(2)}) collective-permute-start(bf16[272,512]{1,0:T(8,128)(2,1)S(1)} %get-tuple-element.118), channel_id=1, source_target_pairs={{0,48},{16,0},{32,16},{48,32},{1,49},{17,1},{33,17},{49,33},{2,50}... | collective-permute-start | bytes 835592 | tf_op jit(solution)/shard_map/ppermute | solution.py:516
  72.5 5.5 %copy-start.1 = (bf16[512,4096]{1,0:T(8,128)(2,1)S(1)}, bf16[512,4096]{1,0:T(8,128)(2,1)}, u32[]{:S(2)}) copy-start(bf16[512,4096]{1,0:T(8,128)(2,1)} %refs_4_.4) | copy-start | bytes 12582916
  82.6 15.7 %collective-permute-start.16 = (bf16[64,4096]{1,0:T(8,128)(2,1)S(1)}, bf16[64,4096]{1,0:T(8,128)(2,1)S(1)}, u32[]{:S(2)}, u32[]{:S(2)}) collective-permute-start(bf16[64,4096]{1,0:T(8,128)(2,1)S(1)} %get-tuple-element.127), channel_id=1, source_target_pairs={{0,2},{2,4},{4,6},{6,0},{1,3},{3,5},{5,7},{7,1},{8,10},{10,12},{12... | collective-permute-start | bytes 1572872 | tf_op jit(solution)/shard_map/ppermute | solution.py:568
  83.9 24.5 %collective-permute-start.17 = (bf16[64,4096]{1,0:T(8,128)(2,1)S(1)}, bf16[64,4096]{1,0:T(8,128)(2,1)S(1)}, u32[]{:S(2)}, u32[]{:S(2)}) collective-permute-start(bf16[64,4096]{1,0:T(8,128)(2,1)S(1)} %get-tuple-element.128), channel_id=1, source_target_pairs={{0,4},{2,6},{4,0},{6,2},{1,5},{3,7},{5,1},{7,3},{8,12},{10,14},{12... | collective-permute-start | bytes 1572872 | tf_op jit(solution)/shard_map/ppermute | solution.py:568
  86.3 22.3 %collective-permute-start.18 = (bf16[64,4096]{1,0:T(8,128)(2,1)S(1)}, bf16[64,4096]{1,0:T(8,128)(2,1)S(1)}, u32[]{:S(2)}, u32[]{:S(2)}) collective-permute-start(bf16[64,4096]{1,0:T(8,128)(2,1)S(1)} %get-tuple-element.129), channel_id=1, source_target_pairs={{0,6},{2,0},{4,2},{6,4},{1,7},{3,1},{5,3},{7,5},{8,14},{10,8},{12,... | collective-permute-start | bytes 1572872 | tf_op jit(solution)/shard_map/ppermute | solution.py:568
  90.8 27.7 %collective-permute-start.23 = (bf16[128,4096]{1,0:T(8,128)(2,1)S(1)}, bf16[128,4096]{1,0:T(8,128)(2,1)S(1)}, u32[]{:S(2)}, u32[]{:S(2)}) collective-permute-start(bf16[128,4096]{1,0:T(8,128)(2,1)S(1)} %get-tuple-element.143), channel_id=1, source_target_pairs={{0,1},{1,0},{2,3},{3,2},{4,5},{5,4},{6,7},{7,6},{8,9},{9,8},{10,11... | collective-permute-start | bytes 3145736 | tf_op jit(solution)/shard_map/ppermute | solution.py:570
  109.2 14.7 %collective-permute-start.22 = (bf16[32,4096]{1,0:T(8,128)(2,1)S(1)}, bf16[32,4096]{1,0:T(8,128)(2,1)S(1)}, u32[]{:S(2)}, u32[]{:S(2)}) collective-permute-start(bf16[32,4096]{1,0:T(8,128)(2,1)S(1)} %get-tuple-element.142), channel_id=1, source_target_pairs={{0,1},{1,0},{2,3},{3,2},{4,5},{5,4},{6,7},{7,6},{8,9},{9,8},{10,11... | collective-permute-start | bytes 786440 | tf_op jit(solution)/shard_map/ppermute | solution.py:573
  119.1 9.8 %collective-permute-start.24 = (bf16[32,4096]{1,0:T(8,128)(2,1)S(1)}, bf16[32,4096]{1,0:T(8,128)(2,1)S(1)}, u32[]{:S(2)}, u32[]{:S(2)}) collective-permute-start(bf16[32,4096]{1,0:T(8,128)(2,1)S(1)} %get-tuple-element.146), channel_id=1, source_target_pairs={{0,2},{2,4},{4,6},{6,0},{1,3},{3,5},{5,7},{7,1},{8,10},{10,12},{12... | collective-permute-start | bytes 786440 | tf_op jit(solution)/shard_map/ppermute | solution.py:576
  119.9 11.8 %collective-permute-start.25 = (bf16[32,4096]{1,0:T(8,128)(2,1)S(1)}, bf16[32,4096]{1,0:T(8,128)(2,1)S(1)}, u32[]{:S(2)}, u32[]{:S(2)}) collective-permute-start(bf16[32,4096]{1,0:T(8,128)(2,1)S(1)} %get-tuple-element.147), channel_id=1, source_target_pairs={{0,4},{2,6},{4,0},{6,2},{1,5},{3,7},{5,1},{7,3},{8,12},{10,14},{12... | collective-permute-start | bytes 786440 | tf_op jit(solution)/shard_map/ppermute | solution.py:576
  122.3 9.4 %collective-permute-start.26 = (bf16[32,4096]{1,0:T(8,128)(2,1)S(1)}, bf16[32,4096]{1,0:T(8,128)(2,1)S(1)}, u32[]{:S(2)}, u32[]{:S(2)}) collective-permute-start(bf16[32,4096]{1,0:T(8,128)(2,1)S(1)} %get-tuple-element.148), channel_id=1, source_target_pairs={{0,6},{2,0},{4,2},{6,4},{1,7},{3,1},{5,3},{7,5},{8,14},{10,8},{12,... | collective-permute-start | bytes 786440 | tf_op jit(solution)/shard_map/ppermute | solution.py:576
